TPU v7x, 768 devices: a whole 4x8x12 slice. The times are simulated.
768 devices in a mesh: east: 96 (over z_lo, y, x), north: 8 (over z_hi, core).
Axes of the slice: x: 4, y: 8, z: 12 (z_hi: 4, z_lo: 3; z = z_hi * 3 + z_lo), core: 2. Of those that a mesh axis runs over, the one named last changes fastest.
Arguments:
- field_prev: float32 [3, 768, 256, 128], P(None, 'east', 'north'), may hold values from -6 to 6
- field_now: float32 [3, 768, 256, 128], P(None, 'east', 'north'), may hold values from -6 to 6
- speed_sq: float32 [768, 256, 128], P('east', 'north'), may hold values from 0.04 to 0.2
- mechanism: float32 [6, 12288], P(None, ('east', 'north')), may hold values from -6 to 6
- sub_cells: int32 [12288], P(('east', 'north')), may hold values from 0 to 32767
- sub_patch: int32 [12288], P(('east', 'north')), may hold values from 0 to 6143
Outputs:
- field_next: float32 [3, 768, 256, 128], P(None, 'east', 'north')
- field_last: float32 [3, 768, 256, 128], P(None, 'east', 'north')
- patch_grad: float32 [6144], P(('east', 'north'))
All inputs are finite; a program needn't handle non-finite values.
Results may differ from a plain program's by a relative error of at most 0.00019.
Values sent between devices are 32-bit elements; how exact they have to be, the bound alone decides.
No kernel may reach another device: no remote copies, remote signals or barrier semaphores. Data moves between devices by JAX's collectives and lax.ppermute only.
A program may use at most 128 MiB of HBM per device.

v0:
```python
import jax
import jax.numpy as jnp
from jax import lax
from jax.sharding import PartitionSpec as P

PATCH_DEV = 8


def padded_2(block, sides, width):
    for axis, dim in sides:
        count = lax.axis_size(axis)
        forward = [(i, i + 1) for i in range(count - 1)]
        backward = [(target, source) for source, target in forward]
        low = lax.ppermute(
            lax.slice_in_dim(block, block.shape[dim] - width, None, axis=dim), axis, forward
        )
        high = lax.ppermute(lax.slice_in_dim(block, 0, width, axis=dim), axis, backward)
        block = jnp.concatenate([low, block, high], axis=dim)
    return block


def second_diff(padded, axis, size):

    def take(offset):
        return lax.slice_in_dim(padded, offset, offset + size, axis=axis)

    return (-take(0) + 16.0 * take(1) - 30.0 * take(2) + 16.0 * take(3) - take(4)) / 12.0


def laplace_valid(field):
    deeper = jnp.pad(field, ((0, 0), (0, 0), (0, 0), (2, 2)))
    east_len = field.shape[1] - 4
    north_len = field.shape[2] - 4
    depth_len = field.shape[3]
    along_east = second_diff(deeper[:, :, 2 : 2 + north_len, 2 : 2 + depth_len], 1, east_len)
    along_north = second_diff(deeper[:, 2 : 2 + east_len, :, 2 : 2 + depth_len], 2, north_len)
    along_depth = second_diff(deeper[:, 2 : 2 + east_len, 2 : 2 + north_len, :], 3, depth_len)
    return along_east + along_north + along_depth


def advance(before, middle, speed_sq):
    widened = padded_2(middle, (("east", 1), ("north", 2)), 2)
    return 2.0 * middle - before + speed_sq[None] * laplace_valid(widened)


def body(field_prev, field_now, speed_sq, mechanism, sub_cells, sub_patch):
    field_next = advance(field_prev, field_now, speed_sq)
    field_last = advance(field_now, field_next, speed_sq)
    flat_next = field_next.reshape(3, -1)
    flat_last = field_last.reshape(3, -1)
    sample_next = jnp.take(flat_next, sub_cells, axis=1)
    sample_last = jnp.take(flat_last, sub_cells, axis=1)
    grads = jnp.sum(mechanism[0:3] * sample_next + mechanism[3:6] * sample_last, axis=0)
    patch_count = PATCH_DEV * lax.axis_size("east") * lax.axis_size("north")
    selector = (sub_patch[:, None] == jnp.arange(patch_count, dtype=jnp.int32)[None, :]).astype(
        jnp.float32
    )
    partial_grad = jnp.dot(
        grads, selector, precision=lax.Precision.HIGHEST, preferred_element_type=jnp.float32
    )
    patch_grad = lax.psum_scatter(partial_grad, ("east", "north"), scatter_dimension=0, tiled=True)
    return (field_next, field_last, patch_grad)


def solution(mesh):
    in_specs = (
        P(None, "east", "north", None),
        P(None, "east", "north", None),
        P("east", "north", None),
        P(None, ("east", "north")),
        P(("east", "north")),
        P(("east", "north")),
    )
    out_specs = (
        P(None, "east", "north", None),
        P(None, "east", "north", None),
        P(("east", "north")),
    )
    return jax.shard_map(body, mesh=mesh, in_specs=in_specs, out_specs=out_specs, check_vma=False)
```

profile of v0, /device:TPU:1, one launch (start us, length us, event | category | flops | bytes accessed | tf_op | source)
XLA Modules:
  0.0 198.5 jit_solution(15368060534116493462)
XLA Ops:
  0.6 1.0 fusion.46
  1.6 4.0 %collective-permute-start = (f32[3,2,32,128]{3,2,1,0:T(8,128)S(1)}, f32[3,2,32,128]{3,2,1,0:T(8,128)S(1)}, u32[]{:S(2)}, u32[]{:S(2)}) collective-permute-start(f32[3,2,32,128]{3,2,1,0:T(8,128)S(1)} %get-tuple-element.16), channel_id=1, source_target_pairs={{0,8},{8,16},{16,24},{24,32},{32,40},{40,48},{48,56},{56,64},{64,7... | collective-permute-start | bytes 294920 | tf_op jit(solution)/shard_map/ppermute | solution.py:14
  5.6 1.3 collective-permute-start.1
  6.9 0.9 broadcast_multiply_fusion
  7.8 0.8 fusion.47
  8.6 1.1 constant_dynamic-update-slice_fusion
  9.7 1.2 collective-permute-done.1
  11.0 9.6 %collective-permute-start.2 = (f32[3,12,2,128]{3,2,1,0:T(2,128)S(1)}, f32[3,12,2,128]{3,2,1,0:T(2,128)S(1)}, u32[]{:S(2)}, u32[]{:S(2)}) collective-permute-start(f32[3,12,2,128]{3,2,1,0:T(2,128)S(1)} %get-tuple-element.8), channel_id=1, source_target_pairs={{0,1},{1,2},{2,3},{3,4},{4,5},{5,6},{6,7},{8,9},{9,10},{10,11},{11... | collective-permute-start | bytes 110600 | tf_op jit(solution)/shard_map/ppermute | solution.py:14
  20.6 2.6 %collective-permute-start.3 = (f32[3,12,2,128]{3,2,1,0:T(2,128)S(1)}, f32[3,12,2,128]{3,2,1,0:T(2,128)S(1)}, u32[]{:S(2)}, u32[]{:S(2)}) collective-permute-start(f32[3,12,2,128]{3,2,1,0:T(2,128)S(1)} %get-tuple-element.9), channel_id=1, source_target_pairs={{1,0},{2,1},{3,2},{4,3},{5,4},{6,5},{7,6},{9,8},{10,9},{11,10},{12... | collective-permute-start | bytes 110600 | tf_op jit(solution)/shard_map/ppermute | solution.py:17
  23.2 4.4 %collective-permute-done.3 = f32[3,12,2,128]{3,2,1,0:T(2,128)S(1)} collective-permute-done((f32[3,12,2,128]{3,2,1,0:T(2,128)S(1)}, f32[3,12,2,128]{3,2,1,0:T(2,128)S(1)}, u32[]{:S(2)}, u32[]{:S(2)}) %collective-permute-start.3) | collective-permute-done | bytes 36896 | tf_op jit(solution)/shard_map/ppermute | solution.py:17
  27.7 0.6 select_maximum_fusion.4
  28.3 0.6 fusion.20
  28.9 0.0 copy-start
  29.0 3.1 %collective-permute-start.4 = (f32[3,2,32,128]{3,2,1,0:T(8,128)S(1)}, f32[3,2,32,128]{3,2,1,0:T(8,128)S(1)}, u32[]{:S(2)}, u32[]{:S(2)}) collective-permute-start(f32[3,2,32,128]{3,2,1,0:T(8,128)S(1)} %get-tuple-element.10), channel_id=1, source_target_pairs={{0,8},{8,16},{16,24},{24,32},{32,40},{40,48},{48,56},{56,64},{64,7... | collective-permute-start | bytes 294920 | tf_op jit(solution)/shard_map/ppermute | solution.py:14
  32.1 1.3 collective-permute-start.5
  33.4 0.3 collective-permute-done.4
  33.7 3.7 %collective-permute-done.5 = f32[3,2,32,128]{3,2,1,0:T(8,128)S(1)} collective-permute-done((f32[3,2,32,128]{3,2,1,0:T(8,128)S(1)}, f32[3,2,32,128]{3,2,1,0:T(8,128)S(1)}, u32[]{:S(2)}, u32[]{:S(2)}) %collective-permute-start.5) | collective-permute-done | bytes 98336 | tf_op jit(solution)/shard_map/ppermute | solution.py:17
  37.5 6.2 %collective-permute-start.6 = (f32[3,12,2,128]{3,2,1,0:T(2,128)S(1)}, f32[3,12,2,128]{3,2,1,0:T(2,128)S(1)}, u32[]{:S(2)}, u32[]{:S(2)}) collective-permute-start(f32[3,12,2,128]{3,2,1,0:T(2,128)S(1)} %get-tuple-element.6), channel_id=1, source_target_pairs={{0,1},{1,2},{2,3},{3,4},{4,5},{5,6},{6,7},{8,9},{9,10},{10,11},{11... | collective-permute-start | bytes 110600 | tf_op jit(solution)/shard_map/ppermute | solution.py:14
  43.7 1.9 collective-permute-start.7
  45.6 0.1 copy.17
  45.7 0.1 copy.18
  45.8 8.6 %copy.14 = f32[3,8,32,128]{0,3,2,1:T(8,128)} copy(f32[3,8,32,128]{3,2,1,0:T(8,128)S(1)} %fusion.20) | data formatting | bytes 786432 | tf_op jit(solution)/shard_map/add | solution.py:43
  54.4 6.3 %gather_fusion = f32[16,3]{1,0:T(8,128)S(1)} fusion(f32[3,32768]{0,1:T(8,128)} %bitcast.17, s32[1024]{0:T(1024)S(1)} %pad_clamp_fusion), kind=kCustom, calls=%fused_computation.clone | custom fusion | bytes 448 | tf_op jit(solution)/shard_map/jit(_take)/gather | solution.py:51
  60.7 0.1 maximum_maximum_fusion
  60.9 0.6 select_maximum_fusion
  61.5 0.6 fusion.8
  62.1 8.6 %copy.16 = f32[3,8,32,128]{0,3,2,1:T(8,128)} copy(f32[3,8,32,128]{3,2,1,0:T(8,128)S(1)} %fusion.8) | data formatting | bytes 786432 | tf_op jit(solution)/shard_map/add | solution.py:43
  70.7 6.3 %gather_fusion.1 = f32[16,3]{1,0:T(8,128)S(1)} fusion(f32[3,32768]{0,1:T(8,128)} %bitcast.16, s32[1024]{0:T(1024)S(1)} %pad_clamp_fusion), kind=kCustom, calls=%fused_computation.1.clone | custom fusion | bytes 448 | tf_op jit(solution)/shard_map/jit(_take)/gather | solution.py:52
  77.0 0.2 fusion.42
  77.2 0.3 fusion.39
  77.5 120.3 %all-reduce.2 = f32[6144]{0:T(1024)S(1)} all-reduce(f32[6144]{0:T(1024)S(1)} %bitcast.18), channel_id=2, replica_groups=mesh['east'=96,'north'=8] {'east','north'}, use_global_device_ids=true, to_apply=%region_1.3.clone | all-reduce | flops 6144 | bytes 49152
  197.9 0.6 dynamic-slice
  (23 shorter events, 0.2 us)
Async XLA Ops:
  0.6 22.6 %copy-start.4 = (s32[16]{0:T(128)S(1)}, s32[16]{0:T(128)}, u32[]{:S(2)}) copy-start(s32[16]{0:T(128)} %param.12) | copy-start | bytes 196
  1.6 7.0 %collective-permute-start = (f32[3,2,32,128]{3,2,1,0:T(8,128)S(1)}, f32[3,2,32,128]{3,2,1,0:T(8,128)S(1)}, u32[]{:S(2)}, u32[]{:S(2)}) collective-permute-start(f32[3,2,32,128]{3,2,1,0:T(8,128)S(1)} %get-tuple-element.16), channel_id=1, source_target_pairs={{0,8},{8,16},{16,24},{24,32},{32,40},{40,48},{48,56},{56,64},{64,7... | collective-permute-start | bytes 294920 | tf_op jit(solution)/shard_map/ppermute | solution.py:14
  5.6 5.4 %collective-permute-start.1 = (f32[3,2,32,128]{3,2,1,0:T(8,128)S(1)}, f32[3,2,32,128]{3,2,1,0:T(8,128)S(1)}, u32[]{:S(2)}, u32[]{:S(2)}) collective-permute-start(f32[3,2,32,128]{3,2,1,0:T(8,128)S(1)} %get-tuple-element.15), channel_id=1, source_target_pairs={{8,0},{16,8},{24,16},{32,24},{40,32},{48,40},{56,48},{64,56},{72,6... | collective-permute-start | bytes 294920 | tf_op jit(solution)/shard_map/ppermute | solution.py:17
  9.7 18.6 %copy-start.1 = (f32[3,8,32,128]{3,2,1,0:T(8,128)S(1)}, f32[3,8,32,128]{3,2,1,0:T(8,128)}, u32[]{:S(2)}) copy-start(f32[3,8,32,128]{3,2,1,0:T(8,128)} %param.9) | copy-start | bytes 1179652
  9.7 18.6 %copy-start.3 = (f32[3,8,32,128]{3,2,1,0:T(8,128)S(1)}, f32[3,8,32,128]{3,2,1,0:T(8,128)}, u32[]{:S(2)}) copy-start(f32[3,8,32,128]{3,2,1,0:T(8,128)} %param.8) | copy-start | bytes 1179652
  11.0 12.3 %collective-permute-start.2 = (f32[3,12,2,128]{3,2,1,0:T(2,128)S(1)}, f32[3,12,2,128]{3,2,1,0:T(2,128)S(1)}, u32[]{:S(2)}, u32[]{:S(2)}) collective-permute-start(f32[3,12,2,128]{3,2,1,0:T(2,128)S(1)} %get-tuple-element.8), channel_id=1, source_target_pairs={{0,1},{1,2},{2,3},{3,4},{4,5},{5,6},{6,7},{8,9},{9,10},{10,11},{11... | collective-permute-start | bytes 110600 | tf_op jit(solution)/shard_map/ppermute | solution.py:14
  20.6 7.1 %collective-permute-start.3 = (f32[3,12,2,128]{3,2,1,0:T(2,128)S(1)}, f32[3,12,2,128]{3,2,1,0:T(2,128)S(1)}, u32[]{:S(2)}, u32[]{:S(2)}) collective-permute-start(f32[3,12,2,128]{3,2,1,0:T(2,128)S(1)} %get-tuple-element.9), channel_id=1, source_target_pairs={{1,0},{2,1},{3,2},{4,3},{5,4},{6,5},{7,6},{9,8},{10,9},{11,10},{12... | collective-permute-start | bytes 110600 | tf_op jit(solution)/shard_map/ppermute | solution.py:17
  28.9 32.5 %copy-start = (f32[3,8,32,128]{3,2,1,0:T(8,128)}, f32[3,8,32,128]{3,2,1,0:T(8,128)S(1)}, u32[]{:S(2)}) copy-start(f32[3,8,32,128]{3,2,1,0:T(8,128)S(1)} %fusion.20) | copy-start | bytes 1179652
  29.0 4.7 %collective-permute-start.4 = (f32[3,2,32,128]{3,2,1,0:T(8,128)S(1)}, f32[3,2,32,128]{3,2,1,0:T(8,128)S(1)}, u32[]{:S(2)}, u32[]{:S(2)}) collective-permute-start(f32[3,2,32,128]{3,2,1,0:T(8,128)S(1)} %get-tuple-element.10), channel_id=1, source_target_pairs={{0,8},{8,16},{16,24},{24,32},{32,40},{40,48},{48,56},{56,64},{64,7... | collective-permute-start | bytes 294920 | tf_op jit(solution)/shard_map/ppermute | solution.py:14
  32.1 5.4 %collective-permute-start.5 = (f32[3,2,32,128]{3,2,1,0:T(8,128)S(1)}, f32[3,2,32,128]{3,2,1,0:T(8,128)S(1)}, u32[]{:S(2)}, u32[]{:S(2)}) collective-permute-start(f32[3,2,32,128]{3,2,1,0:T(8,128)S(1)} %get-tuple-element.11), channel_id=1, source_target_pairs={{8,0},{16,8},{24,16},{32,24},{40,32},{48,40},{56,48},{64,56},{72,6... | collective-permute-start | bytes 294920 | tf_op jit(solution)/shard_map/ppermute | solution.py:17
  37.5 23.2 %collective-permute-start.6 = (f32[3,12,2,128]{3,2,1,0:T(2,128)S(1)}, f32[3,12,2,128]{3,2,1,0:T(2,128)S(1)}, u32[]{:S(2)}, u32[]{:S(2)}) collective-permute-start(f32[3,12,2,128]{3,2,1,0:T(2,128)S(1)} %get-tuple-element.6), channel_id=1, source_target_pairs={{0,1},{1,2},{2,3},{3,4},{4,5},{5,6},{6,7},{8,9},{9,10},{10,11},{11... | collective-permute-start | bytes 110600 | tf_op jit(solution)/shard_map/ppermute | solution.py:14
  43.7 17.0 %collective-permute-start.7 = (f32[3,12,2,128]{3,2,1,0:T(2,128)S(1)}, f32[3,12,2,128]{3,2,1,0:T(2,128)S(1)}, u32[]{:S(2)}, u32[]{:S(2)}) collective-permute-start(f32[3,12,2,128]{3,2,1,0:T(2,128)S(1)} %get-tuple-element.7), channel_id=1, source_target_pairs={{1,0},{2,1},{3,2},{4,3},{5,4},{6,5},{7,6},{9,8},{10,9},{11,10},{12... | collective-permute-start | bytes 110600 | tf_op jit(solution)/shard_map/ppermute | solution.py:17
  62.1 8.6 %copy-start.2 = (f32[3,8,32,128]{3,2,1,0:T(8,128)}, f32[3,8,32,128]{3,2,1,0:T(8,128)S(1)}, u32[]{:S(2)}) copy-start(f32[3,8,32,128]{3,2,1,0:T(8,128)S(1)} %fusion.8) | copy-start | bytes 1179652
  62.1 15.1 %copy-start.5 = (s32[16]{0:T(128)S(1)}, s32[16]{0:T(128)}, u32[]{:S(2)}) copy-start(s32[16]{0:T(128)} %param.13) | copy-start | bytes 196
where the time goes:
time: 199 us; the launch traced here: 198 us
  blocking collectives  120 us (60%)
  local copies, waits for them, and re-layouts  33.6 us (17%)
  starting transfers between devices  30 us (15%)
  waiting for transfers between devices  9.67 us (5%)
  other arithmetic  3.7 us (2%)
    unnamed x1, blocking collectives  120 us
    ppermute x4, starting transfers between devices, padded_2(): lax.ppermute(lax.slice_in_dim(block, block.shape[dim] - width, None, axis...  22.9 us
    add x2, local copies, waits for them, and re-layouts, advance(): return 2.0 * middle - before + speed_sq[None] * laplace_valid(widened)  17.2 us
    ppermute x4, waiting for transfers between devices, padded_2(): lax.ppermute(lax.slice_in_dim(block, 0, width, axis=dim), axis, backward)  9.36 us
    ppermute x4, starting transfers between devices, padded_2(): lax.ppermute(lax.slice_in_dim(block, 0, width, axis=dim), axis, backward)  7.11 us
    gather x1, local copies, waits for them, and re-layouts, body(): sample_last = jnp.take(flat_last, sub_cells, axis=1)  6.33 us
    gather x1, local copies, waits for them, and re-layouts, body(): sample_next = jnp.take(flat_next, sub_cells, axis=1)  6.33 us
  transfers between devices with their start and end apart: 8, of which 4 were waited for; matrix products, arithmetic and copies ran while one was open for 9% of the time, Pallas kernels for 0%

commit v1 on v0

v1 whole, which is shorter than its diff:
```python
import functools

import jax
import jax.numpy as jnp
from jax import lax
from jax.experimental import pallas as pl
from jax.experimental.pallas import tpu as pltpu
from jax.sharding import PartitionSpec as P

BOTH = ("east", "north")
CE, CN, CZ = 8, 32, 128
SUBS = 16
N_NORTH = 8
PLANE = 32
Z_RUN = 3
COLUMN = Z_RUN * N_NORTH
PATCH_DEV = 8
PER_ROW = CZ // PATCH_DEV
ROWS = PLANE // PER_ROW
VMEM = pl.BlockSpec(memory_space=pltpu.VMEM)
SMEM = pl.BlockSpec(memory_space=pltpu.SMEM)
LIMIT = 32 * 1024 * 1024


def column_groups():
    return [
        [(run * PLANE + at) * N_NORTH + n for run in range(Z_RUN) for n in range(N_NORTH)]
        for at in range(PLANE)
    ]


def plane_groups():
    return [
        [(run * PLANE + at) * N_NORTH + n for at in range(PLANE)]
        for run in range(Z_RUN)
        for n in range(N_NORTH)
    ]


def put_strips(field, east_low, east_high, north_low, north_high):
    for c in range(3):
        east_low[c] = field[c, 0:2]
        east_high[c] = field[c, CE - 2 : CE]
        for e in range(CE):
            at = (c * CE + e) * 2
            north_low[at : at + 2, :] = field[c, e, 0:2, :]
            north_high[at : at + 2, :] = field[c, e, CN - 2 : CN, :]


def strips_kernel(field, east_low, east_high, north_low, north_high):
    put_strips(field, east_low, east_high, north_low, north_high)


def strip_shapes():
    east = jax.ShapeDtypeStruct((3, 2, CN, CZ), jnp.float32)
    north = jax.ShapeDtypeStruct((3 * CE * 2, CZ), jnp.float32)
    return [east, east, north, north]


def step(before, middle, speed_sq, from_west, from_east, from_south, from_north, out, wide):
    lane = lax.broadcasted_iota(jnp.int32, (CN, CZ), 1)

    def component(c, carry):
        for e in range(CE):
            slot = c * CE + e
            at = pl.multiple_of(slot * 2, 2)
            here = middle[c, e]
            wide[slot, 8 : 8 + CN, :] = here
            wide[slot, 6:8, :] = from_south[pl.ds(at, 2), :]
            wide[slot, 8 + CN : 10 + CN, :] = from_north[pl.ds(at, 2), :]

            def layer(k):
                if k < 0:
                    return from_west[c, k + 2]
                if k >= CE:
                    return from_east[c, k - CE]
                return middle[c, k]

            near = layer(e - 1) + layer(e + 1)
            far = layer(e - 2) + layer(e + 2)
            near += wide[slot, 7 : 7 + CN, :] + wide[slot, 9 : 9 + CN, :]
            far += wide[slot, 6 : 6 + CN, :] + wide[slot, 10 : 10 + CN, :]
            near += jnp.where(lane >= 1, pltpu.roll(here, 1, 1), 0.0)
            near += jnp.where(lane < CZ - 1, pltpu.roll(here, CZ - 1, 1), 0.0)
            far += jnp.where(lane >= 2, pltpu.roll(here, 2, 1), 0.0)
            far += jnp.where(lane < CZ - 2, pltpu.roll(here, CZ - 2, 1), 0.0)
            laplace = near * (16.0 / 12.0) - far * (1.0 / 12.0) - here * 7.5
            out[c, e] = 2.0 * here - before[c, e] + speed_sq[e] * laplace
        return carry

    lax.fori_loop(0, 3, component, 0)


def first_kernel(before, middle, speed_sq, w, e, s, n, out, east_low, east_high, north_low, north_high, wide):
    step(before, middle, speed_sq, w, e, s, n, out, wide)
    put_strips(out, east_low, east_high, north_low, north_high)


def second_kernel(before, middle, speed_sq, w, e, s, n, mechanism, cells, patches, out, parts, wide):
    step(before, middle, speed_sq, w, e, s, n, out, wide)
    lane = lax.broadcasted_iota(jnp.int32, (1, CZ), 1)
    parts[...] = jnp.zeros_like(parts)
    for i in range(SUBS):
        cell, patch = cells[i], patches[i]
        layer, row, depth = cell >> 12, (cell >> 7) & (CN - 1), cell & (CZ - 1)
        total = jnp.zeros((1, CZ), jnp.float32)
        for c in range(3):
            total += mechanism[c, i] * middle[c, layer, pl.ds(row, 1), :]
            total += mechanism[3 + c, i] * out[c, layer, pl.ds(row, 1), :]
        total = jnp.where(lane == depth, total, 0.0)
        run, at = patch >> 11, (patch >> 6) & (PLANE - 1)
        place = (at & (PER_ROW - 1)) * PATCH_DEV + (patch & (PATCH_DEV - 1))
        turned = pltpu.roll(total, (place - depth) & (CZ - 1), 1)
        to = run * N_NORTH + ((patch >> 3) & (N_NORTH - 1))
        parts[to, pl.ds(at >> 4, 1), :] += turned


def spread_kernel(parts, out):
    total = jnp.sum(parts[...], axis=0)
    for row in range(ROWS):
        out[row * PER_ROW : (row + 1) * PER_ROW] = jnp.broadcast_to(
            total[row : row + 1][None], (PER_ROW, 1, CZ)
        )


def own_kernel(parts, out):
    total = jnp.sum(parts[...], axis=0)
    at = lax.axis_index("east") & (PER_ROW - 1)
    turned = pltpu.roll(total, (CZ - at * PATCH_DEV) & (CZ - 1), 1)
    out[...] = turned[:, 0:PATCH_DEV]


def path(axis, count, ahead):
    if ahead:
        return functools.partial(lax.ppermute, axis_name=axis, perm=[(i, i + 1) for i in range(count - 1)])
    return functools.partial(lax.ppermute, axis_name=axis, perm=[(i + 1, i) for i in range(count - 1)])


def swap(strips):
    east_low, east_high, north_low, north_high = strips
    n_east, n_north = lax.axis_size("east"), lax.axis_size("north")
    return (
        path("east", n_east, True)(east_high),
        path("east", n_east, False)(east_low),
        path("north", n_north, True)(north_high),
        path("north", n_north, False)(north_low),
    )


def body(field_prev, field_now, speed_sq, mechanism, sub_cells, sub_patch):
    params = pltpu.CompilerParams(vmem_limit_bytes=LIMIT)
    field = jax.ShapeDtypeStruct((3, CE, CN, CZ), jnp.float32)
    wide = pltpu.VMEM((3 * CE, CN + 16, CZ), jnp.float32)
    strips = pl.pallas_call(
        strips_kernel, out_shape=strip_shapes(), in_specs=[VMEM], out_specs=[VMEM] * 4,
        compiler_params=params, name="strips",
    )(field_now)
    halos = swap(strips)
    field_next, *strips = pl.pallas_call(
        first_kernel, out_shape=[field] + strip_shapes(), in_specs=[VMEM] * 7,
        out_specs=[VMEM] * 5, scratch_shapes=[wide], compiler_params=params, name="first",
    )(field_prev, field_now, speed_sq, *halos)
    halos = swap(strips)
    parts = jax.ShapeDtypeStruct((COLUMN, ROWS, CZ), jnp.float32)
    field_last, parts = pl.pallas_call(
        second_kernel, out_shape=[field, parts], in_specs=[VMEM] * 7 + [SMEM] * 3,
        out_specs=[VMEM] * 2, scratch_shapes=[wide], compiler_params=params, name="second",
    )(field_now, field_next, speed_sq, *halos, mechanism, sub_cells, sub_patch)
    parts = lax.all_to_all(parts, BOTH, 0, 0, tiled=True, axis_index_groups=column_groups())
    parts = pl.pallas_call(
        spread_kernel, out_shape=jax.ShapeDtypeStruct((PLANE, 1, CZ), jnp.float32),
        in_specs=[VMEM], out_specs=VMEM, compiler_params=params, name="spread",
    )(parts)
    parts = lax.all_to_all(parts, BOTH, 0, 0, tiled=True, axis_index_groups=plane_groups())
    own = pl.pallas_call(
        own_kernel, out_shape=jax.ShapeDtypeStruct((1, PATCH_DEV), jnp.float32),
        in_specs=[VMEM], out_specs=VMEM, compiler_params=params, name="own",
    )(parts)
    return field_next, field_last, own.reshape(PATCH_DEV)


def solution(mesh):
    in_specs = (
        P(None, "east", "north", None),
        P(None, "east", "north", None),
        P("east", "north", None),
        P(None, BOTH),
        P(BOTH),
        P(BOTH),
    )
    out_specs = (
        P(None, "east", "north", None),
        P(None, "east", "north", None),
        P(BOTH),
    )
    return jax.shard_map(body, mesh=mesh, in_specs=in_specs, out_specs=out_specs, check_vma=False)
```

time: 199 us -> 91.9 us (0.46)
  blocking collectives: 120 us -> 43.1 us
  local copies, waits for them, and re-layouts: 33.6 us -> 2.99 us
  Pallas kernels: 0 us -> 4.19 us
  other arithmetic: 3.7 us -> 0 us
    unnamed x1 -> x0, blocking collectives: 120 us -> none
    all_to_all x0 -> x2, blocking collectives: none -> 43.1 us  [the longest x1 30.2 us: body(): lax.all_to_all(parts, BOTH, 0, 0, tiled=True, axis_index_groups=column_gr...]
    add x2 -> x0, local copies, waits for them, and re-layouts: 17.2 us -> none  [advance(): return 2.0 * middle - before + speed_sq[None] * laplace_valid(widened)]
    gather x2 -> x0, local copies, waits for them, and re-layouts: 12.7 us -> none  [the longest x1 6.33 us: body(): sample_last = jnp.take(flat_last, sub_cells, axis=1)]
    pallas_call x0 -> x5, Pallas kernels: none -> 4.19 us  [the longest x1 2.13 us: body(): pl.pallas_call(second_kernel, out_shape=[field, parts], in_specs=[VMEM] *...]
    unnamed x16 -> x14, local copies, waits for them, and re-layouts: 0.8 us -> 2.99 us
  transfers between devices with their start and end apart: 8 -> 8, of which waited for: 4 -> 2; matrix products, arithmetic and copies ran while one was open for 9% -> 0% of each run, Pallas kernels for 0% -> 0%
where the time goes in v1:
time: 91.9 us; the launch traced here: 91.4 us
  blocking collectives  43.1 us (47%)
  starting transfers between devices  29.2 us (32%)
  waiting for transfers between devices  11.1 us (12%)
  Pallas kernels  4.19 us (5%)
  local copies, waits for them, and re-layouts  2.99 us (3%)
    all_to_all x1, blocking collectives, body(): lax.all_to_all(parts, BOTH, 0, 0, tiled=True, axis_index_groups=column_gr...  30.2 us
    ppermute x2, starting transfers between devices, swap(): path('north', n_north, True)(north_high)  13.6 us
    all_to_all x1, blocking collectives, body(): lax.all_to_all(parts, BOTH, 0, 0, tiled=True, axis_index_groups=plane_gro...  12.9 us
    ppermute x2, waiting for transfers between devices, swap(): path('north', n_north, False)(north_low)  11.1 us
    ppermute x2, starting transfers between devices, swap(): path('east', n_east, True)(east_high)  8.47 us
    ppermute x2, starting transfers between devices, swap(): path('north', n_north, False)(north_low)  4.52 us
    unnamed x14, local copies, waits for them, and re-layouts  2.99 us
    ppermute x2, starting transfers between devices, swap(): path('east', n_east, False)(east_low)  2.58 us
  transfers between devices with their start and end apart: 8, of which 2 were waited for; matrix products, arithmetic and copies ran while one was open for 0% of the time, Pallas kernels for 0%

profile of v1, /device:TPU:1, one launch (start us, length us, event | category | flops | bytes accessed | tf_op | source)
XLA Modules:
  0.0 91.4 jit_solution(11784466689790986387)
XLA Ops:
  0.6 0.0 copy-start
  0.6 1.0 %copy-done = f32[3,8,32,128]{3,2,1,0:T(8,128)S(1)} copy-done((f32[3,8,32,128]{3,2,1,0:T(8,128)S(1)}, f32[3,8,32,128]{3,2,1,0:T(8,128)}, u32[]{:S(2)}) %copy-start) | copy-done | bytes 393240
  1.7 4.1 %collective-permute-start = (f32[3,2,32,128]{3,2,1,0:T(8,128)S(1)}, f32[3,2,32,128]{3,2,1,0:T(8,128)S(1)}, u32[]{:S(2)}, u32[]{:S(2)}) collective-permute-start(f32[3,2,32,128]{3,2,1,0:T(8,128)S(1)} %get-tuple-element.14), channel_id=1, source_target_pairs={{0,8},{8,16},{16,24},{24,32},{32,40},{40,48},{48,56},{56,64},{64,7... | collective-permute-start | bytes 294920 | tf_op jit(solution)/shard_map/ppermute | solution.py:143
  5.8 1.3 %collective-permute-start.1 = (f32[3,2,32,128]{3,2,1,0:T(8,128)S(1)}, f32[3,2,32,128]{3,2,1,0:T(8,128)S(1)}, u32[]{:S(2)}, u32[]{:S(2)}) collective-permute-start(f32[3,2,32,128]{3,2,1,0:T(8,128)S(1)} %get-tuple-element.15), channel_id=1, source_target_pairs={{8,0},{16,8},{24,16},{32,24},{40,32},{48,40},{56,48},{64,56},{72,6... | collective-permute-start | bytes 294920 | tf_op jit(solution)/shard_map/ppermute | solution.py:144
  7.1 8.5 %collective-permute-start.2 = (f32[48,128]{1,0:T(8,128)S(1)}, f32[48,128]{1,0:T(8,128)S(1)}, u32[]{:S(2)}, u32[]{:S(2)}) collective-permute-start(f32[48,128]{1,0:T(8,128)S(1)} %get-tuple-element.16), channel_id=1, source_target_pairs={{0,1},{1,2},{2,3},{3,4},{4,5},{5,6},{6,7},{8,9},{9,10},{10,11},{11... | collective-permute-start | bytes 73736 | tf_op jit(solution)/shard_map/ppermute | solution.py:145
  15.5 2.6 %collective-permute-start.3 = (f32[48,128]{1,0:T(8,128)S(1)}, f32[48,128]{1,0:T(8,128)S(1)}, u32[]{:S(2)}, u32[]{:S(2)}) collective-permute-start(f32[48,128]{1,0:T(8,128)S(1)} %get-tuple-element.17), channel_id=1, source_target_pairs={{1,0},{2,1},{3,2},{4,3},{5,4},{6,5},{7,6},{9,8},{10,9},{11,10},{12... | collective-permute-start | bytes 73736 | tf_op jit(solution)/shard_map/ppermute | solution.py:146
  18.1 0.0 collective-permute-done.2.s
  18.1 4.3 %collective-permute-done.3.n = f32[48,128]{1,0:T(8,128)S(1)} collective-permute-done((f32[48,128]{1,0:T(8,128)S(1)}, f32[48,128]{1,0:T(8,128)S(1)}, u32[]{:S(2)}, u32[]{:S(2)}) %collective-permute-start.3) | collective-permute-done | bytes 24608 | tf_op jit(solution)/shard_map/ppermute | solution.py:146
  22.5 0.0 collective-permute-done.w
  22.5 0.0 collective-permute-done.1.e
  22.5 0.0 copy-done.1
  22.5 0.0 copy-start.2
  22.5 1.0 %copy-done.2 = f32[3,8,32,128]{3,2,1,0:T(8,128)S(1)} copy-done((f32[3,8,32,128]{3,2,1,0:T(8,128)S(1)}, f32[3,8,32,128]{3,2,1,0:T(8,128)}, u32[]{:S(2)}) %copy-start.2) | copy-done | bytes 393240
  23.5 1.4 %first.1 = (f32[3,8,32,128]{3,2,1,0:T(8,128)}, f32[3,2,32,128]{3,2,1,0:T(8,128)S(1)}, f32[3,2,32,128]{3,2,1,0:T(8,128)S(1)}, f32[48,128]{1,0:T(8,128)S(1)}, f32[48,128]{1,0:T(8,128)S(1)}) custom-call(f32[3,8,32,128]{3,2,1,0:T(8,128)S(1)} %copy-done.2, f32[3,8,32,128]{3,2,1,0:T(8,128)S(1)} %copy-done, f32[8,32,128]{2,1,0:T(8,128)S(1)} %copy-done.1, ...), custom_call_target="tpu_custom_call" | custom-call | tf_op jit(solution)/shard_map/first/pallas_call | solution.py:159
  24.9 4.4 %collective-permute-start.4 = (f32[3,2,32,128]{3,2,1,0:T(8,128)S(1)}, f32[3,2,32,128]{3,2,1,0:T(8,128)S(1)}, u32[]{:S(2)}, u32[]{:S(2)}) collective-permute-start(f32[3,2,32,128]{3,2,1,0:T(8,128)S(1)} %get-tuple-element.19), channel_id=1, source_target_pairs={{0,8},{8,16},{16,24},{24,32},{32,40},{40,48},{48,56},{56,64},{64,7... | collective-permute-start | bytes 294920 | tf_op jit(solution)/shard_map/ppermute | solution.py:143
  29.3 1.3 %collective-permute-start.5 = (f32[3,2,32,128]{3,2,1,0:T(8,128)S(1)}, f32[3,2,32,128]{3,2,1,0:T(8,128)S(1)}, u32[]{:S(2)}, u32[]{:S(2)}) collective-permute-start(f32[3,2,32,128]{3,2,1,0:T(8,128)S(1)} %get-tuple-element.20), channel_id=1, source_target_pairs={{8,0},{16,8},{24,16},{32,24},{40,32},{48,40},{56,48},{64,56},{72,6... | collective-permute-start | bytes 294920 | tf_op jit(solution)/shard_map/ppermute | solution.py:144
  30.6 5.2 %collective-permute-start.6 = (f32[48,128]{1,0:T(8,128)S(1)}, f32[48,128]{1,0:T(8,128)S(1)}, u32[]{:S(2)}, u32[]{:S(2)}) collective-permute-start(f32[48,128]{1,0:T(8,128)S(1)} %get-tuple-element.21), channel_id=1, source_target_pairs={{0,1},{1,2},{2,3},{3,4},{4,5},{5,6},{6,7},{8,9},{9,10},{10,11},{11... | collective-permute-start | bytes 73736 | tf_op jit(solution)/shard_map/ppermute | solution.py:145
  35.7 0.0 copy-start.5
  35.7 0.0 copy-start.6
  35.7 1.9 %collective-permute-start.7 = (f32[48,128]{1,0:T(8,128)S(1)}, f32[48,128]{1,0:T(8,128)S(1)}, u32[]{:S(2)}, u32[]{:S(2)}) collective-permute-start(f32[48,128]{1,0:T(8,128)S(1)} %get-tuple-element.22), channel_id=1, source_target_pairs={{1,0},{2,1},{3,2},{4,3},{5,4},{6,5},{7,6},{9,8},{10,9},{11,10},{12... | collective-permute-start | bytes 73736 | tf_op jit(solution)/shard_map/ppermute | solution.py:146
  37.7 0.0 collective-permute-done.6.s
  37.7 6.8 %collective-permute-done.7.n = f32[48,128]{1,0:T(8,128)S(1)} collective-permute-done((f32[48,128]{1,0:T(8,128)S(1)}, f32[48,128]{1,0:T(8,128)S(1)}, u32[]{:S(2)}, u32[]{:S(2)}) %collective-permute-start.7) | collective-permute-done | bytes 24608 | tf_op jit(solution)/shard_map/ppermute | solution.py:146
  44.4 0.0 collective-permute-done.4.w
  44.4 0.0 collective-permute-done.5.e
  44.4 0.0 copy-done.4
  44.4 0.0 copy-done.5
  44.5 0.0 copy-start.3
  44.5 1.0 %copy-done.3 = f32[3,8,32,128]{3,2,1,0:T(8,128)S(1)} copy-done((f32[3,8,32,128]{3,2,1,0:T(8,128)S(1)}, f32[3,8,32,128]{3,2,1,0:T(8,128)}, u32[]{:S(2)}) %copy-start.3) | copy-done | bytes 393240
  45.5 2.1 %second.1 = (f32[3,8,32,128]{3,2,1,0:T(8,128)}, f32[24,2,128]{2,1,0:T(2,128)S(1)}) custom-call(f32[3,8,32,128]{3,2,1,0:T(8,128)S(1)} %copy-done, f32[3,8,32,128]{3,2,1,0:T(8,128)S(1)} %copy-done.3, f32[8,32,128]{2,1,0:T(8,128)S(1)} %copy-done.1, f32[3,2,32,128]{3,2,1,0:T(8,128)S(1)} %collective-permute-done.4.w, ...), custom_call_target="tpu_custom_call" | custom-call | tf_op jit(solution)/shard_map/second/pallas_call | solution.py:165
  47.6 30.2 %all_to_all.10.parts = f32[24,2,128]{2,1,0:T(2,128)S(1)} all-to-all(f32[24,2,128]{2,1,0:T(2,128)S(1)} %get-tuple-element.24), channel_id=1, replica_groups={{0,1,2,3,4,5,6,7,256,257,258,259,260,261,262,263,512,513,514,515,516,51..., dimensions={0} | all-to-all | bytes 49152 | tf_op jit(solution)/shard_map/all_to_all | solution.py:169
  77.9 12.9 %all_to_all.11.parts = f32[32,1,128]{2,1,0:T(1,128)S(1)} all-to-all(f32[32,1,128]{2,1,0:T(1,128)S(1)} %spread.1), channel_id=1, replica_groups={{0,8,16,24,32,40,48,56,64,72,80,88,96,104,112,120,128,136,144,152,160,1..., dimensions={0} | all-to-all | bytes 32768 | tf_op jit(solution)/shard_map/all_to_all | solution.py:174
  90.8 0.6 own.1
  (5 shorter events, 0.1 us)
Async XLA Ops:
  0.6 1.0 %copy-start = (f32[3,8,32,128]{3,2,1,0:T(8,128)S(1)}, f32[3,8,32,128]{3,2,1,0:T(8,128)}, u32[]{:S(2)}) copy-start(f32[3,8,32,128]{3,2,1,0:T(8,128)} %before.3) | copy-start | bytes 1179652
  1.6 20.8 %copy-start.1 = (f32[8,32,128]{2,1,0:T(8,128)S(1)}, f32[8,32,128]{2,1,0:T(8,128)}, u32[]{:S(2)}) copy-start(f32[8,32,128]{2,1,0:T(8,128)} %speed_sq.3) | copy-start | bytes 393220
  1.7 20.8 %collective-permute-start = (f32[3,2,32,128]{3,2,1,0:T(8,128)S(1)}, f32[3,2,32,128]{3,2,1,0:T(8,128)S(1)}, u32[]{:S(2)}, u32[]{:S(2)}) collective-permute-start(f32[3,2,32,128]{3,2,1,0:T(8,128)S(1)} %get-tuple-element.14), channel_id=1, source_target_pairs={{0,8},{8,16},{16,24},{24,32},{32,40},{40,48},{48,56},{56,64},{64,7... | collective-permute-start | bytes 294920 | tf_op jit(solution)/shard_map/ppermute | solution.py:143
  5.8 16.7 %collective-permute-start.1 = (f32[3,2,32,128]{3,2,1,0:T(8,128)S(1)}, f32[3,2,32,128]{3,2,1,0:T(8,128)S(1)}, u32[]{:S(2)}, u32[]{:S(2)}) collective-permute-start(f32[3,2,32,128]{3,2,1,0:T(8,128)S(1)} %get-tuple-element.15), channel_id=1, source_target_pairs={{8,0},{16,8},{24,16},{32,24},{40,32},{48,40},{56,48},{64,56},{72,6... | collective-permute-start | bytes 294920 | tf_op jit(solution)/shard_map/ppermute | solution.py:144
  7.1 11.1 %collective-permute-start.2 = (f32[48,128]{1,0:T(8,128)S(1)}, f32[48,128]{1,0:T(8,128)S(1)}, u32[]{:S(2)}, u32[]{:S(2)}) collective-permute-start(f32[48,128]{1,0:T(8,128)S(1)} %get-tuple-element.16), channel_id=1, source_target_pairs={{0,1},{1,2},{2,3},{3,4},{4,5},{5,6},{6,7},{8,9},{9,10},{10,11},{11... | collective-permute-start | bytes 73736 | tf_op jit(solution)/shard_map/ppermute | solution.py:145
  15.5 6.9 %collective-permute-start.3 = (f32[48,128]{1,0:T(8,128)S(1)}, f32[48,128]{1,0:T(8,128)S(1)}, u32[]{:S(2)}, u32[]{:S(2)}) collective-permute-start(f32[48,128]{1,0:T(8,128)S(1)} %get-tuple-element.17), channel_id=1, source_target_pairs={{1,0},{2,1},{3,2},{4,3},{5,4},{6,5},{7,6},{9,8},{10,9},{11,10},{12... | collective-permute-start | bytes 73736 | tf_op jit(solution)/shard_map/ppermute | solution.py:146
  22.5 1.0 %copy-start.2 = (f32[3,8,32,128]{3,2,1,0:T(8,128)S(1)}, f32[3,8,32,128]{3,2,1,0:T(8,128)}, u32[]{:S(2)}) copy-start(f32[3,8,32,128]{3,2,1,0:T(8,128)} %before.2) | copy-start | bytes 1179652
  24.9 19.6 %copy-start.4 = (f32[6,16]{1,0:T(8,128)S(1)}, f32[6,16]{1,0:T(8,128)}, u32[]{:S(2)}) copy-start(f32[6,16]{1,0:T(8,128)} %mechanism.1) | copy-start | bytes 1156
  24.9 19.6 %collective-permute-start.4 = (f32[3,2,32,128]{3,2,1,0:T(8,128)S(1)}, f32[3,2,32,128]{3,2,1,0:T(8,128)S(1)}, u32[]{:S(2)}, u32[]{:S(2)}) collective-permute-start(f32[3,2,32,128]{3,2,1,0:T(8,128)S(1)} %get-tuple-element.19), channel_id=1, source_target_pairs={{0,8},{8,16},{16,24},{24,32},{32,40},{40,48},{48,56},{56,64},{64,7... | collective-permute-start | bytes 294920 | tf_op jit(solution)/shard_map/ppermute | solution.py:143
  29.3 15.2 %collective-permute-start.5 = (f32[3,2,32,128]{3,2,1,0:T(8,128)S(1)}, f32[3,2,32,128]{3,2,1,0:T(8,128)S(1)}, u32[]{:S(2)}, u32[]{:S(2)}) collective-permute-start(f32[3,2,32,128]{3,2,1,0:T(8,128)S(1)} %get-tuple-element.20), channel_id=1, source_target_pairs={{8,0},{16,8},{24,16},{32,24},{40,32},{48,40},{56,48},{64,56},{72,6... | collective-permute-start | bytes 294920 | tf_op jit(solution)/shard_map/ppermute | solution.py:144
  30.6 7.1 %collective-permute-start.6 = (f32[48,128]{1,0:T(8,128)S(1)}, f32[48,128]{1,0:T(8,128)S(1)}, u32[]{:S(2)}, u32[]{:S(2)}) collective-permute-start(f32[48,128]{1,0:T(8,128)S(1)} %get-tuple-element.21), channel_id=1, source_target_pairs={{0,1},{1,2},{2,3},{3,4},{4,5},{5,6},{6,7},{8,9},{9,10},{10,11},{11... | collective-permute-start | bytes 73736 | tf_op jit(solution)/shard_map/ppermute | solution.py:145
  35.7 8.7 %copy-start.5 = (s32[16]{0:T(128)S(1)}, s32[16]{0:T(128)}, u32[]{:S(2)}) copy-start(s32[16]{0:T(128)} %cells.1) | copy-start | bytes 196
  35.7 8.7 %copy-start.6 = (s32[16]{0:T(128)S(1)}, s32[16]{0:T(128)}, u32[]{:S(2)}) copy-start(s32[16]{0:T(128)} %patches.1) | copy-start | bytes 196
  35.7 8.7 %collective-permute-start.7 = (f32[48,128]{1,0:T(8,128)S(1)}, f32[48,128]{1,0:T(8,128)S(1)}, u32[]{:S(2)}, u32[]{:S(2)}) collective-permute-start(f32[48,128]{1,0:T(8,128)S(1)} %get-tuple-element.22), channel_id=1, source_target_pairs={{1,0},{2,1},{3,2},{4,3},{5,4},{6,5},{7,6},{9,8},{10,9},{11,10},{12... | collective-permute-start | bytes 73736 | tf_op jit(solution)/shard_map/ppermute | solution.py:146
  44.5 1.0 %copy-start.3 = (f32[3,8,32,128]{3,2,1,0:T(8,128)S(1)}, f32[3,8,32,128]{3,2,1,0:T(8,128)}, u32[]{:S(2)}) copy-start(f32[3,8,32,128]{3,2,1,0:T(8,128)} %get-tuple-element.11.middle) | copy-start | bytes 1179652

commit v2 on v1

v2 whole, which is shorter than its diff:
```python
import jax
import jax.numpy as jnp
from jax import lax
from jax.experimental import pallas as pl
from jax.experimental.pallas import tpu as pltpu
from jax.sharding import PartitionSpec as P

BOTH = ("east", "north")
CE, CN, CZ = 8, 32, 128
SUBS = 16
N_NORTH = 8
PLANE = 32
Z_RUN = 3
COLUMN = Z_RUN * N_NORTH
PATCH_DEV = 8
PER_ROW = CZ // PATCH_DEV
ROWS = PLANE // PER_ROW
VMEM = pl.BlockSpec(memory_space=pltpu.VMEM)
SMEM = pl.BlockSpec(memory_space=pltpu.SMEM)
HBM = pl.BlockSpec(memory_space=pltpu.HBM)
LIMIT = 32 * 1024 * 1024

E_PREV, E_SPEED, E_LEN = 12, 18, 20
N_PREV, N_SPEED, N_LEN = 144, 192, 208
TOP = 16
LAYERS = CE + 4


def column_groups():
    return [
        [(run * PLANE + at) * N_NORTH + n for run in range(Z_RUN) for n in range(N_NORTH)]
        for at in range(PLANE)
    ]


def plane_groups():
    return [
        [(run * PLANE + at) * N_NORTH + n for at in range(PLANE)]
        for run in range(Z_RUN)
        for n in range(N_NORTH)
    ]


def swap(block, axis, first):
    pairs = [(i, i + 1) for i in range(first, lax.axis_size(axis) - 1, 2)]
    return lax.ppermute(block, axis, pairs + [(j, i) for i, j in pairs])


def east_kernel(before, middle, speed_sq, low_pair, high_pair, sems):
    odd = lax.axis_index("east") & 1
    copies = []
    for message, high in ((low_pair, 1 - odd), (high_pair, odd)):
        four, two = high * (CE - 4), high * (CE - 2)
        for c in range(3):
            copies.append((middle.at[c, pl.ds(four, 4)], message.at[pl.ds(c * 4, 4)]))
            copies.append((before.at[c, pl.ds(two, 2)], message.at[pl.ds(E_PREV + c * 2, 2)]))
        copies.append((speed_sq.at[pl.ds(two, 2)], message.at[pl.ds(E_SPEED, 2)]))
    started = [pltpu.make_async_copy(a, b, sems.at[i]) for i, (a, b) in enumerate(copies)]
    for copy in started:
        copy.start()
    for copy in started:
        copy.wait()


def east_layers(low_pair, high_pair):
    odd = (lax.axis_index("east") & 1) == 1

    def west(k, rows=slice(None)):
        return jnp.where(odd, low_pair[k, rows], high_pair[k, rows])

    def east(k, rows=slice(None)):
        return jnp.where(odd, high_pair[k, rows], low_pair[k, rows])

    return west, east


def north_kernel(before, middle, speed_sq, low_pair, high_pair, near, far):
    odd = (lax.axis_index("north") & 1) == 1
    west, east = east_layers(low_pair, high_pair)

    def put(at, count, low, high):
        near[at : at + count, :] = jnp.where(odd, low, high)
        far[at : at + count, :] = jnp.where(odd, high, low)

    bottom, top = slice(0, 4), slice(CN - 4, CN)
    for c in range(3):
        for k in range(2):
            put((c * LAYERS + k) * 4, 4, west(c * 4 + 2 + k, bottom), west(c * 4 + 2 + k, top))
            put((c * LAYERS + CE + 2 + k) * 4, 4, east(c * 4 + k, bottom), east(c * 4 + k, top))
        for e in range(CE):
            put((c * LAYERS + 2 + e) * 4, 4, middle[c, e, 0:4, :], middle[c, e, CN - 4 : CN, :])
            put(N_PREV + (c * CE + e) * 2, 2, before[c, e, 0:2, :], before[c, e, CN - 2 : CN, :])
    for e in range(CE):
        put(N_SPEED + e * 2, 2, speed_sq[e, 0:2, :], speed_sq[e, CN - 2 : CN, :])


def laplace(here, near, far):
    lane = lax.broadcasted_iota(jnp.int32, here.shape, 1)
    near += jnp.where(lane >= 1, pltpu.roll(here, 1, 1), 0.0)
    near += jnp.where(lane < CZ - 1, pltpu.roll(here, CZ - 1, 1), 0.0)
    far += jnp.where(lane >= 2, pltpu.roll(here, 2, 1), 0.0)
    far += jnp.where(lane < CZ - 2, pltpu.roll(here, CZ - 2, 1), 0.0)
    return near * (16.0 / 12.0) - far * (1.0 / 12.0) - here * 7.5


def steps_kernel(
    before, middle, speed_sq, low_pair, high_pair, near_pair, far_pair, mechanism, cells, patches,
    field_next, field_last, parts, wide, later, edge_before, edge_speed,
):
    west, east = east_layers(low_pair, high_pair)
    odd_north = (lax.axis_index("north") & 1) == 1

    def south(at, count):
        return jnp.where(odd_north, near_pair[pl.ds(at, count), :], far_pair[pl.ds(at, count), :])

    def north(at, count):
        return jnp.where(odd_north, far_pair[pl.ds(at, count), :], near_pair[pl.ds(at, count), :])

    for e in range(CE):
        edge_speed[e, 6:8, :] = south(N_SPEED + e * 2, 2)
        edge_speed[e, 8:10, :] = north(N_SPEED + e * 2, 2)

    def first(c, carry):
        def layer(k):
            if k < 0:
                return west(c * 4 + k + 4)
            if k >= CE:
                return east(c * 4 + k - CE)
            return middle[c, k]

        for e in range(-2, CE + 2):
            k = e + 2
            at = pl.multiple_of((c * LAYERS + k) * 4, 4)
            wide[c, k, TOP : TOP + CN, :] = layer(e)
            wide[c, k, TOP - 4 : TOP, :] = south(at, 4)
            wide[c, k, TOP + CN : TOP + CN + 4, :] = north(at, 4)
        for e in range(-2, CE + 2):
            k = e + 2

            def rows(offset, count=CN):
                return wide[c, k, TOP + offset : TOP + offset + count, :]

            here = rows(0)
            total = laplace(
                here,
                layer(e - 1) + layer(e + 1) + rows(-1) + rows(1),
                layer(e - 2) + layer(e + 2) + rows(-2) + rows(2),
            )
            if 0 <= e < CE:
                old, speed = before[c, e], speed_sq[e]
            elif e < 0:
                old, speed = west(E_PREV + c * 2 + k), west(E_SPEED + k)
            else:
                old, speed = east(E_PREV + c * 2 + e - CE), east(E_SPEED + e - CE)
            new = 2.0 * here - old + speed * total
            later[c, k, TOP : TOP + CN, :] = new
            if 0 <= e < CE:
                field_next[c, e] = new
        for e in range(CE):
            k = e + 2
            at = pl.multiple_of(N_PREV + (c * CE + e) * 2, 2)
            edge_before[k, 6:8, :] = south(at, 2)
            edge_before[k, 8:10, :] = north(at, 2)
            for start, edge, kept in ((TOP - 8, 0, slice(6, 8)), (TOP + CN, 8, slice(0, 2))):

                def tile(layers, offset):
                    return wide[c, k + layers, start + offset : start + offset + 8, :]

                here = tile(0, 0)
                total = laplace(
                    here,
                    tile(-1, 0) + tile(1, 0) + tile(0, -1) + tile(0, 1),
                    tile(-2, 0) + tile(2, 0) + tile(0, -2) + tile(0, 2),
                )
                old, speed = edge_before[k, edge : edge + 8, :], edge_speed[e, edge : edge + 8, :]
                new = 2.0 * here - old + speed * total
                later[c, k, start + kept.start : start + kept.stop, :] = new[kept]
        return carry

    lax.fori_loop(0, 3, first, 0)

    def second(c, carry):
        for e in range(CE):
            k = e + 2

            def rows(layers, offset=0):
                return later[c, k + layers, TOP + offset : TOP + offset + CN, :]

            here = rows(0)
            total = laplace(
                here,
                rows(-1) + rows(1) + rows(0, -1) + rows(0, 1),
                rows(-2) + rows(2) + rows(0, -2) + rows(0, 2),
            )
            field_last[c, e] = 2.0 * here - middle[c, e] + speed_sq[e] * total
        return carry

    lax.fori_loop(0, 3, second, 0)

    lane = lax.broadcasted_iota(jnp.int32, (1, CZ), 1)
    parts[...] = jnp.zeros_like(parts)
    for i in range(SUBS):
        cell, patch = cells[i], patches[i]
        layer, row, depth = cell >> 12, (cell >> 7) & (CN - 1), cell & (CZ - 1)
        total = jnp.zeros((1, CZ), jnp.float32)
        for c in range(3):
            total += mechanism[c, i] * field_next[c, layer, pl.ds(row, 1), :]
            total += mechanism[3 + c, i] * field_last[c, layer, pl.ds(row, 1), :]
        total = jnp.where(lane == depth, total, 0.0)
        run, at = patch >> 11, (patch >> 6) & (PLANE - 1)
        place = (at & (PER_ROW - 1)) * PATCH_DEV + (patch & (PATCH_DEV - 1))
        turned = pltpu.roll(total, (place - depth) & (CZ - 1), 1)
        to = run * N_NORTH + ((patch >> 3) & (N_NORTH - 1))
        parts[to, pl.ds(at >> 4, 1), :] += turned


def spread_kernel(parts, out):
    total = jnp.sum(parts[...], axis=0)
    for row in range(ROWS):
        out[row * PER_ROW : (row + 1) * PER_ROW] = jnp.broadcast_to(
            total[row : row + 1][None], (PER_ROW, 1, CZ)
        )


def own_kernel(parts, out):
    total = jnp.sum(parts[...], axis=0)
    at = lax.axis_index("east") & (PER_ROW - 1)
    turned = pltpu.roll(total, (CZ - at * PATCH_DEV) & (CZ - 1), 1)
    out[...] = turned[:, 0:PATCH_DEV]


def body(field_prev, field_now, speed_sq, mechanism, sub_cells, sub_patch):
    params = pltpu.CompilerParams(vmem_limit_bytes=LIMIT)
    f32 = jnp.float32
    field = jax.ShapeDtypeStruct((3, CE, CN, CZ), f32)
    message = jax.ShapeDtypeStruct((E_LEN, CN, CZ), f32)
    low_pair, high_pair = pl.pallas_call(
        east_kernel, out_shape=[message] * 2, in_specs=[HBM] * 3, out_specs=[VMEM] * 2,
        scratch_shapes=[pltpu.SemaphoreType.DMA((14,))], compiler_params=params, name="east_strips",
    )(field_prev, field_now, speed_sq)
    pairs = swap(low_pair, "east", 0), swap(high_pair, "east", 1)
    message = jax.ShapeDtypeStruct((N_LEN, CZ), f32)
    near, far = pl.pallas_call(
        north_kernel, out_shape=[message] * 2, in_specs=[VMEM] * 5, out_specs=[VMEM] * 2,
        compiler_params=params, name="north_strips",
    )(field_prev, field_now, speed_sq, *pairs)
    far_pair = swap(far, "north", 1)
    near_pair = swap(near, "north", 0)
    wide = pltpu.VMEM((3, LAYERS, CN + 2 * TOP, CZ), f32)
    parts = jax.ShapeDtypeStruct((COLUMN, ROWS, CZ), f32)
    field_next, field_last, parts = pl.pallas_call(
        steps_kernel, out_shape=[field, field, parts], in_specs=[VMEM] * 7 + [SMEM] * 3,
        out_specs=[VMEM] * 3,
        scratch_shapes=[wide, wide, pltpu.VMEM((LAYERS, 16, CZ), f32), pltpu.VMEM((CE, 16, CZ), f32)],
        compiler_params=params, name="steps",
    )(field_prev, field_now, speed_sq, *pairs, near_pair, far_pair, mechanism, sub_cells, sub_patch)
    parts = lax.all_to_all(parts, BOTH, 0, 0, tiled=True, axis_index_groups=column_groups())
    parts = pl.pallas_call(
        spread_kernel, out_shape=jax.ShapeDtypeStruct((PLANE, 1, CZ), f32),
        in_specs=[VMEM], out_specs=VMEM, compiler_params=params, name="spread",
    )(parts)
    parts = lax.all_to_all(parts, BOTH, 0, 0, tiled=True, axis_index_groups=plane_groups())
    own = pl.pallas_call(
        own_kernel, out_shape=jax.ShapeDtypeStruct((1, PATCH_DEV), f32),
        in_specs=[VMEM], out_specs=VMEM, compiler_params=params, name="own",
    )(parts)
    return field_next, field_last, own.reshape(PATCH_DEV)


def solution(mesh):
    in_specs = (
        P(None, "east", "north", None),
        P(None, "east", "north", None),
        P("east", "north", None),
        P(None, BOTH),
        P(BOTH),
        P(BOTH),
    )
    out_specs = (
        P(None, "east", "north", None),
        P(None, "east", "north", None),
        P(BOTH),
    )
    return jax.shard_map(body, mesh=mesh, in_specs=in_specs, out_specs=out_specs, check_vma=False)
```

time: 91.9 us -> 80.8 us (0.88)
  starting transfers between devices: 29.2 us -> 19.5 us
  waiting for transfers between devices: 11.1 us -> 9.65 us
    ppermute x8 -> x4, starting transfers between devices: 29.2 us -> 19.5 us  [swap(): return lax.ppermute(block, axis, pairs + [(j, i) for i, j in pairs])]
    all_to_all x1, blocking collectives: 30.2 us -> 27.8 us  [body(): lax.all_to_all(parts, BOTH, 0, 0, tiled=True, axis_index_groups=column_gr...]
    all_to_all x1, blocking collectives: 12.9 us -> 14.9 us  [body(): lax.all_to_all(parts, BOTH, 0, 0, tiled=True, axis_index_groups=plane_gro...]
    ppermute x8 -> x4, waiting for transfers between devices: 11.1 us -> 9.65 us  [swap(): return lax.ppermute(block, axis, pairs + [(j, i) for i, j in pairs])]
    unnamed x14 -> x12, local copies, waits for them, and re-layouts: 2.99 us -> 2.9 us
  transfers between devices with their start and end apart: 8 -> 4, of which waited for: 2 -> 2; matrix products, arithmetic and copies ran while one was open for 0% -> 0% of each run, Pallas kernels for 0% -> 0%
where the time goes in v2:
time: 80.8 us; the launch traced here: 80.5 us
  blocking collectives  42.6 us (53%)
  starting transfers between devices  19.5 us (24%)
  waiting for transfers between devices  9.65 us (12%)
  Pallas kernels  5.01 us (6%)
  local copies, waits for them, and re-layouts  2.9 us (4%)
    all_to_all x1, blocking collectives, body(): lax.all_to_all(parts, BOTH, 0, 0, tiled=True, axis_index_groups=column_gr...  27.8 us
    ppermute x4, starting transfers between devices, swap(): return lax.ppermute(block, axis, pairs + [(j, i) for i, j in pairs])  19.5 us
    all_to_all x1, blocking collectives, body(): lax.all_to_all(parts, BOTH, 0, 0, tiled=True, axis_index_groups=plane_gro...  14.9 us
    ppermute x4, waiting for transfers between devices, swap(): return lax.ppermute(block, axis, pairs + [(j, i) for i, j in pairs])  9.65 us
    pallas_call x1, Pallas kernels, body(): pl.pallas_call(steps_kernel, out_shape=[field, field, parts], in_specs=[V...  3.35 us
    unnamed x12, local copies, waits for them, and re-layouts  2.9 us
  transfers between devices with their start and end apart: 4, of which 2 were waited for; matrix products, arithmetic and copies ran while one was open for 0% of the time, Pallas kernels for 0%

profile of v2, /device:TPU:1, one launch (start us, length us, event | category | flops | bytes accessed | tf_op | source)
XLA Modules:
  0.0 80.5 jit_solution(12478949659864151541)
XLA Ops:
  0.6 0.0 copy-start
  0.6 1.0 %copy-done = f32[3,8,32,128]{3,2,1,0:T(8,128)S(1)} copy-done((f32[3,8,32,128]{3,2,1,0:T(8,128)S(1)}, f32[3,8,32,128]{3,2,1,0:T(8,128)}, u32[]{:S(2)}) %copy-start) | copy-done | bytes 393240
  1.6 0.0 copy-start.1
  1.6 1.0 %copy-done.1 = f32[3,8,32,128]{3,2,1,0:T(8,128)S(1)} copy-done((f32[3,8,32,128]{3,2,1,0:T(8,128)S(1)}, f32[3,8,32,128]{3,2,1,0:T(8,128)}, u32[]{:S(2)}) %copy-start.1) | copy-done | bytes 393240
  2.6 0.0 copy-start.2
  2.6 0.9 %copy-done.2 = f32[8,32,128]{2,1,0:T(8,128)S(1)} copy-done((f32[8,32,128]{2,1,0:T(8,128)S(1)}, f32[8,32,128]{2,1,0:T(8,128)}, u32[]{:S(2)}) %copy-start.2) | copy-done | bytes 131096
  3.5 1.0 %east_strips.1 = (f32[20,32,128]{2,1,0:T(8,128)S(1)}, f32[20,32,128]{2,1,0:T(8,128)S(1)}) custom-call(f32[3,8,32,128]{3,2,1,0:T(8,128)S(1)} %copy-done, f32[3,8,32,128]{3,2,1,0:T(8,128)S(1)} %copy-done.1, f32[8,32,128]{2,1,0:T(8,128)S(1)} %copy-done.2), custom_call_target="tpu_custom_call" | custom-call | tf_op jit(solution)/shard_map/east_strips/pallas_call | solution.py:237
  4.5 3.9 %collective-permute-start = (f32[20,32,128]{2,1,0:T(8,128)S(1)}, f32[20,32,128]{2,1,0:T(8,128)S(1)}, u32[]{:S(2)}, u32[]{:S(2)}) collective-permute-start(f32[20,32,128]{2,1,0:T(8,128)S(1)} %get-tuple-element.10), channel_id=1, source_target_pairs={{0,8},{16,24},{32,40},{48,56},{64,72},{80,88},{96,104},{112,120},{... | collective-permute-start | bytes 983048 | tf_op jit(solution)/shard_map/ppermute | solution.py:46
  8.5 0.7 collective-permute-start.1
  9.1 3.8 %collective-permute-done.low_pair = f32[20,32,128]{2,1,0:T(8,128)S(1)} collective-permute-done((f32[20,32,128]{2,1,0:T(8,128)S(1)}, f32[20,32,128]{2,1,0:T(8,128)S(1)}, u32[]{:S(2)}, u32[]{:S(2)}) %collective-permute-start) | collective-permute-done | bytes 327712 | tf_op jit(solution)/shard_map/ppermute | solution.py:46
  12.9 0.0 collective-permute-done.1.high_pair
  12.9 0.0 copy-start.3
  12.9 0.1 north_strips.1
  13.0 0.0 copy-start.4
  13.0 0.0 copy-start.5
  13.0 13.0 %collective-permute-start.2 = (f32[208,128]{1,0:T(8,128)S(1)}, f32[208,128]{1,0:T(8,128)S(1)}, u32[]{:S(2)}, u32[]{:S(2)}) collective-permute-start(f32[208,128]{1,0:T(8,128)S(1)} %get-tuple-element.12), channel_id=1, source_target_pairs={{0,1},{2,3},{4,5},{6,7},{1,0},{3,2},{5,4},{7,6},{8,9},{10,11},{12,... | collective-permute-start | bytes 319496 | tf_op jit(solution)/shard_map/ppermute | solution.py:46
  26.0 1.9 %collective-permute-start.3 = (f32[208,128]{1,0:T(8,128)S(1)}, f32[208,128]{1,0:T(8,128)S(1)}, u32[]{:S(2)}, u32[]{:S(2)}) collective-permute-start(f32[208,128]{1,0:T(8,128)S(1)} %get-tuple-element.13), channel_id=1, source_target_pairs={{1,2},{3,4},{5,6},{2,1},{4,3},{6,5},{9,10},{11,12},{13,14},{10,9},... | collective-permute-start | bytes 319496 | tf_op jit(solution)/shard_map/ppermute | solution.py:46
  27.9 0.0 collective-permute-done.2.near_pair
  27.9 5.9 %collective-permute-done.3.far_pair = f32[208,128]{1,0:T(8,128)S(1)} collective-permute-done((f32[208,128]{1,0:T(8,128)S(1)}, f32[208,128]{1,0:T(8,128)S(1)}, u32[]{:S(2)}, u32[]{:S(2)}) %collective-permute-start.3) | collective-permute-done | bytes 106528 | tf_op jit(solution)/shard_map/ppermute | solution.py:46
  33.8 0.0 copy-done.3
  33.8 0.0 copy-done.4
  33.8 0.0 copy-done.5
  33.8 3.3 %steps.1 = (f32[3,8,32,128]{3,2,1,0:T(8,128)}, f32[3,8,32,128]{3,2,1,0:T(8,128)}, f32[24,2,128]{2,1,0:T(2,128)S(1)}) custom-call(f32[3,8,32,128]{3,2,1,0:T(8,128)S(1)} %copy-done, f32[3,8,32,128]{3,2,1,0:T(8,128)S(1)} %copy-done.1, f32[8,32,128]{2,1,0:T(8,128)S(1)} %copy-done.2, f32[20,32,128]{2,1,0:T(8,128)S(1)} %collective-permute-done.low_pair, ...), custom_call_target="tpu_custom_call" | custom-call | tf_op jit(solution)/shard_map/steps/pallas_call | solution.py:251
  37.2 27.8 %all_to_all.10.parts = f32[24,2,128]{2,1,0:T(2,128)S(1)} all-to-all(f32[24,2,128]{2,1,0:T(2,128)S(1)} %get-tuple-element.16), channel_id=1, replica_groups={{0,1,2,3,4,5,6,7,256,257,258,259,260,261,262,263,512,513,514,515,516,51..., dimensions={0} | all-to-all | bytes 49152 | tf_op jit(solution)/shard_map/all_to_all | solution.py:257
  65.0 14.9 %all_to_all.11.parts = f32[32,1,128]{2,1,0:T(1,128)S(1)} all-to-all(f32[32,1,128]{2,1,0:T(1,128)S(1)} %spread.1), channel_id=1, replica_groups={{0,8,16,24,32,40,48,56,64,72,80,88,96,104,112,120,128,136,144,152,160,1..., dimensions={0} | all-to-all | bytes 32768 | tf_op jit(solution)/shard_map/all_to_all | solution.py:262
  79.9 0.6 own.1
  (1 shorter events, 0.0 us)
Async XLA Ops:
  0.6 1.0 %copy-start = (f32[3,8,32,128]{3,2,1,0:T(8,128)S(1)}, f32[3,8,32,128]{3,2,1,0:T(8,128)}, u32[]{:S(2)}) copy-start(f32[3,8,32,128]{3,2,1,0:T(8,128)} %before.5) | copy-start | bytes 1179652
  1.6 1.0 %copy-start.1 = (f32[3,8,32,128]{3,2,1,0:T(8,128)S(1)}, f32[3,8,32,128]{3,2,1,0:T(8,128)}, u32[]{:S(2)}) copy-start(f32[3,8,32,128]{3,2,1,0:T(8,128)} %middle.5) | copy-start | bytes 1179652
  2.6 0.9 %copy-start.2 = (f32[8,32,128]{2,1,0:T(8,128)S(1)}, f32[8,32,128]{2,1,0:T(8,128)}, u32[]{:S(2)}) copy-start(f32[8,32,128]{2,1,0:T(8,128)} %speed_sq.5) | copy-start | bytes 393220
  4.5 8.4 %collective-permute-start = (f32[20,32,128]{2,1,0:T(8,128)S(1)}, f32[20,32,128]{2,1,0:T(8,128)S(1)}, u32[]{:S(2)}, u32[]{:S(2)}) collective-permute-start(f32[20,32,128]{2,1,0:T(8,128)S(1)} %get-tuple-element.10), channel_id=1, source_target_pairs={{0,8},{16,24},{32,40},{48,56},{64,72},{80,88},{96,104},{112,120},{... | collective-permute-start | bytes 983048 | tf_op jit(solution)/shard_map/ppermute | solution.py:46
  8.5 4.5 %collective-permute-start.1 = (f32[20,32,128]{2,1,0:T(8,128)S(1)}, f32[20,32,128]{2,1,0:T(8,128)S(1)}, u32[]{:S(2)}, u32[]{:S(2)}) collective-permute-start(f32[20,32,128]{2,1,0:T(8,128)S(1)} %get-tuple-element.11), channel_id=1, source_target_pairs={{8,16},{24,32},{40,48},{56,64},{72,80},{88,96},{104,112},{120,128}... | collective-permute-start | bytes 983048 | tf_op jit(solution)/shard_map/ppermute | solution.py:46
  12.9 20.9 %copy-start.3 = (f32[6,16]{1,0:T(8,128)S(1)}, f32[6,16]{1,0:T(8,128)}, u32[]{:S(2)}) copy-start(f32[6,16]{1,0:T(8,128)} %mechanism.1) | copy-start | bytes 1156
  13.0 20.8 %copy-start.4 = (s32[16]{0:T(128)S(1)}, s32[16]{0:T(128)}, u32[]{:S(2)}) copy-start(s32[16]{0:T(128)} %cells.1) | copy-start | bytes 196
  13.0 20.8 %copy-start.5 = (s32[16]{0:T(128)S(1)}, s32[16]{0:T(128)}, u32[]{:S(2)}) copy-start(s32[16]{0:T(128)} %patches.1) | copy-start | bytes 196
  13.0 14.9 %collective-permute-start.2 = (f32[208,128]{1,0:T(8,128)S(1)}, f32[208,128]{1,0:T(8,128)S(1)}, u32[]{:S(2)}, u32[]{:S(2)}) collective-permute-start(f32[208,128]{1,0:T(8,128)S(1)} %get-tuple-element.12), channel_id=1, source_target_pairs={{0,1},{2,3},{4,5},{6,7},{1,0},{3,2},{5,4},{7,6},{8,9},{10,11},{12,... | collective-permute-start | bytes 319496 | tf_op jit(solution)/shard_map/ppermute | solution.py:46
  26.0 7.8 %collective-permute-start.3 = (f32[208,128]{1,0:T(8,128)S(1)}, f32[208,128]{1,0:T(8,128)S(1)}, u32[]{:S(2)}, u32[]{:S(2)}) collective-permute-start(f32[208,128]{1,0:T(8,128)S(1)} %get-tuple-element.13), channel_id=1, source_target_pairs={{1,2},{3,4},{5,6},{2,1},{4,3},{6,5},{9,10},{11,12},{13,14},{10,9},... | collective-permute-start | bytes 319496 | tf_op jit(solution)/shard_map/ppermute | solution.py:46

commit v3 on v2

--- a/solution.py
+++ b/solution.py
@@ -21,7 +21,8 @@
 LIMIT = 32 * 1024 * 1024
 
 E_PREV, E_SPEED, E_LEN = 12, 18, 20
-N_PREV, N_SPEED, N_LEN = 144, 192, 208
+N_PREV, N_SPEED, N_LEN = 96, 144, 160
+C_LEN = 24
 TOP = 16
 LAYERS = CE + 4
 
@@ -46,9 +47,11 @@
     return lax.ppermute(block, axis, pairs + [(j, i) for i, j in pairs])
 
 
-def east_kernel(before, middle, speed_sq, low_pair, high_pair, sems):
+def load_kernel(
+    before, middle, speed_sq, before_here, middle_here, speed_here, low_pair, high_pair, near, far, sems
+):
     odd = lax.axis_index("east") & 1
-    copies = []
+    copies = [(middle, middle_here), (before, before_here), (speed_sq, speed_here)]
     for message, high in ((low_pair, 1 - odd), (high_pair, odd)):
         four, two = high * (CE - 4), high * (CE - 2)
         for c in range(3):
@@ -58,40 +61,61 @@
     started = [pltpu.make_async_copy(a, b, sems.at[i]) for i, (a, b) in enumerate(copies)]
     for copy in started:
         copy.start()
-    for copy in started:
+    for copy in started[:3]:
+        copy.wait()
+    odd_north = (lax.axis_index("north") & 1) == 1
+
+    def put(at, count, low, high):
+        near[at : at + count, :] = jnp.where(odd_north, low, high)
+        far[at : at + count, :] = jnp.where(odd_north, high, low)
+
+    for e in range(CE):
+        for c in range(3):
+            slot = c * CE + e
+            put(slot * 4, 4, middle_here[c, e, 0:4, :], middle_here[c, e, CN - 4 : CN, :])
+            put(N_PREV + slot * 2, 2, before_here[c, e, 0:2, :], before_here[c, e, CN - 2 : CN, :])
+        put(N_SPEED + e * 2, 2, speed_here[e, 0:2, :], speed_here[e, CN - 2 : CN, :])
+    for copy in started[3:]:
         copy.wait()
 
 
 def east_layers(low_pair, high_pair):
     odd = (lax.axis_index("east") & 1) == 1
 
-    def west(k, rows=slice(None)):
-        return jnp.where(odd, low_pair[k, rows], high_pair[k, rows])
-
-    def east(k, rows=slice(None)):
-        return jnp.where(odd, high_pair[k, rows], low_pair[k, rows])
+    def west(k):
+        return jnp.where(odd, low_pair[k], high_pair[k])
+
+    def east(k):
+        return jnp.where(odd, high_pair[k], low_pair[k])
 
     return west, east
 
 
-def north_kernel(before, middle, speed_sq, low_pair, high_pair, near, far):
+def north_rows(near_pair, far_pair):
     odd = (lax.axis_index("north") & 1) == 1
-    west, east = east_layers(low_pair, high_pair)
-
-    def put(at, count, low, high):
-        near[at : at + count, :] = jnp.where(odd, low, high)
-        far[at : at + count, :] = jnp.where(odd, high, low)
-
-    bottom, top = slice(0, 4), slice(CN - 4, CN)
+
+    def south(at, count):
+        return jnp.where(odd, near_pair[pl.ds(at, count), :], far_pair[pl.ds(at, count), :])
+
+    def north(at, count):
+        return jnp.where(odd, far_pair[pl.ds(at, count), :], near_pair[pl.ds(at, count), :])
+
+    return south, north
+
+
+def corner_kernel(near_pair, far_pair, low_pair, high_pair):
+    odd = (lax.axis_index("east") & 1) == 1
+    south, north = north_rows(near_pair, far_pair)
     for c in range(3):
         for k in range(2):
-            put((c * LAYERS + k) * 4, 4, west(c * 4 + 2 + k, bottom), west(c * 4 + 2 + k, top))
-            put((c * LAYERS + CE + 2 + k) * 4, 4, east(c * 4 + k, bottom), east(c * 4 + k, top))
-        for e in range(CE):
-            put((c * LAYERS + 2 + e) * 4, 4, middle[c, e, 0:4, :], middle[c, e, CN - 4 : CN, :])
-            put(N_PREV + (c * CE + e) * 2, 2, before[c, e, 0:2, :], before[c, e, CN - 2 : CN, :])
-    for e in range(CE):
-        put(N_SPEED + e * 2, 2, speed_sq[e, 0:2, :], speed_sq[e, CN - 2 : CN, :])
+            at = (c * 2 + k) * 4
+            low, high = (c * CE + k) * 4, (c * CE + CE - 2 + k) * 4
+            for rows, lows, highs in (
+                (slice(at, at + 2), south(low + 2, 2), south(high + 2, 2)),
+                (slice(at + 2, at + 4), north(low, 2), north(high, 2)),
+            ):
+                low_pair[rows, :] = jnp.where(odd, lows, highs)
+                high_pair[rows, :] = jnp.where(odd, highs, lows)
 
 
 def laplace(here, near, far):
@@ -104,17 +128,12 @@
 
 
 def steps_kernel(
-    before, middle, speed_sq, low_pair, high_pair, near_pair, far_pair, mechanism, cells, patches,
-    field_next, field_last, parts, wide, later, edge_before, edge_speed,
+    before, middle, speed_sq, low_pair, high_pair, near_pair, far_pair, low_corner, high_corner,
+    mechanism, cells, patches, field_next, field_last, parts, wide, later, edge_before, edge_speed,
 ):
     west, east = east_layers(low_pair, high_pair)
-    odd_north = (lax.axis_index("north") & 1) == 1
-
-    def south(at, count):
-        return jnp.where(odd_north, near_pair[pl.ds(at, count), :], far_pair[pl.ds(at, count), :])
-
-    def north(at, count):
-        return jnp.where(odd_north, far_pair[pl.ds(at, count), :], near_pair[pl.ds(at, count), :])
+    south, north = north_rows(near_pair, far_pair)
+    odd = (lax.axis_index("east") & 1) == 1
 
     for e in range(CE):
         edge_speed[e, 6:8, :] = south(N_SPEED + e * 2, 2)
@@ -130,10 +149,17 @@
 
         for e in range(-2, CE + 2):
             k = e + 2
-            at = pl.multiple_of((c * LAYERS + k) * 4, 4)
             wide[c, k, TOP : TOP + CN, :] = layer(e)
-            wide[c, k, TOP - 4 : TOP, :] = south(at, 4)
-            wide[c, k, TOP + CN : TOP + CN + 4, :] = north(at, 4)
+            if 0 <= e < CE:
+                at = pl.multiple_of((c * CE + e) * 4, 4)
+                wide[c, k, TOP - 4 : TOP, :] = south(at, 4)
+                wide[c, k, TOP + CN : TOP + CN + 4, :] = north(at, 4)
+            else:
+                at = pl.multiple_of((c * 2 + e % CE % 6) * 4, 4)
+                low, high = low_corner[pl.ds(at, 4), :], high_corner[pl.ds(at, 4), :]
+                corner = jnp.where(odd, low, high) if e < 0 else jnp.where(odd, high, low)
+                wide[c, k, TOP - 2 : TOP, :] = corner[0:2]
+                wide[c, k, TOP + CN : TOP + CN + 2, :] = corner[2:4]
         for e in range(-2, CE + 2):
             k = e + 2
 
@@ -233,27 +259,31 @@
     params = pltpu.CompilerParams(vmem_limit_bytes=LIMIT)
     f32 = jnp.float32
     field = jax.ShapeDtypeStruct((3, CE, CN, CZ), f32)
-    message = jax.ShapeDtypeStruct((E_LEN, CN, CZ), f32)
-    low_pair, high_pair = pl.pallas_call(
-        east_kernel, out_shape=[message] * 2, in_specs=[HBM] * 3, out_specs=[VMEM] * 2,
-        scratch_shapes=[pltpu.SemaphoreType.DMA((14,))], compiler_params=params, name="east_strips",
-    )(field_prev, field_now, speed_sq)
+    held = (
+        pltpu.VMEM((3, CE, CN, CZ), f32), pltpu.VMEM((3, CE, CN, CZ), f32), pltpu.VMEM((CE, CN, CZ), f32)
+    )
+    east_message, north_message = pltpu.VMEM((E_LEN, CN, CZ), f32), pltpu.VMEM((N_LEN, CZ), f32)
+    inputs = [pltpu.with_memory_space_constraint(x, pltpu.HBM) for x in (field_prev, field_now, speed_sq)]
+    field_prev, field_now, speed_sq, low_pair, high_pair, near, far = pl.pallas_call(
+        load_kernel, out_shape=[*held] + [east_message] * 2 + [north_message] * 2,
+        in_specs=[HBM] * 3, out_specs=[VMEM] * 7,
+        scratch_shapes=[pltpu.SemaphoreType.DMA((17,))], compiler_params=params, name="load",
+    )(*inputs)
+    near_pair, far_pair = swap(near, "north", 0), swap(far, "north", 1)
     pairs = swap(low_pair, "east", 0), swap(high_pair, "east", 1)
-    message = jax.ShapeDtypeStruct((N_LEN, CZ), f32)
-    near, far = pl.pallas_call(
-        north_kernel, out_shape=[message] * 2, in_specs=[VMEM] * 5, out_specs=[VMEM] * 2,
-        compiler_params=params, name="north_strips",
-    )(field_prev, field_now, speed_sq, *pairs)
-    far_pair = swap(far, "north", 1)
-    near_pair = swap(near, "north", 0)
+    low_corner, high_corner = pl.pallas_call(
+        corner_kernel, out_shape=[pltpu.VMEM((C_LEN, CZ), f32)] * 2, in_specs=[VMEM] * 2,
+        out_specs=[VMEM] * 2, compiler_params=params, name="corners",
+    )(near_pair, far_pair)
+    corners = swap(low_corner, "east", 0), swap(high_corner, "east", 1)
     wide = pltpu.VMEM((3, LAYERS, CN + 2 * TOP, CZ), f32)
     parts = jax.ShapeDtypeStruct((COLUMN, ROWS, CZ), f32)
     field_next, field_last, parts = pl.pallas_call(
-        steps_kernel, out_shape=[field, field, parts], in_specs=[VMEM] * 7 + [SMEM] * 3,
+        steps_kernel, out_shape=[field, field, parts], in_specs=[VMEM] * 9 + [SMEM] * 3,
         out_specs=[VMEM] * 3,
         scratch_shapes=[wide, wide, pltpu.VMEM((LAYERS, 16, CZ), f32), pltpu.VMEM((CE, 16, CZ), f32)],
         compiler_params=params, name="steps",
-    )(field_prev, field_now, speed_sq, *pairs, near_pair, far_pair, mechanism, sub_cells, sub_patch)
+    )(field_prev, field_now, speed_sq, *pairs, near_pair, far_pair, *corners, mechanism, sub_cells, sub_patch)
     parts = lax.all_to_all(parts, BOTH, 0, 0, tiled=True, axis_index_groups=column_groups())
     parts = pl.pallas_call(
         spread_kernel, out_shape=jax.ShapeDtypeStruct((PLANE, 1, CZ), f32),

time: 80.8 us -> 79.1 us (0.979)
  starting transfers between devices: 19.5 us -> 23.4 us
  waiting for transfers between devices: 9.65 us -> 6.03 us
  local copies, waits for them, and re-layouts: 2.9 us -> 0.65 us
    ppermute x4 -> x6, starting transfers between devices: 19.5 us -> 23.4 us  [swap(): return lax.ppermute(block, axis, pairs + [(j, i) for i, j in pairs])]
    ppermute x4 -> x6, waiting for transfers between devices: 9.65 us -> 6.03 us  [swap(): return lax.ppermute(block, axis, pairs + [(j, i) for i, j in pairs])]
    all_to_all x1, blocking collectives: 14.9 us -> 11.7 us  [body(): lax.all_to_all(parts, BOTH, 0, 0, tiled=True, axis_index_groups=plane_gro...]
    all_to_all x1, blocking collectives: 27.8 us -> 30.6 us  [body(): lax.all_to_all(parts, BOTH, 0, 0, tiled=True, axis_index_groups=column_gr...]
    unnamed x12 -> x6, local copies, waits for them, and re-layouts: 2.9 us -> 0.65 us
  transfers between devices with their start and end apart: 4 -> 6, of which waited for: 2 -> 2; matrix products, arithmetic and copies ran while one was open for 0% -> 0% of each run, Pallas kernels for 0% -> 0%
where the time goes in v3:
time: 79.1 us; the launch traced here: 78.7 us
  blocking collectives  42.4 us (54%)
  starting transfers between devices  23.4 us (30%)
  waiting for transfers between devices  6.03 us (8%)
  Pallas kernels  5.54 us (7%)
    all_to_all x1, blocking collectives, body(): lax.all_to_all(parts, BOTH, 0, 0, tiled=True, axis_index_groups=column_gr...  30.6 us
    ppermute x6, starting transfers between devices, swap(): return lax.ppermute(block, axis, pairs + [(j, i) for i, j in pairs])  23.4 us
    all_to_all x1, blocking collectives, body(): lax.all_to_all(parts, BOTH, 0, 0, tiled=True, axis_index_groups=plane_gro...  11.7 us
    ppermute x6, waiting for transfers between devices, swap(): return lax.ppermute(block, axis, pairs + [(j, i) for i, j in pairs])  6.03 us
    pallas_call x1, Pallas kernels, body(): pl.pallas_call(steps_kernel, out_shape=[field, field, parts], in_specs=[V...  3.4 us
  transfers between devices with their start and end apart: 6, of which 2 were waited for; matrix products, arithmetic and copies ran while one was open for 0% of the time, Pallas kernels for 0%

profile of v3, /device:TPU:1, one launch (start us, length us, event | category | flops | bytes accessed | tf_op | source)
XLA Modules:
  0.0 78.7 jit_solution(4546359180868006530)
XLA Ops:
  0.6 1.5 %load.1 = (f32[3,8,32,128]{3,2,1,0:T(8,128)S(1)}, f32[3,8,32,128]{3,2,1,0:T(8,128)S(1)}, f32[8,32,128]{2,1,0:T(8,128)S(1)}, f32[20,32,128]{2,1,0:T(8,128)S(1)}, ...) custom-call(f32[3,8,32,128]{3,2,1,0:T(8,128)} %before.1, f32[3,8,32,128]{3,2,1,0:T(8,128)} %middle.1, ...), custom_call_target="tpu_custom_call" | custom-call | tf_op jit(solution)/shard_map/load/pallas_call | solution.py:267
  2.1 3.9 %collective-permute-start = (f32[20,32,128]{2,1,0:T(8,128)S(1)}, f32[20,32,128]{2,1,0:T(8,128)S(1)}, u32[]{:S(2)}, u32[]{:S(2)}) collective-permute-start(f32[20,32,128]{2,1,0:T(8,128)S(1)} %get-tuple-element.18), channel_id=1, source_target_pairs={{0,8},{16,24},{32,40},{48,56},{64,72},{80,88},{96,104},{112,120},{... | collective-permute-start | bytes 983048 | tf_op jit(solution)/shard_map/ppermute | solution.py:47
  6.1 0.7 collective-permute-start.1
  6.8 10.4 %collective-permute-start.2 = (f32[160,128]{1,0:T(8,128)S(1)}, f32[160,128]{1,0:T(8,128)S(1)}, u32[]{:S(2)}, u32[]{:S(2)}) collective-permute-start(f32[160,128]{1,0:T(8,128)S(1)} %get-tuple-element.20), channel_id=1, source_target_pairs={{0,1},{2,3},{4,5},{6,7},{1,0},{3,2},{5,4},{7,6},{8,9},{10,11},{12,... | collective-permute-start | bytes 245768 | tf_op jit(solution)/shard_map/ppermute | solution.py:47
  17.2 1.9 %collective-permute-start.3 = (f32[160,128]{1,0:T(8,128)S(1)}, f32[160,128]{1,0:T(8,128)S(1)}, u32[]{:S(2)}, u32[]{:S(2)}) collective-permute-start(f32[160,128]{1,0:T(8,128)S(1)} %get-tuple-element.21), channel_id=1, source_target_pairs={{1,2},{3,4},{5,6},{2,1},{4,3},{6,5},{9,10},{11,12},{13,14},{10,9},... | collective-permute-start | bytes 245768 | tf_op jit(solution)/shard_map/ppermute | solution.py:47
  19.1 0.0 collective-permute-done.2.near_pair
  19.1 5.6 %collective-permute-done.3.far_pair = f32[160,128]{1,0:T(8,128)S(1)} collective-permute-done((f32[160,128]{1,0:T(8,128)S(1)}, f32[160,128]{1,0:T(8,128)S(1)}, u32[]{:S(2)}, u32[]{:S(2)}) %collective-permute-start.3) | collective-permute-done | bytes 81952 | tf_op jit(solution)/shard_map/ppermute | solution.py:47
  24.7 0.0 copy-start
  24.8 5.8 %collective-permute-start.4 = (f32[24,128]{1,0:T(8,128)S(1)}, f32[24,128]{1,0:T(8,128)S(1)}, u32[]{:S(2)}, u32[]{:S(2)}) collective-permute-start(f32[24,128]{1,0:T(8,128)S(1)} %get-tuple-element.22), channel_id=1, source_target_pairs={{0,8},{16,24},{32,40},{48,56},{64,72},{80,88},{96,104},{112,120},{... | collective-permute-start | bytes 36872 | tf_op jit(solution)/shard_map/ppermute | solution.py:47
  30.5 0.7 collective-permute-start.5
  31.2 0.4 collective-permute-done.4.low_corner
  31.6 0.0 collective-permute-done.5.high_corner
  31.6 0.0 collective-permute-done.low_pair
  31.6 0.0 collective-permute-done.1.high_pair
  31.6 0.0 copy-start.1
  31.6 0.0 copy-start.2
  31.6 0.0 copy-done
  31.6 0.6 copy-done.1
  32.3 0.0 copy-done.2
  32.3 3.4 %steps.1 = (f32[3,8,32,128]{3,2,1,0:T(8,128)}, f32[3,8,32,128]{3,2,1,0:T(8,128)}, f32[24,2,128]{2,1,0:T(2,128)S(1)}) custom-call(f32[3,8,32,128]{3,2,1,0:T(8,128)S(1)} %get-tuple-element.15.before, f32[3,8,32,128]{3,2,1,0:T(8,128)S(1)} %get-tuple-element.16.middle, f32[8,32,128]{2,1,0:T(8,128)S(1)} %get-tuple-element.17.speed_sq, ...), custom_call_target="tpu_custom_call" | custom-call | tf_op jit(solution)/shard_map/steps/pallas_call | solution.py:281
  35.7 30.6 %all_to_all.10.parts = f32[24,2,128]{2,1,0:T(2,128)S(1)} all-to-all(f32[24,2,128]{2,1,0:T(2,128)S(1)} %get-tuple-element.26), channel_id=1, replica_groups={{0,1,2,3,4,5,6,7,256,257,258,259,260,261,262,263,512,513,514,515,516,51..., dimensions={0} | all-to-all | bytes 49152 | tf_op jit(solution)/shard_map/all_to_all | solution.py:287
  66.4 11.7 %all_to_all.11.parts = f32[32,1,128]{2,1,0:T(1,128)S(1)} all-to-all(f32[32,1,128]{2,1,0:T(1,128)S(1)} %spread.1), channel_id=1, replica_groups={{0,8,16,24,32,40,48,56,64,72,80,88,96,104,112,120,128,136,144,152,160,1..., dimensions={0} | all-to-all | bytes 32768 | tf_op jit(solution)/shard_map/all_to_all | solution.py:292
  78.1 0.6 own.1
  (2 shorter events, 0.1 us)
Async XLA Ops:
  2.1 29.5 %collective-permute-start = (f32[20,32,128]{2,1,0:T(8,128)S(1)}, f32[20,32,128]{2,1,0:T(8,128)S(1)}, u32[]{:S(2)}, u32[]{:S(2)}) collective-permute-start(f32[20,32,128]{2,1,0:T(8,128)S(1)} %get-tuple-element.18), channel_id=1, source_target_pairs={{0,8},{16,24},{32,40},{48,56},{64,72},{80,88},{96,104},{112,120},{... | collective-permute-start | bytes 983048 | tf_op jit(solution)/shard_map/ppermute | solution.py:47
  6.1 25.5 %collective-permute-start.1 = (f32[20,32,128]{2,1,0:T(8,128)S(1)}, f32[20,32,128]{2,1,0:T(8,128)S(1)}, u32[]{:S(2)}, u32[]{:S(2)}) collective-permute-start(f32[20,32,128]{2,1,0:T(8,128)S(1)} %get-tuple-element.19), channel_id=1, source_target_pairs={{8,16},{24,32},{40,48},{56,64},{72,80},{88,96},{104,112},{120,128}... | collective-permute-start | bytes 983048 | tf_op jit(solution)/shard_map/ppermute | solution.py:47
  6.8 12.3 %collective-permute-start.2 = (f32[160,128]{1,0:T(8,128)S(1)}, f32[160,128]{1,0:T(8,128)S(1)}, u32[]{:S(2)}, u32[]{:S(2)}) collective-permute-start(f32[160,128]{1,0:T(8,128)S(1)} %get-tuple-element.20), channel_id=1, source_target_pairs={{0,1},{2,3},{4,5},{6,7},{1,0},{3,2},{5,4},{7,6},{8,9},{10,11},{12,... | collective-permute-start | bytes 245768 | tf_op jit(solution)/shard_map/ppermute | solution.py:47
  17.2 7.6 %collective-permute-start.3 = (f32[160,128]{1,0:T(8,128)S(1)}, f32[160,128]{1,0:T(8,128)S(1)}, u32[]{:S(2)}, u32[]{:S(2)}) collective-permute-start(f32[160,128]{1,0:T(8,128)S(1)} %get-tuple-element.21), channel_id=1, source_target_pairs={{1,2},{3,4},{5,6},{2,1},{4,3},{6,5},{9,10},{11,12},{13,14},{10,9},... | collective-permute-start | bytes 245768 | tf_op jit(solution)/shard_map/ppermute | solution.py:47
  24.7 6.9 %copy-start = (f32[6,16]{1,0:T(8,128)S(1)}, f32[6,16]{1,0:T(8,128)}, u32[]{:S(2)}) copy-start(f32[6,16]{1,0:T(8,128)} %mechanism.1) | copy-start | bytes 1156
  24.8 6.8 %collective-permute-start.4 = (f32[24,128]{1,0:T(8,128)S(1)}, f32[24,128]{1,0:T(8,128)S(1)}, u32[]{:S(2)}, u32[]{:S(2)}) collective-permute-start(f32[24,128]{1,0:T(8,128)S(1)} %get-tuple-element.22), channel_id=1, source_target_pairs={{0,8},{16,24},{32,40},{48,56},{64,72},{80,88},{96,104},{112,120},{... | collective-permute-start | bytes 36872 | tf_op jit(solution)/shard_map/ppermute | solution.py:47
  30.5 1.1 %collective-permute-start.5 = (f32[24,128]{1,0:T(8,128)S(1)}, f32[24,128]{1,0:T(8,128)S(1)}, u32[]{:S(2)}, u32[]{:S(2)}) collective-permute-start(f32[24,128]{1,0:T(8,128)S(1)} %get-tuple-element.23), channel_id=1, source_target_pairs={{8,16},{24,32},{40,48},{56,64},{72,80},{88,96},{104,112},{120,128}... | collective-permute-start | bytes 36872 | tf_op jit(solution)/shard_map/ppermute | solution.py:47
  31.6 0.7 copy-start.1
  31.6 0.7 copy-start.2

commit v4 on v3

--- a/solution.py
+++ b/solution.py
@@ -48,7 +48,7 @@
 
 
 def load_kernel(
-    before, middle, speed_sq, before_here, middle_here, speed_here, low_pair, high_pair, near, far, sems
+    before, middle, speed_sq, before_here, middle_here, speed_here, far, near, low_pair, high_pair, sems
 ):
     odd = lax.axis_index("east") & 1
     copies = [(middle, middle_here), (before, before_here), (speed_sq, speed_here)]
@@ -103,7 +103,7 @@
     return south, north
 
 
-def corner_kernel(near_pair, far_pair, low_pair, high_pair):
+def corner_kernel(far_pair, near_pair, low_pair, high_pair):
     odd = (lax.axis_index("east") & 1) == 1
     south, north = north_rows(near_pair, far_pair)
     for c in range(3):
@@ -128,9 +128,26 @@
 
 
 def steps_kernel(
-    before, middle, speed_sq, low_pair, high_pair, near_pair, far_pair, low_corner, high_corner,
-    mechanism, cells, patches, field_next, field_last, parts, wide, later, edge_before, edge_speed,
+    before, middle, speed_sq, far_pair, near_pair, low_pair, high_pair, low_corner, high_corner,
+    mechanism_far, cells_far, patches_far, next_out, last_out, parts,
+    wide, later, field_last, edge_before, edge_speed, mechanism, cells, patches, sub_sems, out_sems,
 ):
+    subs = [
+        pltpu.make_async_copy(a, b, sub_sems.at[i])
+        for i, (a, b) in enumerate(
+            ((mechanism_far, mechanism), (cells_far, cells), (patches_far, patches))
+        )
+    ]
+    for copy in subs:
+        copy.start()
+
+    def next_copy(c):
+        own = later.at[c, pl.ds(2, CE), pl.ds(TOP, CN)]
+        return pltpu.make_async_copy(own, next_out.at[c], out_sems.at[c])
+
+    def last_copy(c):
+        return pltpu.make_async_copy(field_last.at[c], last_out.at[c], out_sems.at[3 + c])
+
     west, east = east_layers(low_pair, high_pair)
     south, north = north_rows(near_pair, far_pair)
     odd = (lax.axis_index("east") & 1) == 1
@@ -180,8 +197,7 @@
                 old, speed = east(E_PREV + c * 2 + e - CE), east(E_SPEED + e - CE)
             new = 2.0 * here - old + speed * total
             later[c, k, TOP : TOP + CN, :] = new
-            if 0 <= e < CE:
-                field_next[c, e] = new
+        next_copy(c).start()
         for e in range(CE):
             k = e + 2
             at = pl.multiple_of(N_PREV + (c * CE + e) * 2, 2)
@@ -219,18 +235,21 @@
                 rows(-2) + rows(2) + rows(0, -2) + rows(0, 2),
             )
             field_last[c, e] = 2.0 * here - middle[c, e] + speed_sq[e] * total
+        last_copy(c).start()
         return carry
 
     lax.fori_loop(0, 3, second, 0)
 
     lane = lax.broadcasted_iota(jnp.int32, (1, CZ), 1)
     parts[...] = jnp.zeros_like(parts)
+    for copy in subs:
+        copy.wait()
     for i in range(SUBS):
         cell, patch = cells[i], patches[i]
         layer, row, depth = cell >> 12, (cell >> 7) & (CN - 1), cell & (CZ - 1)
         total = jnp.zeros((1, CZ), jnp.float32)
         for c in range(3):
-            total += mechanism[c, i] * field_next[c, layer, pl.ds(row, 1), :]
+            total += mechanism[c, i] * later[c, layer + 2, pl.ds(TOP + row, 1), :]
             total += mechanism[3 + c, i] * field_last[c, layer, pl.ds(row, 1), :]
         total = jnp.where(lane == depth, total, 0.0)
         run, at = patch >> 11, (patch >> 6) & (PLANE - 1)
@@ -238,6 +257,9 @@
         turned = pltpu.roll(total, (place - depth) & (CZ - 1), 1)
         to = run * N_NORTH + ((patch >> 3) & (N_NORTH - 1))
         parts[to, pl.ds(at >> 4, 1), :] += turned
+    for c in range(3):
+        next_copy(c).wait()
+        last_copy(c).wait()
 
 
 def spread_kernel(parts, out):
@@ -258,32 +280,39 @@
 def body(field_prev, field_now, speed_sq, mechanism, sub_cells, sub_patch):
     params = pltpu.CompilerParams(vmem_limit_bytes=LIMIT)
     f32 = jnp.float32
-    field = jax.ShapeDtypeStruct((3, CE, CN, CZ), f32)
     held = (
         pltpu.VMEM((3, CE, CN, CZ), f32), pltpu.VMEM((3, CE, CN, CZ), f32), pltpu.VMEM((CE, CN, CZ), f32)
     )
     east_message, north_message = pltpu.VMEM((E_LEN, CN, CZ), f32), pltpu.VMEM((N_LEN, CZ), f32)
     inputs = [pltpu.with_memory_space_constraint(x, pltpu.HBM) for x in (field_prev, field_now, speed_sq)]
-    field_prev, field_now, speed_sq, low_pair, high_pair, near, far = pl.pallas_call(
-        load_kernel, out_shape=[*held] + [east_message] * 2 + [north_message] * 2,
+    field_prev, field_now, speed_sq, far, near, low_pair, high_pair = pl.pallas_call(
+        load_kernel, out_shape=[*held] + [north_message] * 2 + [east_message] * 2,
         in_specs=[HBM] * 3, out_specs=[VMEM] * 7,
         scratch_shapes=[pltpu.SemaphoreType.DMA((17,))], compiler_params=params, name="load",
     )(*inputs)
-    near_pair, far_pair = swap(near, "north", 0), swap(far, "north", 1)
+    far_pair = swap(far, "north", 1)
+    near_pair = swap(near, "north", 0)
     pairs = swap(low_pair, "east", 0), swap(high_pair, "east", 1)
     low_corner, high_corner = pl.pallas_call(
         corner_kernel, out_shape=[pltpu.VMEM((C_LEN, CZ), f32)] * 2, in_specs=[VMEM] * 2,
         out_specs=[VMEM] * 2, compiler_params=params, name="corners",
-    )(near_pair, far_pair)
+    )(far_pair, near_pair)
     corners = swap(low_corner, "east", 0), swap(high_corner, "east", 1)
     wide = pltpu.VMEM((3, LAYERS, CN + 2 * TOP, CZ), f32)
-    parts = jax.ShapeDtypeStruct((COLUMN, ROWS, CZ), f32)
+    parts = pltpu.VMEM((COLUMN, ROWS, CZ), f32)
+    field = pltpu.HBM((3, CE, CN, CZ), f32)
+    subs = [pltpu.with_memory_space_constraint(x, pltpu.HBM) for x in (mechanism, sub_cells, sub_patch)]
     field_next, field_last, parts = pl.pallas_call(
-        steps_kernel, out_shape=[field, field, parts], in_specs=[VMEM] * 9 + [SMEM] * 3,
-        out_specs=[VMEM] * 3,
-        scratch_shapes=[wide, wide, pltpu.VMEM((LAYERS, 16, CZ), f32), pltpu.VMEM((CE, 16, CZ), f32)],
+        steps_kernel, out_shape=[field, field, parts], in_specs=[VMEM] * 9 + [HBM] * 3,
+        out_specs=[HBM, HBM, VMEM],
+        scratch_shapes=[
+            wide, wide, pltpu.VMEM((3, CE, CN, CZ), f32),
+            pltpu.VMEM((LAYERS, 16, CZ), f32), pltpu.VMEM((CE, 16, CZ), f32),
+            pltpu.SMEM((6, SUBS), f32), pltpu.SMEM((SUBS,), jnp.int32), pltpu.SMEM((SUBS,), jnp.int32),
+            pltpu.SemaphoreType.DMA((3,)), pltpu.SemaphoreType.DMA((6,)),
+        ],
         compiler_params=params, name="steps",
-    )(field_prev, field_now, speed_sq, *pairs, near_pair, far_pair, *corners, mechanism, sub_cells, sub_patch)
+    )(field_prev, field_now, speed_sq, far_pair, near_pair, *pairs, *corners, *subs)
     parts = lax.all_to_all(parts, BOTH, 0, 0, tiled=True, axis_index_groups=column_groups())
     parts = pl.pallas_call(
         spread_kernel, out_shape=jax.ShapeDtypeStruct((PLANE, 1, CZ), f32),

time: 79.1 us -> 75.5 us (0.954)
  waiting for transfers between devices: 6.03 us -> 1.3 us
  blocking collectives: 42.4 us -> 47 us
  starting transfers between devices: 23.4 us -> 21.6 us
  Pallas kernels: 5.54 us -> 4.63 us
    all_to_all x1, blocking collectives: 30.6 us -> 35.4 us  [body(): lax.all_to_all(parts, BOTH, 0, 0, tiled=True, axis_index_groups=column_gr...]
    ppermute x6, waiting for transfers between devices: 6.03 us -> 1.3 us  [swap(): return lax.ppermute(block, axis, pairs + [(j, i) for i, j in pairs])]
    ppermute x6, starting transfers between devices: 23.4 us -> 21.6 us  [swap(): return lax.ppermute(block, axis, pairs + [(j, i) for i, j in pairs])]
    pallas_call x1, Pallas kernels: 3.4 us -> 2.49 us  [body(): pl.pallas_call(steps_kernel, out_shape=[field, field, parts], in_specs=[V...]
where the time goes in v4:
time: 75.5 us; the launch traced here: 75.2 us
  blocking collectives  47 us (62%)
  starting transfers between devices  21.6 us (29%)
  Pallas kernels  4.63 us (6%)
  waiting for transfers between devices  1.3 us (2%)
    all_to_all x1, blocking collectives, body(): lax.all_to_all(parts, BOTH, 0, 0, tiled=True, axis_index_groups=column_gr...  35.4 us
    ppermute x6, starting transfers between devices, swap(): return lax.ppermute(block, axis, pairs + [(j, i) for i, j in pairs])  21.6 us
    all_to_all x1, blocking collectives, body(): lax.all_to_all(parts, BOTH, 0, 0, tiled=True, axis_index_groups=plane_gro...  11.6 us
    pallas_call x1, Pallas kernels, body(): pl.pallas_call(steps_kernel, out_shape=[field, field, parts], in_specs=[V...  2.49 us
  transfers between devices with their start and end apart: 6, of which 2 were waited for; matrix products, arithmetic and copies ran while one was open for 0% of the time, Pallas kernels for 0%

profile of v4, /device:TPU:1, one launch (start us, length us, event | category | flops | bytes accessed | tf_op | source)
XLA Modules:
  0.0 75.2 jit_solution(4236141372184003328)
XLA Ops:
  0.6 1.5 %load.1 = (f32[3,8,32,128]{3,2,1,0:T(8,128)S(1)}, f32[3,8,32,128]{3,2,1,0:T(8,128)S(1)}, f32[8,32,128]{2,1,0:T(8,128)S(1)}, f32[160,128]{1,0:T(8,128)S(1)}, f32[...) custom-call(f32[3,8,32,128]{3,2,1,0:T(8,128)} %before.1, f32[3,8,32,128]{3,2,1,0:T(8,128)} %middle.1, ...), custom_call_target="tpu_custom_call" | custom-call | tf_op jit(solution)/shard_map/load/pallas_call | solution.py:288
  2.1 3.9 %collective-permute-start.2 = (f32[20,32,128]{2,1,0:T(8,128)S(1)}, f32[20,32,128]{2,1,0:T(8,128)S(1)}, u32[]{:S(2)}, u32[]{:S(2)}) collective-permute-start(f32[20,32,128]{2,1,0:T(8,128)S(1)} %get-tuple-element.20), channel_id=1, source_target_pairs={{0,8},{16,24},{32,40},{48,56},{64,72},{80,88},{96,104},{112,120},{... | collective-permute-start | bytes 983048 | tf_op jit(solution)/shard_map/ppermute | solution.py:47
  6.1 0.7 collective-permute-start.3
  6.8 8.5 %collective-permute-start = (f32[160,128]{1,0:T(8,128)S(1)}, f32[160,128]{1,0:T(8,128)S(1)}, u32[]{:S(2)}, u32[]{:S(2)}) collective-permute-start(f32[160,128]{1,0:T(8,128)S(1)} %get-tuple-element.18), channel_id=1, source_target_pairs={{1,2},{3,4},{5,6},{2,1},{4,3},{6,5},{9,10},{11,12},{13,14},{10,9},... | collective-permute-start | bytes 245768 | tf_op jit(solution)/shard_map/ppermute | solution.py:47
  15.2 2.6 %collective-permute-start.1 = (f32[160,128]{1,0:T(8,128)S(1)}, f32[160,128]{1,0:T(8,128)S(1)}, u32[]{:S(2)}, u32[]{:S(2)}) collective-permute-start(f32[160,128]{1,0:T(8,128)S(1)} %get-tuple-element.19), channel_id=1, source_target_pairs={{0,1},{2,3},{4,5},{6,7},{1,0},{3,2},{5,4},{7,6},{8,9},{10,11},{12,... | collective-permute-start | bytes 245768 | tf_op jit(solution)/shard_map/ppermute | solution.py:47
  17.8 0.0 collective-permute-done.far_pair
  17.8 0.9 %collective-permute-done.1.near_pair = f32[160,128]{1,0:T(8,128)S(1)} collective-permute-done((f32[160,128]{1,0:T(8,128)S(1)}, f32[160,128]{1,0:T(8,128)S(1)}, u32[]{:S(2)}, u32[]{:S(2)}) %collective-permute-start.1) | collective-permute-done | bytes 81952 | tf_op jit(solution)/shard_map/ppermute | solution.py:47
  18.8 5.2 %collective-permute-start.4 = (f32[24,128]{1,0:T(8,128)S(1)}, f32[24,128]{1,0:T(8,128)S(1)}, u32[]{:S(2)}, u32[]{:S(2)}) collective-permute-start(f32[24,128]{1,0:T(8,128)S(1)} %get-tuple-element.22), channel_id=1, source_target_pairs={{0,8},{16,24},{32,40},{48,56},{64,72},{80,88},{96,104},{112,120},{... | collective-permute-start | bytes 36872 | tf_op jit(solution)/shard_map/ppermute | solution.py:47
  24.0 0.7 collective-permute-start.5
  24.6 0.4 collective-permute-done.4.low_corner
  25.0 0.0 collective-permute-done.5.high_corner
  25.0 0.0 collective-permute-done.2.low_pair
  25.1 0.0 collective-permute-done.3.high_pair
  25.1 2.5 %steps.1 = (f32[3,8,32,128]{3,2,1,0:T(8,128)}, f32[3,8,32,128]{3,2,1,0:T(8,128)}, f32[24,2,128]{2,1,0:T(2,128)S(1)}) custom-call(f32[3,8,32,128]{3,2,1,0:T(8,128)S(1)} %get-tuple-element.15.before, f32[3,8,32,128]{3,2,1,0:T(8,128)S(1)} %get-tuple-element.16.middle, f32[8,32,128]{2,1,0:T(8,128)S(1)} %get-tuple-element.17.speed_sq, ...), custom_call_target="tpu_custom_call" | custom-call | tf_op jit(solution)/shard_map/steps/pallas_call | solution.py:305
  27.6 35.4 %all_to_all.10.parts = f32[24,2,128]{2,1,0:T(2,128)S(1)} all-to-all(f32[24,2,128]{2,1,0:T(2,128)S(1)} %get-tuple-element.26), channel_id=1, replica_groups={{0,1,2,3,4,5,6,7,256,257,258,259,260,261,262,263,512,513,514,515,516,51..., dimensions={0} | all-to-all | bytes 49152 | tf_op jit(solution)/shard_map/all_to_all | solution.py:316
  63.0 11.6 %all_to_all.11.parts = f32[32,1,128]{2,1,0:T(1,128)S(1)} all-to-all(f32[32,1,128]{2,1,0:T(1,128)S(1)} %spread.1), channel_id=1, replica_groups={{0,8,16,24,32,40,48,56,64,72,80,88,96,104,112,120,128,136,144,152,160,1..., dimensions={0} | all-to-all | bytes 32768 | tf_op jit(solution)/shard_map/all_to_all | solution.py:321
  74.6 0.6 own.1
  (2 shorter events, 0.1 us)
Async XLA Ops:
  2.1 22.9 %collective-permute-start.2 = (f32[20,32,128]{2,1,0:T(8,128)S(1)}, f32[20,32,128]{2,1,0:T(8,128)S(1)}, u32[]{:S(2)}, u32[]{:S(2)}) collective-permute-start(f32[20,32,128]{2,1,0:T(8,128)S(1)} %get-tuple-element.20), channel_id=1, source_target_pairs={{0,8},{16,24},{32,40},{48,56},{64,72},{80,88},{96,104},{112,120},{... | collective-permute-start | bytes 983048 | tf_op jit(solution)/shard_map/ppermute | solution.py:47
  6.1 19.0 %collective-permute-start.3 = (f32[20,32,128]{2,1,0:T(8,128)S(1)}, f32[20,32,128]{2,1,0:T(8,128)S(1)}, u32[]{:S(2)}, u32[]{:S(2)}) collective-permute-start(f32[20,32,128]{2,1,0:T(8,128)S(1)} %get-tuple-element.21), channel_id=1, source_target_pairs={{8,16},{24,32},{40,48},{56,64},{72,80},{88,96},{104,112},{120,128}... | collective-permute-start | bytes 983048 | tf_op jit(solution)/shard_map/ppermute | solution.py:47
  6.8 11.1 %collective-permute-start = (f32[160,128]{1,0:T(8,128)S(1)}, f32[160,128]{1,0:T(8,128)S(1)}, u32[]{:S(2)}, u32[]{:S(2)}) collective-permute-start(f32[160,128]{1,0:T(8,128)S(1)} %get-tuple-element.18), channel_id=1, source_target_pairs={{1,2},{3,4},{5,6},{2,1},{4,3},{6,5},{9,10},{11,12},{13,14},{10,9},... | collective-permute-start | bytes 245768 | tf_op jit(solution)/shard_map/ppermute | solution.py:47
  15.2 3.5 %collective-permute-start.1 = (f32[160,128]{1,0:T(8,128)S(1)}, f32[160,128]{1,0:T(8,128)S(1)}, u32[]{:S(2)}, u32[]{:S(2)}) collective-permute-start(f32[160,128]{1,0:T(8,128)S(1)} %get-tuple-element.19), channel_id=1, source_target_pairs={{0,1},{2,3},{4,5},{6,7},{1,0},{3,2},{5,4},{7,6},{8,9},{10,11},{12,... | collective-permute-start | bytes 245768 | tf_op jit(solution)/shard_map/ppermute | solution.py:47
  18.8 6.3 %collective-permute-start.4 = (f32[24,128]{1,0:T(8,128)S(1)}, f32[24,128]{1,0:T(8,128)S(1)}, u32[]{:S(2)}, u32[]{:S(2)}) collective-permute-start(f32[24,128]{1,0:T(8,128)S(1)} %get-tuple-element.22), channel_id=1, source_target_pairs={{0,8},{16,24},{32,40},{48,56},{64,72},{80,88},{96,104},{112,120},{... | collective-permute-start | bytes 36872 | tf_op jit(solution)/shard_map/ppermute | solution.py:47
  24.0 1.1 %collective-permute-start.5 = (f32[24,128]{1,0:T(8,128)S(1)}, f32[24,128]{1,0:T(8,128)S(1)}, u32[]{:S(2)}, u32[]{:S(2)}) collective-permute-start(f32[24,128]{1,0:T(8,128)S(1)} %get-tuple-element.23), channel_id=1, source_target_pairs={{8,16},{24,32},{40,48},{56,64},{72,80},{88,96},{104,112},{120,128}... | collective-permute-start | bytes 36872 | tf_op jit(solution)/shard_map/ppermute | solution.py:47

commit v5 on v4

--- a/solution.py
+++ b/solution.py
@@ -20,11 +20,13 @@
 HBM = pl.BlockSpec(memory_space=pltpu.HBM)
 LIMIT = 32 * 1024 * 1024
 
-E_PREV, E_SPEED, E_LEN = 12, 18, 20
-N_PREV, N_SPEED, N_LEN = 96, 144, 160
+E_PREV, E_SPEED, E_SUBS, E_LEN = 12, 18, 20, 21
+N_PREV, N_SPEED, N_SUBS, N_LEN = 96, 144, 160, 168
+S_LEN = 8
 C_LEN = 24
 TOP = 16
 LAYERS = CE + 4
+NEAR, FAR = 16.0 / 12.0, -1.0 / 12.0
 
 
 def column_groups():
@@ -48,10 +50,16 @@
 
 
 def load_kernel(
-    before, middle, speed_sq, before_here, middle_here, speed_here, far, near, low_pair, high_pair, sems
+    before, middle, speed_sq, mechanism_far, cells_far, cells_row_far, patches_row_far,
+    before_here, middle_here, speed_here, far, near, low_pair, high_pair,
+    mechanism, cells, cells_row, patches_row, sems,
 ):
     odd = lax.axis_index("east") & 1
-    copies = [(middle, middle_here), (before, before_here), (speed_sq, speed_here)]
+    copies = [
+        (cells_far, cells), (cells_row_far, cells_row), (patches_row_far, patches_row),
+        (mechanism_far, mechanism), (speed_sq, speed_here), (middle, middle_here), (before, before_here),
+    ]
+    first = len(copies)
     for message, high in ((low_pair, 1 - odd), (high_pair, odd)):
         four, two = high * (CE - 4), high * (CE - 2)
         for c in range(3):
@@ -61,7 +69,7 @@
     started = [pltpu.make_async_copy(a, b, sems.at[i]) for i, (a, b) in enumerate(copies)]
     for copy in started:
         copy.start()
-    for copy in started[:3]:
+    for copy in started[:first]:
         copy.wait()
     odd_north = (lax.axis_index("north") & 1) == 1
 
@@ -75,7 +83,22 @@
             put(slot * 4, 4, middle_here[c, e, 0:4, :], middle_here[c, e, CN - 4 : CN, :])
             put(N_PREV + slot * 2, 2, before_here[c, e, 0:2, :], before_here[c, e, CN - 2 : CN, :])
         put(N_SPEED + e * 2, 2, speed_here[e, 0:2, :], speed_here[e, CN - 2 : CN, :])
-    for copy in started[3:]:
+    lane = lax.broadcasted_iota(jnp.int32, (1, CZ), 1)
+    speeds = jnp.zeros((1, CZ), jnp.float32)
+    for i in range(SUBS):
+        cell = cells[i]
+        depth = cell & (CZ - 1)
+        row = speed_here[cell >> 12, pl.ds((cell >> 7) & (CN - 1), 1), :]
+        speeds += pltpu.roll(jnp.where(lane == depth, row, 0.0), (i - depth) & (CZ - 1), 1)
+    for message in (near, far):
+        message[N_SUBS : N_SUBS + S_LEN, :] = jnp.zeros((S_LEN, CZ), jnp.float32)
+        message[N_SUBS : N_SUBS + 1, 0:SUBS] = cells_row[...].astype(jnp.float32)
+        message[N_SUBS + 1 : N_SUBS + 2, 0:SUBS] = patches_row[...].astype(jnp.float32)
+        message[N_SUBS + 2 : N_SUBS + 5, 0:SUBS] = mechanism[3:6, :] * speeds[:, 0:SUBS]
+    for message in (low_pair, high_pair):
+        message[E_SUBS] = jnp.zeros((CN, CZ), jnp.float32)
+        message[E_SUBS, 0:S_LEN, :] = near[N_SUBS : N_SUBS + S_LEN, :]
+    for copy in started[first:]:
         copy.wait()
 
 
@@ -103,9 +126,8 @@
     return south, north
 
 
-def corner_kernel(far_pair, near_pair, low_pair, high_pair):
+def put_corners(south, north, low_pair, high_pair):
     odd = (lax.axis_index("east") & 1) == 1
-    south, north = north_rows(near_pair, far_pair)
     for c in range(3):
         for k in range(2):
             at = (c * 2 + k) * 4
@@ -128,14 +150,20 @@
 
 
 def steps_kernel(
-    before, middle, speed_sq, far_pair, near_pair, low_pair, high_pair, low_corner, high_corner,
-    mechanism_far, cells_far, patches_far, next_out, last_out, parts,
-    wide, later, field_last, edge_before, edge_speed, mechanism, cells, patches, sub_sems, out_sems,
+    before, middle, speed_sq, far_pair, near_pair, low_pair, high_pair,
+    mechanism_far, cells_far, patches_far, next_out, field_last, parts, low_corner, high_corner,
+    wide, later, beyond, edge_before, edge_speed, mechanism, cells, patches, theirs, sub_sems, out_sems,
 ):
     subs = [
         pltpu.make_async_copy(a, b, sub_sems.at[i])
         for i, (a, b) in enumerate(
-            ((mechanism_far, mechanism), (cells_far, cells), (patches_far, patches))
+            (
+                (mechanism_far, mechanism), (cells_far, cells), (patches_far, patches),
+                (low_pair.at[E_SUBS, pl.ds(0, S_LEN)], theirs.at[0]),
+                (high_pair.at[E_SUBS, pl.ds(0, S_LEN)], theirs.at[1]),
+                (near_pair.at[pl.ds(N_SUBS, S_LEN)], theirs.at[2]),
+                (far_pair.at[pl.ds(N_SUBS, S_LEN)], theirs.at[3]),
+            )
         )
     ]
     for copy in subs:
@@ -145,16 +173,47 @@
         own = later.at[c, pl.ds(2, CE), pl.ds(TOP, CN)]
         return pltpu.make_async_copy(own, next_out.at[c], out_sems.at[c])
 
-    def last_copy(c):
-        return pltpu.make_async_copy(field_last.at[c], last_out.at[c], out_sems.at[3 + c])
 
     west, east = east_layers(low_pair, high_pair)
     south, north = north_rows(near_pair, far_pair)
-    odd = (lax.axis_index("east") & 1) == 1
-
+    put_corners(south, north, low_corner, high_corner)
     for e in range(CE):
         edge_speed[e, 6:8, :] = south(N_SPEED + e * 2, 2)
         edge_speed[e, 8:10, :] = north(N_SPEED + e * 2, 2)
+
+    beyond[...] = jnp.zeros_like(beyond)
+
+    def put_beyond(c):
+        def row(layer, at):
+            return wide[c, layer + 2, TOP + at : TOP + at + 1, :]
+
+        def two(one, other):
+            return NEAR * one + FAR * other, FAR * one
+
+        def put(side, e, n, value):
+            at = (e if e < 2 else e - 4) * 4 + (n if n < 2 else n - CN + 4)
+            beyond[side, c, at : at + 1, :] = value
+
+        for side, e, step in ((0, 0, 1), (1, CE - 1, -1)):
+            mine = CE - 1 - e
+            for n, inward, halo in ((0, 1, -1), (CN - 1, -1, CN)):
+                sums = []
+                for layer in (mine, mine - step):
+                    near, far = two(row(layer, halo), row(layer, halo - inward))
+                    sums.append((speed_sq[layer, n : n + 1, :] * near, speed_sq[layer, n + inward : n + inward + 1, :] * far))
+                for j in range(2):
+                    for i, value in enumerate(two(sums[0][j], sums[1][j])):
+                        put(side, e + i * step, n + j * inward, value)
+        for side, n, step in ((2, 0, 1), (3, CN - 1, -1)):
+            mine = CN - 1 - n
+            for e, inward, halo in ((0, 1, -1), (CE - 1, -1, CE)):
+                sums = []
+                for at in (mine, mine - step):
+                    near, far = two(row(halo, at), row(halo - inward, at))
+                    sums.append((speed_sq[e, at : at + 1, :] * near, speed_sq[e + inward, at : at + 1, :] * far))
+                for i in range(2):
+                    for j, value in enumerate(two(sums[0][i], sums[1][i])):
+                        put(side, e + i * inward, n + j * step, value)
 
     def first(c, carry):
         def layer(k):
@@ -172,11 +231,8 @@
                 wide[c, k, TOP - 4 : TOP, :] = south(at, 4)
                 wide[c, k, TOP + CN : TOP + CN + 4, :] = north(at, 4)
             else:
-                at = pl.multiple_of((c * 2 + e % CE % 6) * 4, 4)
-                low, high = low_corner[pl.ds(at, 4), :], high_corner[pl.ds(at, 4), :]
-                corner = jnp.where(odd, low, high) if e < 0 else jnp.where(odd, high, low)
-                wide[c, k, TOP - 2 : TOP, :] = corner[0:2]
-                wide[c, k, TOP + CN : TOP + CN + 2, :] = corner[2:4]
+                wide[c, k, TOP - 2 : TOP, :] = jnp.zeros((2, CZ), jnp.float32)
+                wide[c, k, TOP + CN : TOP + CN + 2, :] = jnp.zeros((2, CZ), jnp.float32)
         for e in range(-2, CE + 2):
             k = e + 2
 
@@ -198,6 +254,7 @@
             new = 2.0 * here - old + speed * total
             later[c, k, TOP : TOP + CN, :] = new
         next_copy(c).start()
+        put_beyond(c)
         for e in range(CE):
             k = e + 2
             at = pl.multiple_of(N_PREV + (c * CE + e) * 2, 2)
@@ -235,13 +292,20 @@
                 rows(-2) + rows(2) + rows(0, -2) + rows(0, 2),
             )
             field_last[c, e] = 2.0 * here - middle[c, e] + speed_sq[e] * total
-        last_copy(c).start()
         return carry
 
     lax.fori_loop(0, 3, second, 0)
 
     lane = lax.broadcasted_iota(jnp.int32, (1, CZ), 1)
     parts[...] = jnp.zeros_like(parts)
+
+    def add(total, depth, patch):
+        run, at = patch >> 11, (patch >> 6) & (PLANE - 1)
+        place = (at & (PER_ROW - 1)) * PATCH_DEV + (patch & (PATCH_DEV - 1))
+        turned = pltpu.roll(jnp.where(lane == depth, total, 0.0), (place - depth) & (CZ - 1), 1)
+        to = run * N_NORTH + ((patch >> 3) & (N_NORTH - 1))
+        parts[to, pl.ds(at >> 4, 1), :] += turned
+
     for copy in subs:
         copy.wait()
     for i in range(SUBS):
@@ -251,18 +315,63 @@
         for c in range(3):
             total += mechanism[c, i] * later[c, layer + 2, pl.ds(TOP + row, 1), :]
             total += mechanism[3 + c, i] * field_last[c, layer, pl.ds(row, 1), :]
-        total = jnp.where(lane == depth, total, 0.0)
-        run, at = patch >> 11, (patch >> 6) & (PLANE - 1)
-        place = (at & (PER_ROW - 1)) * PATCH_DEV + (patch & (PATCH_DEV - 1))
-        turned = pltpu.roll(total, (place - depth) & (CZ - 1), 1)
-        to = run * N_NORTH + ((patch >> 3) & (N_NORTH - 1))
-        parts[to, pl.ds(at >> 4, 1), :] += turned
+        add(total, depth, patch)
+
+    odd, odd_north = lax.axis_index("east") & 1, lax.axis_index("north") & 1
+    sides = odd, 1 - odd, 2 + odd_north, 3 - odd_north
+
+    def neighbours(i, carry):
+        for m, side in enumerate(sides):
+            cell = theirs[m, 0, i].astype(jnp.int32)
+            layer, row, depth = cell >> 12, (cell >> 7) & (CN - 1), cell & (CZ - 1)
+
+            @pl.when(((layer < 2) | (layer >= CE - 2)) & ((row < 2) | (row >= CN - 2)))
+            def _():
+                at = jnp.where(layer < 2, layer, layer - 4) * 4 + jnp.where(row < 2, row, row - CN + 4)
+                total = jnp.zeros((1, CZ), jnp.float32)
+                for c in range(3):
+                    total += theirs[m, 2 + c, i] * beyond[side, c, pl.ds(at, 1), :]
+                add(total, depth, theirs[m, 1, i].astype(jnp.int32))
+
+        return carry
+
+    lax.fori_loop(0, SUBS, neighbours, 0)
     for c in range(3):
         next_copy(c).wait()
-        last_copy(c).wait()
-
-
-def spread_kernel(parts, out):
+
+
+def corner_kernel(
+    last, speed_sq, far_pair, near_pair, low_pair, high_pair, low_corner, high_corner, out
+):
+    west, east = east_layers(low_pair, high_pair)
+    south, north = north_rows(near_pair, far_pair)
+    odd = (lax.axis_index("east") & 1) == 1
+    low, high = low_corner[...], high_corner[...]
+    weight = {1: NEAR, 2: FAR}
+    out[...] = last[...]
+    for column, corner, e0, e_step in (
+        (west, jnp.where(odd, low, high), 0, 1), (east, jnp.where(odd, high, low), CE - 1, -1)
+    ):
+        columns = {i: column(E_SPEED + (2 - i if e0 == 0 else i - 1)) for i in (1, 2)}
+        for rows, n0, n_step, first in ((south, 0, 1, 0), (north, CN - 1, -1, 2)):
+            for e_in in range(2):
+                e = e0 + e_in * e_step
+                beside = rows(N_SPEED + e * 2, 2)
+                for n_in in range(2):
+                    n = n0 + n_in * n_step
+                    for c in range(3):
+                        total = jnp.zeros((1, CZ), jnp.float32)
+                        for i in range(1, 3 - e_in):
+                            k = 2 - i if e0 == 0 else i - 1
+                            for j in range(1, 3 - n_in):
+                                r = 2 - j if n0 == 0 else j - 1
+                                at = (c * 2 + k) * 4 + first + r
+                                speeds = columns[i][n : n + 1, :] + beside[r : r + 1, :]
+                                total += (weight[e_in + i] * weight[n_in + j]) * corner[at : at + 1, :] * speeds
+                        out[c, e, n : n + 1, :] += speed_sq[e, n : n + 1, :] * total
+
+
+def spread_kernel(parts, _, out):
     total = jnp.sum(parts[...], axis=0)
     for row in range(ROWS):
         out[row * PER_ROW : (row + 1) * PER_ROW] = jnp.broadcast_to(
@@ -284,45 +393,57 @@
         pltpu.VMEM((3, CE, CN, CZ), f32), pltpu.VMEM((3, CE, CN, CZ), f32), pltpu.VMEM((CE, CN, CZ), f32)
     )
     east_message, north_message = pltpu.VMEM((E_LEN, CN, CZ), f32), pltpu.VMEM((N_LEN, CZ), f32)
-    inputs = [pltpu.with_memory_space_constraint(x, pltpu.HBM) for x in (field_prev, field_now, speed_sq)]
+    inputs = [
+        pltpu.with_memory_space_constraint(x, pltpu.HBM)
+        for x in (
+            field_prev, field_now, speed_sq, mechanism, sub_cells,
+            sub_cells.reshape(1, SUBS), sub_patch.reshape(1, SUBS), sub_patch,
+        )
+    ]
+    i32 = jnp.int32
     field_prev, field_now, speed_sq, far, near, low_pair, high_pair = pl.pallas_call(
         load_kernel, out_shape=[*held] + [north_message] * 2 + [east_message] * 2,
-        in_specs=[HBM] * 3, out_specs=[VMEM] * 7,
-        scratch_shapes=[pltpu.SemaphoreType.DMA((17,))], compiler_params=params, name="load",
-    )(*inputs)
+        in_specs=[HBM] * 7, out_specs=[VMEM] * 7,
+        scratch_shapes=[
+            pltpu.VMEM((6, SUBS), f32), pltpu.SMEM((SUBS,), i32), pltpu.VMEM((1, SUBS), i32),
+            pltpu.VMEM((1, SUBS), i32), pltpu.SemaphoreType.DMA((21,)),
+        ],
+        compiler_params=params, name="load",
+    )(*inputs[:7])
     far_pair = swap(far, "north", 1)
     near_pair = swap(near, "north", 0)
-    pairs = swap(low_pair, "east", 0), swap(high_pair, "east", 1)
-    low_corner, high_corner = pl.pallas_call(
-        corner_kernel, out_shape=[pltpu.VMEM((C_LEN, CZ), f32)] * 2, in_specs=[VMEM] * 2,
-        out_specs=[VMEM] * 2, compiler_params=params, name="corners",
-    )(far_pair, near_pair)
-    corners = swap(low_corner, "east", 0), swap(high_corner, "east", 1)
+    halos = far_pair, near_pair, swap(low_pair, "east", 0), swap(high_pair, "east", 1)
     wide = pltpu.VMEM((3, LAYERS, CN + 2 * TOP, CZ), f32)
     parts = pltpu.VMEM((COLUMN, ROWS, CZ), f32)
-    field = pltpu.HBM((3, CE, CN, CZ), f32)
-    subs = [pltpu.with_memory_space_constraint(x, pltpu.HBM) for x in (mechanism, sub_cells, sub_patch)]
-    field_next, field_last, parts = pl.pallas_call(
-        steps_kernel, out_shape=[field, field, parts], in_specs=[VMEM] * 9 + [HBM] * 3,
-        out_specs=[HBM, HBM, VMEM],
+    corner = pltpu.VMEM((C_LEN, CZ), f32)
+    field_next, field_last, parts, low_corner, high_corner = pl.pallas_call(
+        steps_kernel,
+        out_shape=[pltpu.HBM((3, CE, CN, CZ), f32), pltpu.VMEM((3, CE, CN, CZ), f32), parts, corner, corner],
+        in_specs=[VMEM] * 7 + [HBM] * 3, out_specs=[HBM] + [VMEM] * 4,
         scratch_shapes=[
-            wide, wide, pltpu.VMEM((3, CE, CN, CZ), f32),
+            wide, wide, pltpu.VMEM((4, 3, 16, CZ), f32),
             pltpu.VMEM((LAYERS, 16, CZ), f32), pltpu.VMEM((CE, 16, CZ), f32),
-            pltpu.SMEM((6, SUBS), f32), pltpu.SMEM((SUBS,), jnp.int32), pltpu.SMEM((SUBS,), jnp.int32),
-            pltpu.SemaphoreType.DMA((3,)), pltpu.SemaphoreType.DMA((6,)),
+            pltpu.SMEM((6, SUBS), f32), pltpu.SMEM((SUBS,), i32), pltpu.SMEM((SUBS,), i32),
+            pltpu.SMEM((4, S_LEN, CZ), f32),
+            pltpu.SemaphoreType.DMA((7,)), pltpu.SemaphoreType.DMA((3,)),
         ],
         compiler_params=params, name="steps",
-    )(field_prev, field_now, speed_sq, far_pair, near_pair, *pairs, *corners, *subs)
+    )(field_prev, field_now, speed_sq, *halos, inputs[3], inputs[4], inputs[7])
+    corners = swap(low_corner, "east", 0), swap(high_corner, "east", 1)
     parts = lax.all_to_all(parts, BOTH, 0, 0, tiled=True, axis_index_groups=column_groups())
     parts = pl.pallas_call(
-        spread_kernel, out_shape=jax.ShapeDtypeStruct((PLANE, 1, CZ), f32),
-        in_specs=[VMEM], out_specs=VMEM, compiler_params=params, name="spread",
-    )(parts)
+        spread_kernel, out_shape=pltpu.VMEM((PLANE, 1, CZ), f32),
+        in_specs=[VMEM] * 2, out_specs=VMEM, compiler_params=params, name="spread",
+    )(parts, corners[0])
     parts = lax.all_to_all(parts, BOTH, 0, 0, tiled=True, axis_index_groups=plane_groups())
     own = pl.pallas_call(
         own_kernel, out_shape=jax.ShapeDtypeStruct((1, PATCH_DEV), f32),
         in_specs=[VMEM], out_specs=VMEM, compiler_params=params, name="own",
     )(parts)
+    field_last = pl.pallas_call(
+        corner_kernel, out_shape=jax.ShapeDtypeStruct((3, CE, CN, CZ), f32), in_specs=[VMEM] * 8,
+        out_specs=VMEM, compiler_params=params, name="corners",
+    )(field_last, speed_sq, *halos, *corners)
     return field_next, field_last, own.reshape(PATCH_DEV)
 
 

time: 75.5 us -> 70 us (0.927); the launches traced: 75.2 us -> 68.9 us
  blocking collectives: 47 us -> 0 us
  starting transfers between devices: 21.6 us -> 44.6 us
  waiting for transfers between devices: 1.3 us -> 15.7 us
  Pallas kernels: 4.63 us -> 7.92 us
    all_to_all x2 -> x0, blocking collectives: 47 us -> none  [the longest x1 35.4 us: body(): lax.all_to_all(parts, BOTH, 0, 0, tiled=True, axis_index_groups=column_gr...]
    all_to_all x0 -> x2, starting transfers between devices: none -> 26.3 us  [the longest x1 21.7 us: body(): lax.all_to_all(parts, BOTH, 0, 0, tiled=True, axis_index_groups=column_gr...]
    all_to_all x0 -> x2, waiting for transfers between devices: none -> 12 us  [the longest x1 7.07 us: body(): lax.all_to_all(parts, BOTH, 0, 0, tiled=True, axis_index_groups=plane_gro...]
    ppermute x6, starting transfers between devices: 21.6 us -> 18.3 us  [swap(): return lax.ppermute(block, axis, pairs + [(j, i) for i, j in pairs])]
    pallas_call x3, Pallas kernels: 2.55 us -> 5.71 us  [the longest x1 4.24 us: body(): pl.pallas_call(steps_kernel, out_shape=[pltpu.HBM((3, CE, CN, CZ), f32),...]
    ppermute x6, waiting for transfers between devices: 1.3 us -> 3.71 us  [swap(): return lax.ppermute(block, axis, pairs + [(j, i) for i, j in pairs])]
  transfers between devices with their start and end apart: 6 -> 8, of which waited for: 2 -> 4; matrix products, arithmetic and copies ran while one was open for 0% -> 0% of each run, Pallas kernels for 0% -> 1%
where the time goes in v5:
time: 70 us; the launch traced here: 68.9 us
  starting transfers between devices  44.6 us (64%)
  waiting for transfers between devices  15.7 us (22%)
  Pallas kernels  7.92 us (11%)
  between operations  0.73 us (1%)
    all_to_all x1, starting transfers between devices, body(): lax.all_to_all(parts, BOTH, 0, 0, tiled=True, axis_index_groups=column_gr...  21.7 us
    ppermute x6, starting transfers between devices, swap(): return lax.ppermute(block, axis, pairs + [(j, i) for i, j in pairs])  18.3 us
    all_to_all x1, waiting for transfers between devices, body(): lax.all_to_all(parts, BOTH, 0, 0, tiled=True, axis_index_groups=plane_gro...  7.07 us
    all_to_all x1, waiting for transfers between devices, body(): lax.all_to_all(parts, BOTH, 0, 0, tiled=True, axis_index_groups=column_gr...  4.92 us
    all_to_all x1, starting transfers between devices, body(): lax.all_to_all(parts, BOTH, 0, 0, tiled=True, axis_index_groups=plane_gro...  4.56 us
    pallas_call x1, Pallas kernels, body(): pl.pallas_call(steps_kernel, out_shape=[pltpu.HBM((3, CE, CN, CZ), f32),...  4.24 us
    ppermute x6, waiting for transfers between devices, swap(): return lax.ppermute(block, axis, pairs + [(j, i) for i, j in pairs])  3.71 us
    pallas_call x1, Pallas kernels, body(): pl.pallas_call(load_kernel, out_shape=[*held] + [north_message] * 2 + [ea...  1.6 us
  transfers between devices with their start and end apart: 8, of which 4 were waited for; matrix products, arithmetic and copies ran while one was open for 0% of the time, Pallas kernels for 1%

profile of v5, /device:TPU:1, one launch (start us, length us, event | category | flops | bytes accessed | tf_op | source)
XLA Modules:
  0.0 68.9 jit_solution(11550368168710796851)
XLA Ops:
  0.6 1.6 %load.1 = (f32[3,8,32,128]{3,2,1,0:T(8,128)S(1)}, f32[3,8,32,128]{3,2,1,0:T(8,128)S(1)}, f32[8,32,128]{2,1,0:T(8,128)S(1)}, f32[168,128]{1,0:T(8,128)S(1)}, f32[...) custom-call(f32[3,8,32,128]{3,2,1,0:T(8,128)} %before.1, f32[3,8,32,128]{3,2,1,0:T(8,128)} %middle.1, ...), custom_call_target="tpu_custom_call" | custom-call | tf_op jit(solution)/shard_map/load/pallas_call | solution.py:404
  2.2 3.9 %collective-permute-start.2 = (f32[21,32,128]{2,1,0:T(8,128)S(1)}, f32[21,32,128]{2,1,0:T(8,128)S(1)}, u32[]{:S(2)}, u32[]{:S(2)}) collective-permute-start(f32[21,32,128]{2,1,0:T(8,128)S(1)} %get-tuple-element.20), channel_id=1, source_target_pairs={{0,8},{16,24},{32,40},{48,56},{64,72},{80,88},{96,104},{112,120},{... | collective-permute-start | bytes 1032200 | tf_op jit(solution)/shard_map/ppermute | solution.py:49
  6.2 0.7 collective-permute-start.3
  6.9 8.5 %collective-permute-start = (f32[168,128]{1,0:T(8,128)S(1)}, f32[168,128]{1,0:T(8,128)S(1)}, u32[]{:S(2)}, u32[]{:S(2)}) collective-permute-start(f32[168,128]{1,0:T(8,128)S(1)} %get-tuple-element.18), channel_id=1, source_target_pairs={{1,2},{3,4},{5,6},{2,1},{4,3},{6,5},{9,10},{11,12},{13,14},{10,9},... | collective-permute-start | bytes 258056 | tf_op jit(solution)/shard_map/ppermute | solution.py:49
  15.3 2.6 %collective-permute-start.1 = (f32[168,128]{1,0:T(8,128)S(1)}, f32[168,128]{1,0:T(8,128)S(1)}, u32[]{:S(2)}, u32[]{:S(2)}) collective-permute-start(f32[168,128]{1,0:T(8,128)S(1)} %get-tuple-element.19), channel_id=1, source_target_pairs={{0,1},{2,3},{4,5},{6,7},{1,0},{3,2},{5,4},{7,6},{8,9},{10,11},{12,... | collective-permute-start | bytes 258056 | tf_op jit(solution)/shard_map/ppermute | solution.py:49
  18.0 0.0 collective-permute-done.far_pair
  18.0 0.9 %collective-permute-done.1.near_pair = f32[168,128]{1,0:T(8,128)S(1)} collective-permute-done((f32[168,128]{1,0:T(8,128)S(1)}, f32[168,128]{1,0:T(8,128)S(1)}, u32[]{:S(2)}, u32[]{:S(2)}) %collective-permute-start.1) | collective-permute-done | bytes 86048 | tf_op jit(solution)/shard_map/ppermute | solution.py:49
  18.9 0.0 collective-permute-done.2.low_pair
  18.9 0.0 collective-permute-done.3.high_pair
  18.9 4.2 %steps.1 = (f32[3,8,32,128]{3,2,1,0:T(8,128)}, f32[3,8,32,128]{3,2,1,0:T(8,128)S(1)}, f32[24,2,128]{2,1,0:T(2,128)}, f32[24,128]{1,0:T(8,128)S(1)}, f32[24,128]{1,0:T(8,128)S(1)}) custom-call(f32[3,8,32,128]{3,2,1,0:T(8,128)S(1)} %get-tuple-element.15.before, f32[3,8,32,128]{3,2,1,0:T(8,128)S(1)} %get-tuple-element.16.middle, ...), custom_call_target="tpu_custom_call" | custom-call | tf_op jit(solution)/shard_map/steps/pallas_call | solution.py:419
  23.1 21.7 %all-to-all-start = ((f32[24,2,128]{2,1,0:T(2,128)}), f32[24,2,128]{2,1,0:T(2,128)S(1)}, u32[]{:S(2)}, u32[]{:S(2)}) async-start(f32[24,2,128]{2,1,0:T(2,128)} %get-tuple-element.26), calls=%async_computation | async-start | bytes 49152 | tf_op jit(solution)/shard_map/all_to_all | solution.py:433
  44.9 1.9 %collective-permute-start.4 = (f32[24,128]{1,0:T(8,128)S(1)}, f32[24,128]{1,0:T(8,128)S(1)}, u32[]{:S(2)}, u32[]{:S(2)}) collective-permute-start(f32[24,128]{1,0:T(8,128)S(1)} %get-tuple-element.24), channel_id=1, source_target_pairs={{0,8},{16,24},{32,40},{48,56},{64,72},{80,88},{96,104},{112,120},{... | collective-permute-start | bytes 36872 | tf_op jit(solution)/shard_map/ppermute | solution.py:49
  46.8 2.8 %collective-permute-done.4.low_corner._ = f32[24,128]{1,0:T(8,128)S(1)} collective-permute-done((f32[24,128]{1,0:T(8,128)S(1)}, f32[24,128]{1,0:T(8,128)S(1)}, u32[]{:S(2)}, u32[]{:S(2)}) %collective-permute-start.4) | collective-permute-done | bytes 12320 | tf_op jit(solution)/shard_map/ppermute | solution.py:49
  49.6 4.9 %all-to-all-done.parts = f32[24,2,128]{2,1,0:T(2,128)S(1)} async-done(((f32[24,2,128]{2,1,0:T(2,128)}), f32[24,2,128]{2,1,0:T(2,128)S(1)}, u32[]{:S(2)}, u32[]{:S(2)}) %all-to-all-start) | async-done | bytes 24608 | tf_op jit(solution)/shard_map/all_to_all | solution.py:433
  54.5 0.6 spread.1
  55.1 4.6 %all-to-all-start.1 = ((f32[32,1,128]{2,1,0:T(1,128)}), f32[32,1,128]{2,1,0:T(1,128)S(1)}, u32[]{:S(2)}, u32[]{:S(2)}) async-start(f32[32,1,128]{2,1,0:T(1,128)} %spread.1), calls=%async_computation.1 | async-start | bytes 32768 | tf_op jit(solution)/shard_map/all_to_all | solution.py:438
  59.7 0.7 collective-permute-start.5
  60.4 0.0 collective-permute-done.5.high_corner
  60.4 0.8 %corners.1 = f32[3,8,32,128]{3,2,1,0:T(8,128)} custom-call(f32[3,8,32,128]{3,2,1,0:T(8,128)S(1)} %get-tuple-element.23.last, f32[8,32,128]{2,1,0:T(8,128)S(1)} %get-tuple-element.17.speed_sq, f32[168,128]{1,0:T(8,128)S(1)} %collective-permute-done.far_pair, f32[168,128]{1,0:T(8,128)S(1)} %collective-permute-done.1.near_pair, ...), custom_call_target="tpu_custom_call" | custom-call | tf_op jit(solution)/shard_map/corners/pallas_call | solution.py:443
  61.2 7.1 %all-to-all-done.1.parts = f32[32,1,128]{2,1,0:T(1,128)S(1)} async-done(((f32[32,1,128]{2,1,0:T(1,128)}), f32[32,1,128]{2,1,0:T(1,128)S(1)}, u32[]{:S(2)}, u32[]{:S(2)}) %all-to-all-start.1) | async-done | bytes 16416 | tf_op jit(solution)/shard_map/all_to_all | solution.py:438
  68.3 0.6 own.1
Async XLA Ops:
  2.2 16.6 %collective-permute-start.2 = (f32[21,32,128]{2,1,0:T(8,128)S(1)}, f32[21,32,128]{2,1,0:T(8,128)S(1)}, u32[]{:S(2)}, u32[]{:S(2)}) collective-permute-start(f32[21,32,128]{2,1,0:T(8,128)S(1)} %get-tuple-element.20), channel_id=1, source_target_pairs={{0,8},{16,24},{32,40},{48,56},{64,72},{80,88},{96,104},{112,120},{... | collective-permute-start | bytes 1032200 | tf_op jit(solution)/shard_map/ppermute | solution.py:49
  6.2 12.7 %collective-permute-start.3 = (f32[21,32,128]{2,1,0:T(8,128)S(1)}, f32[21,32,128]{2,1,0:T(8,128)S(1)}, u32[]{:S(2)}, u32[]{:S(2)}) collective-permute-start(f32[21,32,128]{2,1,0:T(8,128)S(1)} %get-tuple-element.21), channel_id=1, source_target_pairs={{8,16},{24,32},{40,48},{56,64},{72,80},{88,96},{104,112},{120,128}... | collective-permute-start | bytes 1032200 | tf_op jit(solution)/shard_map/ppermute | solution.py:49
  6.9 11.1 %collective-permute-start = (f32[168,128]{1,0:T(8,128)S(1)}, f32[168,128]{1,0:T(8,128)S(1)}, u32[]{:S(2)}, u32[]{:S(2)}) collective-permute-start(f32[168,128]{1,0:T(8,128)S(1)} %get-tuple-element.18), channel_id=1, source_target_pairs={{1,2},{3,4},{5,6},{2,1},{4,3},{6,5},{9,10},{11,12},{13,14},{10,9},... | collective-permute-start | bytes 258056 | tf_op jit(solution)/shard_map/ppermute | solution.py:49
  15.3 3.5 %collective-permute-start.1 = (f32[168,128]{1,0:T(8,128)S(1)}, f32[168,128]{1,0:T(8,128)S(1)}, u32[]{:S(2)}, u32[]{:S(2)}) collective-permute-start(f32[168,128]{1,0:T(8,128)S(1)} %get-tuple-element.19), channel_id=1, source_target_pairs={{0,1},{2,3},{4,5},{6,7},{1,0},{3,2},{5,4},{7,6},{8,9},{10,11},{12,... | collective-permute-start | bytes 258056 | tf_op jit(solution)/shard_map/ppermute | solution.py:49
  23.1 31.4 %all-to-all-start = ((f32[24,2,128]{2,1,0:T(2,128)}), f32[24,2,128]{2,1,0:T(2,128)S(1)}, u32[]{:S(2)}, u32[]{:S(2)}) async-start(f32[24,2,128]{2,1,0:T(2,128)} %get-tuple-element.26), calls=%async_computation | async-start | bytes 49152 | tf_op jit(solution)/shard_map/all_to_all | solution.py:433
  44.9 4.7 %collective-permute-start.4 = (f32[24,128]{1,0:T(8,128)S(1)}, f32[24,128]{1,0:T(8,128)S(1)}, u32[]{:S(2)}, u32[]{:S(2)}) collective-permute-start(f32[24,128]{1,0:T(8,128)S(1)} %get-tuple-element.24), channel_id=1, source_target_pairs={{0,8},{16,24},{32,40},{48,56},{64,72},{80,88},{96,104},{112,120},{... | collective-permute-start | bytes 36872 | tf_op jit(solution)/shard_map/ppermute | solution.py:49
  55.1 13.1 %all-to-all-start.1 = ((f32[32,1,128]{2,1,0:T(1,128)}), f32[32,1,128]{2,1,0:T(1,128)S(1)}, u32[]{:S(2)}, u32[]{:S(2)}) async-start(f32[32,1,128]{2,1,0:T(1,128)} %spread.1), calls=%async_computation.1 | async-start | bytes 32768 | tf_op jit(solution)/shard_map/all_to_all | solution.py:438
  59.7 0.7 collective-permute-start.5

commit v6 on v5

--- a/solution.py
+++ b/solution.py
@@ -151,8 +151,8 @@
 
 def steps_kernel(
     before, middle, speed_sq, far_pair, near_pair, low_pair, high_pair,
-    mechanism_far, cells_far, patches_far, next_out, field_last, parts, low_corner, high_corner,
-    wide, later, beyond, edge_before, edge_speed, mechanism, cells, patches, theirs, sub_sems, out_sems,
+    mechanism_far, cells_far, patches_far, next_out, later, parts, low_corner, high_corner,
+    wide, beyond, edge_before, edge_speed, mechanism, cells, patches, theirs, sub_sems, out_sems,
 ):
     subs = [
         pltpu.make_async_copy(a, b, sub_sems.at[i])
@@ -278,24 +278,6 @@
 
     lax.fori_loop(0, 3, first, 0)
 
-    def second(c, carry):
-        for e in range(CE):
-            k = e + 2
-
-            def rows(layers, offset=0):
-                return later[c, k + layers, TOP + offset : TOP + offset + CN, :]
-
-            here = rows(0)
-            total = laplace(
-                here,
-                rows(-1) + rows(1) + rows(0, -1) + rows(0, 1),
-                rows(-2) + rows(2) + rows(0, -2) + rows(0, 2),
-            )
-            field_last[c, e] = 2.0 * here - middle[c, e] + speed_sq[e] * total
-        return carry
-
-    lax.fori_loop(0, 3, second, 0)
-
     lane = lax.broadcasted_iota(jnp.int32, (1, CZ), 1)
     parts[...] = jnp.zeros_like(parts)
 
@@ -311,10 +293,18 @@
     for i in range(SUBS):
         cell, patch = cells[i], patches[i]
         layer, row, depth = cell >> 12, (cell >> 7) & (CN - 1), cell & (CZ - 1)
-        total = jnp.zeros((1, CZ), jnp.float32)
+        total, here, near, far = (jnp.zeros((1, CZ), jnp.float32) for _ in range(4))
         for c in range(3):
-            total += mechanism[c, i] * later[c, layer + 2, pl.ds(TOP + row, 1), :]
-            total += mechanism[3 + c, i] * field_last[c, layer, pl.ds(row, 1), :]
+
+            def point(layers=0, rows=0):
+                return later[c, layer + 2 + layers, pl.ds(TOP + row + rows, 1), :]
+
+            weight = mechanism[3 + c, i]
+            total += mechanism[c, i] * point() - weight * middle[c, layer, pl.ds(row, 1), :]
+            here += weight * point()
+            near += weight * (point(-1) + point(1) + point(0, -1) + point(0, 1))
+            far += weight * (point(-2) + point(2) + point(0, -2) + point(0, 2))
+        total += 2.0 * here + speed_sq[layer, pl.ds(row, 1), :] * laplace(here, near, far)
         add(total, depth, patch)
 
     odd, odd_north = lax.axis_index("east") & 1, lax.axis_index("north") & 1
@@ -338,6 +328,25 @@
     lax.fori_loop(0, SUBS, neighbours, 0)
     for c in range(3):
         next_copy(c).wait()
+
+
+def last_kernel(middle, speed_sq, later, out):
+    def component(c, carry):
+        for e in range(CE):
+
+            def rows(layers, offset=0):
+                return later[c, e + 2 + layers, TOP + offset : TOP + offset + CN, :]
+
+            here = rows(0)
+            total = laplace(
+                here,
+                rows(-1) + rows(1) + rows(0, -1) + rows(0, 1),
+                rows(-2) + rows(2) + rows(0, -2) + rows(0, 2),
+            )
+            out[c, e] = 2.0 * here - middle[c, e] + speed_sq[e] * total
+        return carry
+
+    lax.fori_loop(0, 3, component, 0)
 
 
 def corner_kernel(
@@ -416,12 +425,12 @@
     wide = pltpu.VMEM((3, LAYERS, CN + 2 * TOP, CZ), f32)
     parts = pltpu.VMEM((COLUMN, ROWS, CZ), f32)
     corner = pltpu.VMEM((C_LEN, CZ), f32)
-    field_next, field_last, parts, low_corner, high_corner = pl.pallas_call(
+    field_next, later, parts, low_corner, high_corner = pl.pallas_call(
         steps_kernel,
-        out_shape=[pltpu.HBM((3, CE, CN, CZ), f32), pltpu.VMEM((3, CE, CN, CZ), f32), parts, corner, corner],
+        out_shape=[pltpu.HBM((3, CE, CN, CZ), f32), wide, parts, corner, corner],
         in_specs=[VMEM] * 7 + [HBM] * 3, out_specs=[HBM] + [VMEM] * 4,
         scratch_shapes=[
-            wide, wide, pltpu.VMEM((4, 3, 16, CZ), f32),
+            wide, pltpu.VMEM((4, 3, 16, CZ), f32),
             pltpu.VMEM((LAYERS, 16, CZ), f32), pltpu.VMEM((CE, 16, CZ), f32),
             pltpu.SMEM((6, SUBS), f32), pltpu.SMEM((SUBS,), i32), pltpu.SMEM((SUBS,), i32),
             pltpu.SMEM((4, S_LEN, CZ), f32),
@@ -430,11 +439,16 @@
         compiler_params=params, name="steps",
     )(field_prev, field_now, speed_sq, *halos, inputs[3], inputs[4], inputs[7])
     corners = swap(low_corner, "east", 0), swap(high_corner, "east", 1)
+    field_last = pl.pallas_call(
+        last_kernel, out_shape=pltpu.VMEM((3, CE, CN, CZ), f32), in_specs=[VMEM] * 3, out_specs=VMEM,
+        compiler_params=params, name="last",
+        cost_estimate=pl.CostEstimate(flops=3_000_000, bytes_accessed=1_000_000, transcendentals=0),
+    )(field_now, speed_sq, later)
     parts = lax.all_to_all(parts, BOTH, 0, 0, tiled=True, axis_index_groups=column_groups())
     parts = pl.pallas_call(
         spread_kernel, out_shape=pltpu.VMEM((PLANE, 1, CZ), f32),
         in_specs=[VMEM] * 2, out_specs=VMEM, compiler_params=params, name="spread",
-    )(parts, corners[0])
+    )(parts, corners[1])
     parts = lax.all_to_all(parts, BOTH, 0, 0, tiled=True, axis_index_groups=plane_groups())
     own = pl.pallas_call(
         own_kernel, out_shape=jax.ShapeDtypeStruct((1, PATCH_DEV), f32),

time: 70 us -> 68.7 us (0.981); the launches traced: 68.9 us -> 68.4 us
  waiting for transfers between devices: 15.7 us -> 13.8 us
  starting transfers between devices: 44.6 us -> 45.9 us
    all_to_all x1, waiting for transfers between devices: 7.07 us -> 3.01 us  [body(): lax.all_to_all(parts, BOTH, 0, 0, tiled=True, axis_index_groups=plane_gro...]
    all_to_all x1, waiting for transfers between devices: 4.92 us -> 8.97 us  [body(): lax.all_to_all(parts, BOTH, 0, 0, tiled=True, axis_index_groups=column_gr...]
    ppermute x6, waiting for transfers between devices: 3.71 us -> 1.87 us  [swap(): return lax.ppermute(block, axis, pairs + [(j, i) for i, j in pairs])]
    ppermute x6, starting transfers between devices: 18.3 us -> 19.5 us  [swap(): return lax.ppermute(block, axis, pairs + [(j, i) for i, j in pairs])]
  transfers between devices with their start and end apart: 8 -> 8, of which waited for: 4 -> 4; matrix products, arithmetic and copies ran while one was open for 0% -> 0% of each run, Pallas kernels for 1% -> 2%
where the time goes in v6:
time: 68.7 us; the launch traced here: 68.4 us
  starting transfers between devices  45.9 us (67%)
  waiting for transfers between devices  13.8 us (20%)
  Pallas kernels  7.85 us (11%)
  between operations  0.74 us (1%)
    all_to_all x1, starting transfers between devices, body(): lax.all_to_all(parts, BOTH, 0, 0, tiled=True, axis_index_groups=column_gr...  21.9 us
    ppermute x6, starting transfers between devices, swap(): return lax.ppermute(block, axis, pairs + [(j, i) for i, j in pairs])  19.5 us
    all_to_all x1, waiting for transfers between devices, body(): lax.all_to_all(parts, BOTH, 0, 0, tiled=True, axis_index_groups=column_gr...  8.97 us
    all_to_all x1, starting transfers between devices, body(): lax.all_to_all(parts, BOTH, 0, 0, tiled=True, axis_index_groups=plane_gro...  4.54 us
    pallas_call x1, Pallas kernels, body(): pl.pallas_call(steps_kernel, out_shape=[pltpu.HBM((3, CE, CN, CZ), f32),...  3.55 us
    all_to_all x1, waiting for transfers between devices, body(): lax.all_to_all(parts, BOTH, 0, 0, tiled=True, axis_index_groups=plane_gro...  3.01 us
    ppermute x6, waiting for transfers between devices, swap(): return lax.ppermute(block, axis, pairs + [(j, i) for i, j in pairs])  1.87 us
    pallas_call x1, Pallas kernels, body(): pl.pallas_call(load_kernel, out_shape=[*held] + [north_message] * 2 + [ea...  1.6 us
  transfers between devices with their start and end apart: 8, of which 4 were waited for; matrix products, arithmetic and copies ran while one was open for 0% of the time, Pallas kernels for 2%

profile of v6, /device:TPU:1, one launch (start us, length us, event | category | flops | bytes accessed | tf_op | source)
XLA Modules:
  0.0 68.4 jit_solution(9735503817217792366)
XLA Ops:
  0.6 1.6 %load.1 = (f32[3,8,32,128]{3,2,1,0:T(8,128)S(1)}, f32[3,8,32,128]{3,2,1,0:T(8,128)S(1)}, f32[8,32,128]{2,1,0:T(8,128)S(1)}, f32[168,128]{1,0:T(8,128)S(1)}, f32[...) custom-call(f32[3,8,32,128]{3,2,1,0:T(8,128)} %before.1, f32[3,8,32,128]{3,2,1,0:T(8,128)} %middle.1, ...), custom_call_target="tpu_custom_call" | custom-call | tf_op jit(solution)/shard_map/load/pallas_call | solution.py:413
  2.2 3.9 %collective-permute-start.2 = (f32[21,32,128]{2,1,0:T(8,128)S(1)}, f32[21,32,128]{2,1,0:T(8,128)S(1)}, u32[]{:S(2)}, u32[]{:S(2)}) collective-permute-start(f32[21,32,128]{2,1,0:T(8,128)S(1)} %get-tuple-element.20), channel_id=1, source_target_pairs={{0,8},{16,24},{32,40},{48,56},{64,72},{80,88},{96,104},{112,120},{... | collective-permute-start | bytes 1032200 | tf_op jit(solution)/shard_map/ppermute | solution.py:49
  6.2 0.7 collective-permute-start.3
  6.9 8.5 %collective-permute-start = (f32[168,128]{1,0:T(8,128)S(1)}, f32[168,128]{1,0:T(8,128)S(1)}, u32[]{:S(2)}, u32[]{:S(2)}) collective-permute-start(f32[168,128]{1,0:T(8,128)S(1)} %get-tuple-element.18), channel_id=1, source_target_pairs={{1,2},{3,4},{5,6},{2,1},{4,3},{6,5},{9,10},{11,12},{13,14},{10,9},... | collective-permute-start | bytes 258056 | tf_op jit(solution)/shard_map/ppermute | solution.py:49
  15.3 2.6 %collective-permute-start.1 = (f32[168,128]{1,0:T(8,128)S(1)}, f32[168,128]{1,0:T(8,128)S(1)}, u32[]{:S(2)}, u32[]{:S(2)}) collective-permute-start(f32[168,128]{1,0:T(8,128)S(1)} %get-tuple-element.19), channel_id=1, source_target_pairs={{0,1},{2,3},{4,5},{6,7},{1,0},{3,2},{5,4},{7,6},{8,9},{10,11},{12,... | collective-permute-start | bytes 258056 | tf_op jit(solution)/shard_map/ppermute | solution.py:49
  18.0 0.0 collective-permute-done.far_pair
  18.0 0.9 %collective-permute-done.1.near_pair = f32[168,128]{1,0:T(8,128)S(1)} collective-permute-done((f32[168,128]{1,0:T(8,128)S(1)}, f32[168,128]{1,0:T(8,128)S(1)}, u32[]{:S(2)}, u32[]{:S(2)}) %collective-permute-start.1) | collective-permute-done | bytes 86048 | tf_op jit(solution)/shard_map/ppermute | solution.py:49
  18.9 0.0 collective-permute-done.2.low_pair
  18.9 0.0 collective-permute-done.3.high_pair
  18.9 3.5 %steps.1 = (f32[3,8,32,128]{3,2,1,0:T(8,128)}, f32[3,12,64,128]{3,2,1,0:T(8,128)S(1)}, f32[24,2,128]{2,1,0:T(2,128)}, f32[24,128]{1,0:T(8,128)S(1)}, f32[24,128]{1,0:T(8,128)S(1)}) custom-call(f32[3,8,32,128]{3,2,1,0:T(8,128)S(1)} %get-tuple-element.15.before, f32[3,8,32,128]{3,2,1,0:T(8,128)S(1)} %get-tuple-element.16.middle, ...), custom_call_target="tpu_custom_call" | custom-call | tf_op jit(solution)/shard_map/steps/pallas_call | solution.py:428
  22.4 21.9 %all-to-all-start = ((f32[24,2,128]{2,1,0:T(2,128)}), f32[24,2,128]{2,1,0:T(2,128)S(1)}, u32[]{:S(2)}, u32[]{:S(2)}) async-start(f32[24,2,128]{2,1,0:T(2,128)} %get-tuple-element.26), calls=%async_computation | async-start | bytes 49152 | tf_op jit(solution)/shard_map/all_to_all | solution.py:447
  44.3 0.7 collective-permute-start.5
  45.0 0.0 collective-permute-done.5.high_corner._
  45.0 9.0 %all-to-all-done.parts = f32[24,2,128]{2,1,0:T(2,128)S(1)} async-done(((f32[24,2,128]{2,1,0:T(2,128)}), f32[24,2,128]{2,1,0:T(2,128)S(1)}, u32[]{:S(2)}, u32[]{:S(2)}) %all-to-all-start) | async-done | bytes 24608 | tf_op jit(solution)/shard_map/all_to_all | solution.py:447
  54.0 0.6 spread.1
  54.6 4.5 %all-to-all-start.1 = ((f32[32,1,128]{2,1,0:T(1,128)}), f32[32,1,128]{2,1,0:T(1,128)S(1)}, u32[]{:S(2)}, u32[]{:S(2)}) async-start(f32[32,1,128]{2,1,0:T(1,128)} %spread.1), calls=%async_computation.1 | async-start | bytes 32768 | tf_op jit(solution)/shard_map/all_to_all | solution.py:452
  59.2 3.1 %collective-permute-start.4 = (f32[24,128]{1,0:T(8,128)S(1)}, f32[24,128]{1,0:T(8,128)S(1)}, u32[]{:S(2)}, u32[]{:S(2)}) collective-permute-start(f32[24,128]{1,0:T(8,128)S(1)} %get-tuple-element.24), channel_id=1, source_target_pairs={{0,8},{16,24},{32,40},{48,56},{64,72},{80,88},{96,104},{112,120},{... | collective-permute-start | bytes 36872 | tf_op jit(solution)/shard_map/ppermute | solution.py:49
  62.3 0.6 last.1
  63.0 1.0 %collective-permute-done.4.low_corner = f32[24,128]{1,0:T(8,128)S(1)} collective-permute-done((f32[24,128]{1,0:T(8,128)S(1)}, f32[24,128]{1,0:T(8,128)S(1)}, u32[]{:S(2)}, u32[]{:S(2)}) %collective-permute-start.4) | collective-permute-done | bytes 12320 | tf_op jit(solution)/shard_map/ppermute | solution.py:49
  63.9 0.8 %corners.1 = f32[3,8,32,128]{3,2,1,0:T(8,128)} custom-call(f32[3,8,32,128]{3,2,1,0:T(8,128)S(1)} %last.1, f32[8,32,128]{2,1,0:T(8,128)S(1)} %get-tuple-element.17.speed_sq, f32[168,128]{1,0:T(8,128)S(1)} %collective-permute-done.far_pair, f32[168,128]{1,0:T(8,128)S(1)} %collective-permute-done.1.near_pair, ...), custom_call_target="tpu_custom_call" | custom-call | tf_op jit(solution)/shard_map/corners/pallas_call | solution.py:457
  64.8 3.0 %all-to-all-done.1.parts = f32[32,1,128]{2,1,0:T(1,128)S(1)} async-done(((f32[32,1,128]{2,1,0:T(1,128)}), f32[32,1,128]{2,1,0:T(1,128)S(1)}, u32[]{:S(2)}, u32[]{:S(2)}) %all-to-all-start.1) | async-done | bytes 16416 | tf_op jit(solution)/shard_map/all_to_all | solution.py:452
  67.8 0.6 own.1
Async XLA Ops:
  2.2 16.6 %collective-permute-start.2 = (f32[21,32,128]{2,1,0:T(8,128)S(1)}, f32[21,32,128]{2,1,0:T(8,128)S(1)}, u32[]{:S(2)}, u32[]{:S(2)}) collective-permute-start(f32[21,32,128]{2,1,0:T(8,128)S(1)} %get-tuple-element.20), channel_id=1, source_target_pairs={{0,8},{16,24},{32,40},{48,56},{64,72},{80,88},{96,104},{112,120},{... | collective-permute-start | bytes 1032200 | tf_op jit(solution)/shard_map/ppermute | solution.py:49
  6.2 12.7 %collective-permute-start.3 = (f32[21,32,128]{2,1,0:T(8,128)S(1)}, f32[21,32,128]{2,1,0:T(8,128)S(1)}, u32[]{:S(2)}, u32[]{:S(2)}) collective-permute-start(f32[21,32,128]{2,1,0:T(8,128)S(1)} %get-tuple-element.21), channel_id=1, source_target_pairs={{8,16},{24,32},{40,48},{56,64},{72,80},{88,96},{104,112},{120,128}... | collective-permute-start | bytes 1032200 | tf_op jit(solution)/shard_map/ppermute | solution.py:49
  6.9 11.1 %collective-permute-start = (f32[168,128]{1,0:T(8,128)S(1)}, f32[168,128]{1,0:T(8,128)S(1)}, u32[]{:S(2)}, u32[]{:S(2)}) collective-permute-start(f32[168,128]{1,0:T(8,128)S(1)} %get-tuple-element.18), channel_id=1, source_target_pairs={{1,2},{3,4},{5,6},{2,1},{4,3},{6,5},{9,10},{11,12},{13,14},{10,9},... | collective-permute-start | bytes 258056 | tf_op jit(solution)/shard_map/ppermute | solution.py:49
  15.3 3.5 %collective-permute-start.1 = (f32[168,128]{1,0:T(8,128)S(1)}, f32[168,128]{1,0:T(8,128)S(1)}, u32[]{:S(2)}, u32[]{:S(2)}) collective-permute-start(f32[168,128]{1,0:T(8,128)S(1)} %get-tuple-element.19), channel_id=1, source_target_pairs={{0,1},{2,3},{4,5},{6,7},{1,0},{3,2},{5,4},{7,6},{8,9},{10,11},{12,... | collective-permute-start | bytes 258056 | tf_op jit(solution)/shard_map/ppermute | solution.py:49
  22.4 31.6 %all-to-all-start = ((f32[24,2,128]{2,1,0:T(2,128)}), f32[24,2,128]{2,1,0:T(2,128)S(1)}, u32[]{:S(2)}, u32[]{:S(2)}) async-start(f32[24,2,128]{2,1,0:T(2,128)} %get-tuple-element.26), calls=%async_computation | async-start | bytes 49152 | tf_op jit(solution)/shard_map/all_to_all | solution.py:447
  44.3 0.7 collective-permute-start.5
  54.6 13.1 %all-to-all-start.1 = ((f32[32,1,128]{2,1,0:T(1,128)}), f32[32,1,128]{2,1,0:T(1,128)S(1)}, u32[]{:S(2)}, u32[]{:S(2)}) async-start(f32[32,1,128]{2,1,0:T(1,128)} %spread.1), calls=%async_computation.1 | async-start | bytes 32768 | tf_op jit(solution)/shard_map/all_to_all | solution.py:452
  59.2 4.7 %collective-permute-start.4 = (f32[24,128]{1,0:T(8,128)S(1)}, f32[24,128]{1,0:T(8,128)S(1)}, u32[]{:S(2)}, u32[]{:S(2)}) collective-permute-start(f32[24,128]{1,0:T(8,128)S(1)} %get-tuple-element.24), channel_id=1, source_target_pairs={{0,8},{16,24},{32,40},{48,56},{64,72},{80,88},{96,104},{112,120},{... | collective-permute-start | bytes 36872 | tf_op jit(solution)/shard_map/ppermute | solution.py:49

commit v7 on v6

v7 whole, which is shorter than its diff:
```python
import jax
import jax.numpy as jnp
from jax import lax
from jax.experimental import pallas as pl
from jax.experimental.pallas import tpu as pltpu
from jax.sharding import PartitionSpec as P

BOTH = ("east", "north")
CE, CN, CZ = 8, 32, 128
SUBS = 16
N_NORTH = 8
PLANE = 32
Z_RUN = 3
COLUMN = Z_RUN * N_NORTH
PATCH_DEV = 8
PER_ROW = CZ // PATCH_DEV
ROWS = PLANE // PER_ROW
VMEM = pl.BlockSpec(memory_space=pltpu.VMEM)
SMEM = pl.BlockSpec(memory_space=pltpu.SMEM)
HBM = pl.BlockSpec(memory_space=pltpu.HBM)
LIMIT = 32 * 1024 * 1024

TILES = CN // 8
E_AHEAD, E_SPEED, E_SUBS = 6, 12, 14 * TILES
E_LEN = E_SUBS + 1
N_AHEAD, N_SPEED, N_SUBS, N_LEN = 48, 96, 112, 120
S_LEN = 8
C_LEN = 24
TOP = 16
LAYERS = CE + 4
NEAR, FAR = 16.0 / 12.0, -1.0 / 12.0


def column_groups():
    return [
        [(run * PLANE + at) * N_NORTH + n for run in range(Z_RUN) for n in range(N_NORTH)]
        for at in range(PLANE)
    ]


def plane_groups():
    return [
        [(run * PLANE + at) * N_NORTH + n for at in range(PLANE)]
        for run in range(Z_RUN)
        for n in range(N_NORTH)
    ]


def swap(block, axis, first):
    pairs = [(i, i + 1) for i in range(first, lax.axis_size(axis) - 1, 2)]
    return lax.ppermute(block, axis, pairs + [(j, i) for i, j in pairs])


def laplace(here, near, far):
    lane = lax.broadcasted_iota(jnp.int32, here.shape, 1)
    near += jnp.where(lane >= 1, pltpu.roll(here, 1, 1), 0.0)
    near += jnp.where(lane < CZ - 1, pltpu.roll(here, CZ - 1, 1), 0.0)
    far += jnp.where(lane >= 2, pltpu.roll(here, 2, 1), 0.0)
    far += jnp.where(lane < CZ - 2, pltpu.roll(here, CZ - 2, 1), 0.0)
    return near * NEAR + far * FAR - here * 7.5


def load_kernel(
    before_far, middle_far, speed_far, mechanism_far, cells_far, cells_row_far, patches_row_far,
    ahead, middle, speed_sq, far, near, low_pair, high_pair,
    before, wide, mechanism, cells, cells_row, patches_row, sems,
):
    copies = [
        (middle_far, middle), (before_far, before), (speed_far, speed_sq), (mechanism_far, mechanism),
        (cells_far, cells), (cells_row_far, cells_row), (patches_row_far, patches_row),
    ]
    started = [pltpu.make_async_copy(a, b, sems.at[i]) for i, (a, b) in enumerate(copies)]
    for copy in started:
        copy.start()
    odd = (lax.axis_index("east") & 1) == 1
    odd_north = (lax.axis_index("north") & 1) == 1
    for copy in started:
        copy.wait()

    def put_east(k, low, high):
        low, high = low.reshape(TILES, 8, CZ), high.reshape(TILES, 8, CZ)
        low_pair[pl.ds(k * TILES, TILES)] = jnp.where(odd, low, high)
        high_pair[pl.ds(k * TILES, TILES)] = jnp.where(odd, high, low)

    def put_north(at, field):
        low, high = field[0:2, :], field[CN - 2 : CN, :]
        near[pl.ds(at, 2), :] = jnp.where(odd_north, low, high)
        far[pl.ds(at, 2), :] = jnp.where(odd_north, high, low)

    def component(c, carry):
        for e in range(CE):
            here = middle[c, e]
            wide[e, 6:8, :] = jnp.zeros((2, CZ), jnp.float32)
            wide[e, 8 : 8 + CN, :] = here
            wide[e, 8 + CN : 10 + CN, :] = jnp.zeros((2, CZ), jnp.float32)

            def rows(offset):
                return wide[e, 8 + offset : 8 + offset + CN, :]

            near_sum, far_sum = rows(-1) + rows(1), rows(-2) + rows(2)
            for k in (e - 1, e + 1):
                near_sum += middle[c, k] if 0 <= k < CE else 0.0
            for k in (e - 2, e + 2):
                far_sum += middle[c, k] if 0 <= k < CE else 0.0
            total = 2.0 * here - before[c, e] + speed_sq[e] * laplace(here, near_sum, far_sum)
            ahead[c, e] = total
            at = pl.multiple_of((c * CE + e) * 2, 2)
            put_north(at, here)
            put_north(pl.multiple_of(N_AHEAD + at, 2), total)
        for k in range(2):
            put_east(c * 2 + k, middle[c, k], middle[c, CE - 2 + k])
            put_east(E_AHEAD + c * 2 + k, ahead[c, k], ahead[c, CE - 2 + k])
        return carry

    lax.fori_loop(0, 3, component, 0)
    for k in range(2):
        put_east(E_SPEED + k, speed_sq[k], speed_sq[CE - 2 + k])
    for e in range(CE):
        put_north(N_SPEED + e * 2, speed_sq[e])
    lane = lax.broadcasted_iota(jnp.int32, (1, CZ), 1)
    speeds = jnp.zeros((1, CZ), jnp.float32)
    for i in range(SUBS):
        cell = cells[i]
        depth = cell & (CZ - 1)
        row = speed_sq[cell >> 12, pl.ds((cell >> 7) & (CN - 1), 1), :]
        speeds += pltpu.roll(jnp.where(lane == depth, row, 0.0), (i - depth) & (CZ - 1), 1)
    near[N_SUBS : N_SUBS + S_LEN, :] = jnp.zeros((S_LEN, CZ), jnp.float32)
    near[N_SUBS : N_SUBS + 1, 0:SUBS] = cells_row[...].astype(jnp.float32)
    near[N_SUBS + 1 : N_SUBS + 2, 0:SUBS] = patches_row[...].astype(jnp.float32)
    near[N_SUBS + 2 : N_SUBS + 5, 0:SUBS] = mechanism[3:6, :] * speeds[:, 0:SUBS]
    subs = near[N_SUBS : N_SUBS + S_LEN, :]
    far[N_SUBS : N_SUBS + S_LEN, :] = subs
    low_pair[E_SUBS] = subs
    high_pair[E_SUBS] = subs


def east_layers(low_pair, high_pair):
    odd = (lax.axis_index("east") & 1) == 1

    def part(message, k, row):
        if row is None:
            return message[pl.ds(k * TILES, TILES)].reshape(CN, CZ)
        return message[k * TILES + row // 8, row % 8 : row % 8 + 1, :]

    def west(k, row=None):
        return jnp.where(odd, part(low_pair, k, row), part(high_pair, k, row))

    def east(k, row=None):
        return jnp.where(odd, part(high_pair, k, row), part(low_pair, k, row))

    return west, east


def north_rows(near_pair, far_pair):
    odd = (lax.axis_index("north") & 1) == 1

    def south(at, count):
        return jnp.where(odd, near_pair[pl.ds(at, count), :], far_pair[pl.ds(at, count), :])

    def north(at, count):
        return jnp.where(odd, far_pair[pl.ds(at, count), :], near_pair[pl.ds(at, count), :])

    return south, north


def put_corners(south, north, low_pair, high_pair):
    odd = (lax.axis_index("east") & 1) == 1
    for c in range(3):
        for k in range(2):
            at = (c * 2 + k) * 4
            low, high = (c * CE + k) * 2, (c * CE + CE - 2 + k) * 2
            for rows, lows, highs in (
                (slice(at, at + 2), south(low, 2), south(high, 2)),
                (slice(at + 2, at + 4), north(low, 2), north(high, 2)),
            ):
                low_pair[rows, :] = jnp.where(odd, lows, highs)
                high_pair[rows, :] = jnp.where(odd, highs, lows)


def steps_kernel(
    ahead, middle, speed_sq, far_pair, near_pair, low_pair, high_pair,
    mechanism_far, cells_far, patches_far, next_out, later, parts, low_corner, high_corner,
    beyond, mechanism, cells, patches, theirs, sub_sems, out_sems,
):
    subs = [
        pltpu.make_async_copy(a, b, sub_sems.at[i])
        for i, (a, b) in enumerate(
            (
                (mechanism_far, mechanism), (cells_far, cells), (patches_far, patches),
                (low_pair.at[E_SUBS], theirs.at[0]),
                (high_pair.at[E_SUBS], theirs.at[1]),
                (near_pair.at[pl.ds(N_SUBS, S_LEN)], theirs.at[2]),
                (far_pair.at[pl.ds(N_SUBS, S_LEN)], theirs.at[3]),
            )
        )
    ]
    for copy in subs:
        copy.start()

    def next_copy(c):
        own = later.at[c, pl.ds(2, CE), pl.ds(TOP, CN)]
        return pltpu.make_async_copy(own, next_out.at[c], out_sems.at[c])


    west, east = east_layers(low_pair, high_pair)
    south, north = north_rows(near_pair, far_pair)
    put_corners(south, north, low_corner, high_corner)
    beyond[...] = jnp.zeros_like(beyond)

    def put_beyond(c):
        def row(layer, at):
            if layer < 0:
                return west(c * 2 + layer + 2, at)
            if layer >= CE:
                return east(c * 2 + layer - CE, at)
            if at < 0:
                return south((c * CE + layer) * 2 + at + 2, 1)
            return north((c * CE + layer) * 2 + at - CN, 1)

        def two(one, other):
            return NEAR * one + FAR * other, FAR * one

        def put(side, e, n, value):
            at = (e if e < 2 else e - 4) * 4 + (n if n < 2 else n - CN + 4)
            beyond[side, c, at : at + 1, :] = value

        for side, e, step in ((0, 0, 1), (1, CE - 1, -1)):
            mine = CE - 1 - e
            for n, inward, halo in ((0, 1, -1), (CN - 1, -1, CN)):
                sums = []
                for layer in (mine, mine - step):
                    near, far = two(row(layer, halo), row(layer, halo - inward))
                    sums.append((speed_sq[layer, n : n + 1, :] * near, speed_sq[layer, n + inward : n + inward + 1, :] * far))
                for j in range(2):
                    for i, value in enumerate(two(sums[0][j], sums[1][j])):
                        put(side, e + i * step, n + j * inward, value)
        for side, n, step in ((2, 0, 1), (3, CN - 1, -1)):
            mine = CN - 1 - n
            for e, inward, halo in ((0, 1, -1), (CE - 1, -1, CE)):
                sums = []
                for at in (mine, mine - step):
                    near, far = two(row(halo, at), row(halo - inward, at))
                    sums.append((speed_sq[e, at : at + 1, :] * near, speed_sq[e + inward, at : at + 1, :] * far))
                for i in range(2):
                    for j, value in enumerate(two(sums[0][i], sums[1][i])):
                        put(side, e + i * inward, n + j * step, value)

    def first(c, carry):
        west_far, west_near = west(c * 2), west(c * 2 + 1)
        east_near, east_far = east(c * 2), east(c * 2 + 1)
        terms = {
            0: NEAR * west_near + FAR * west_far, 1: FAR * west_near,
            CE - 1: NEAR * east_near + FAR * east_far, CE - 2: FAR * east_near,
        }
        for e in range(CE):
            k = e + 2
            new = ahead[c, e]
            if e in terms:
                new += speed_sq[e] * terms[e]
            later[c, k, TOP : TOP + CN, :] = new
            at = (c * CE + e) * 2
            for take, n, step, one, two in ((south, 0, 1, 1, 0), (north, CN - 1, -1, 0, 1)):
                theirs_near, theirs_far = take(at + one, 1), take(at + two, 1)
                mine_near, mine_far = middle[c, e, n : n + 1, :], middle[c, e, n + step : n + step + 1, :]
                for row, extra in ((n, NEAR * theirs_near + FAR * theirs_far), (n + step, FAR * theirs_near)):
                    later[c, k, TOP + row : TOP + row + 1, :] += speed_sq[e, row : row + 1, :] * extra
                for row, part, extra in (
                    (n - step, one, NEAR * mine_near + FAR * mine_far), (n - 2 * step, two, FAR * mine_near)
                ):
                    later[c, k, TOP + row : TOP + row + 1, :] = (
                        take(N_AHEAD + at + part, 1) + take(N_SPEED + e * 2 + part, 1) * extra
                    )
        for k, take, part, extra in (
            (0, west, 0, FAR * middle[c, 0]), (1, west, 1, NEAR * middle[c, 0] + FAR * middle[c, 1]),
            (CE + 2, east, 0, NEAR * middle[c, CE - 1] + FAR * middle[c, CE - 2]),
            (CE + 3, east, 1, FAR * middle[c, CE - 1]),
        ):
            later[c, k, TOP : TOP + CN, :] = take(E_AHEAD + c * 2 + part) + take(E_SPEED + part) * extra
        next_copy(c).start()
        put_beyond(c)
        return carry

    lax.fori_loop(0, 3, first, 0)

    lane = lax.broadcasted_iota(jnp.int32, (1, CZ), 1)
    parts[...] = jnp.zeros_like(parts)

    def add(total, depth, patch):
        run, at = patch >> 11, (patch >> 6) & (PLANE - 1)
        place = (at & (PER_ROW - 1)) * PATCH_DEV + (patch & (PATCH_DEV - 1))
        turned = pltpu.roll(jnp.where(lane == depth, total, 0.0), (place - depth) & (CZ - 1), 1)
        to = run * N_NORTH + ((patch >> 3) & (N_NORTH - 1))
        parts[to, pl.ds(at >> 4, 1), :] += turned

    for copy in subs:
        copy.wait()
    for i in range(SUBS):
        cell, patch = cells[i], patches[i]
        layer, row, depth = cell >> 12, (cell >> 7) & (CN - 1), cell & (CZ - 1)
        total, here, near, far = (jnp.zeros((1, CZ), jnp.float32) for _ in range(4))
        for c in range(3):

            def point(layers=0, rows=0):
                return later[c, layer + 2 + layers, pl.ds(TOP + row + rows, 1), :]

            weight = mechanism[3 + c, i]
            total += mechanism[c, i] * point() - weight * middle[c, layer, pl.ds(row, 1), :]
            here += weight * point()
            near += weight * (point(-1) + point(1) + point(0, -1) + point(0, 1))
            far += weight * (point(-2) + point(2) + point(0, -2) + point(0, 2))
        total += 2.0 * here + speed_sq[layer, pl.ds(row, 1), :] * laplace(here, near, far)
        add(total, depth, patch)

    odd, odd_north = lax.axis_index("east") & 1, lax.axis_index("north") & 1
    sides = odd, 1 - odd, 2 + odd_north, 3 - odd_north

    def neighbours(i, carry):
        for m, side in enumerate(sides):
            cell = theirs[m, 0, i].astype(jnp.int32)
            layer, row, depth = cell >> 12, (cell >> 7) & (CN - 1), cell & (CZ - 1)

            @pl.when(((layer < 2) | (layer >= CE - 2)) & ((row < 2) | (row >= CN - 2)))
            def _():
                at = jnp.where(layer < 2, layer, layer - 4) * 4 + jnp.where(row < 2, row, row - CN + 4)
                total = jnp.zeros((1, CZ), jnp.float32)
                for c in range(3):
                    total += theirs[m, 2 + c, i] * beyond[side, c, pl.ds(at, 1), :]
                add(total, depth, theirs[m, 1, i].astype(jnp.int32))

        return carry

    lax.fori_loop(0, SUBS, neighbours, 0)
    for c in range(3):
        next_copy(c).wait()


def last_kernel(middle, speed_sq, later, out):
    def component(c, carry):
        for e in range(CE):

            def rows(layers, offset=0):
                return later[c, e + 2 + layers, TOP + offset : TOP + offset + CN, :]

            here = rows(0)
            total = laplace(
                here,
                rows(-1) + rows(1) + rows(0, -1) + rows(0, 1),
                rows(-2) + rows(2) + rows(0, -2) + rows(0, 2),
            )
            out[c, e] = 2.0 * here - middle[c, e] + speed_sq[e] * total
        return carry

    lax.fori_loop(0, 3, component, 0)


def corner_kernel(
    last, speed_sq, far_pair, near_pair, low_pair, high_pair, low_corner, high_corner, out
):
    west, east = east_layers(low_pair, high_pair)
    south, north = north_rows(near_pair, far_pair)
    odd = (lax.axis_index("east") & 1) == 1
    low, high = low_corner[...], high_corner[...]
    weight = {1: NEAR, 2: FAR}
    out[...] = last[...]
    for column, corner, e0, e_step in (
        (west, jnp.where(odd, low, high), 0, 1), (east, jnp.where(odd, high, low), CE - 1, -1)
    ):
        for rows, n0, n_step, first in ((south, 0, 1, 0), (north, CN - 1, -1, 2)):
            for e_in in range(2):
                e = e0 + e_in * e_step
                beside = rows(N_SPEED + e * 2, 2)
                for n_in in range(2):
                    n = n0 + n_in * n_step
                    for c in range(3):
                        total = jnp.zeros((1, CZ), jnp.float32)
                        for i in range(1, 3 - e_in):
                            k = 2 - i if e0 == 0 else i - 1
                            for j in range(1, 3 - n_in):
                                r = 2 - j if n0 == 0 else j - 1
                                at = (c * 2 + k) * 4 + first + r
                                speeds = column(E_SPEED + k, n) + beside[r : r + 1, :]
                                total += (weight[e_in + i] * weight[n_in + j]) * corner[at : at + 1, :] * speeds
                        out[c, e, n : n + 1, :] += speed_sq[e, n : n + 1, :] * total


def spread_kernel(parts, _, out):
    total = jnp.sum(parts[...], axis=0)
    for row in range(ROWS):
        out[row * PER_ROW : (row + 1) * PER_ROW] = jnp.broadcast_to(
            total[row : row + 1][None], (PER_ROW, 1, CZ)
        )


def own_kernel(parts, out):
    total = jnp.sum(parts[...], axis=0)
    at = lax.axis_index("east") & (PER_ROW - 1)
    turned = pltpu.roll(total, (CZ - at * PATCH_DEV) & (CZ - 1), 1)
    out[...] = turned[:, 0:PATCH_DEV]


def body(field_prev, field_now, speed_sq, mechanism, sub_cells, sub_patch):
    params = pltpu.CompilerParams(vmem_limit_bytes=LIMIT)
    f32 = jnp.float32
    field = pltpu.VMEM((3, CE, CN, CZ), f32)
    held = field, field, pltpu.VMEM((CE, CN, CZ), f32)
    east_message, north_message = pltpu.VMEM((E_LEN, 8, CZ), f32), pltpu.VMEM((N_LEN, CZ), f32)
    inputs = [
        pltpu.with_memory_space_constraint(x, pltpu.HBM)
        for x in (
            field_prev, field_now, speed_sq, mechanism, sub_cells,
            sub_cells.reshape(1, SUBS), sub_patch.reshape(1, SUBS), sub_patch,
        )
    ]
    i32 = jnp.int32
    ahead, field_now, speed_sq, far, near, low_pair, high_pair = pl.pallas_call(
        load_kernel, out_shape=[*held] + [north_message] * 2 + [east_message] * 2,
        in_specs=[HBM] * 7, out_specs=[VMEM] * 7,
        scratch_shapes=[
            field, pltpu.VMEM((CE, CN + 16, CZ), f32), pltpu.VMEM((6, SUBS), f32), pltpu.SMEM((SUBS,), i32),
            pltpu.VMEM((1, SUBS), i32), pltpu.VMEM((1, SUBS), i32), pltpu.SemaphoreType.DMA((7,)),
        ],
        compiler_params=params, name="load",
    )(*inputs[:7])
    far_pair = swap(far, "north", 1)
    near_pair = swap(near, "north", 0)
    halos = far_pair, near_pair, swap(low_pair, "east", 0), swap(high_pair, "east", 1)
    later = pltpu.VMEM((3, LAYERS, CN + 2 * TOP, CZ), f32)
    parts = pltpu.VMEM((COLUMN, ROWS, CZ), f32)
    corner = pltpu.VMEM((C_LEN, CZ), f32)
    field_next, later, parts, low_corner, high_corner = pl.pallas_call(
        steps_kernel,
        out_shape=[pltpu.HBM((3, CE, CN, CZ), f32), later, parts, corner, corner],
        in_specs=[VMEM] * 7 + [HBM] * 3, out_specs=[HBM] + [VMEM] * 4,
        scratch_shapes=[
            pltpu.VMEM((4, 3, 16, CZ), f32),
            pltpu.SMEM((6, SUBS), f32), pltpu.SMEM((SUBS,), i32), pltpu.SMEM((SUBS,), i32),
            pltpu.SMEM((4, S_LEN, CZ), f32),
            pltpu.SemaphoreType.DMA((7,)), pltpu.SemaphoreType.DMA((3,)),
        ],
        compiler_params=params, name="steps",
    )(ahead, field_now, speed_sq, *halos, inputs[3], inputs[4], inputs[7])
    corners = swap(low_corner, "east", 0), swap(high_corner, "east", 1)
    field_last = pl.pallas_call(
        last_kernel, out_shape=pltpu.VMEM((3, CE, CN, CZ), f32), in_specs=[VMEM] * 3, out_specs=VMEM,
        compiler_params=params, name="last",
        cost_estimate=pl.CostEstimate(flops=3_000_000, bytes_accessed=1_000_000, transcendentals=0),
    )(field_now, speed_sq, later)
    parts = lax.all_to_all(parts, BOTH, 0, 0, tiled=True, axis_index_groups=column_groups())
    parts = pl.pallas_call(
        spread_kernel, out_shape=pltpu.VMEM((PLANE, 1, CZ), f32),
        in_specs=[VMEM] * 2, out_specs=VMEM, compiler_params=params, name="spread",
    )(parts, corners[1])
    parts = lax.all_to_all(parts, BOTH, 0, 0, tiled=True, axis_index_groups=plane_groups())
    own = pl.pallas_call(
        own_kernel, out_shape=jax.ShapeDtypeStruct((1, PATCH_DEV), f32),
        in_specs=[VMEM], out_specs=VMEM, compiler_params=params, name="own",
    )(parts)
    field_last = pl.pallas_call(
        corner_kernel, out_shape=jax.ShapeDtypeStruct((3, CE, CN, CZ), f32), in_specs=[VMEM] * 8,
        out_specs=VMEM, compiler_params=params, name="corners",
    )(field_last, speed_sq, *halos, *corners)
    return field_next, field_last, own.reshape(PATCH_DEV)


def solution(mesh):
    in_specs = (
        P(None, "east", "north", None),
        P(None, "east", "north", None),
        P("east", "north", None),
        P(None, BOTH),
        P(BOTH),
        P(BOTH),
    )
    out_specs = (
        P(None, "east", "north", None),
        P(None, "east", "north", None),
        P(BOTH),
    )
    return jax.shard_map(body, mesh=mesh, in_specs=in_specs, out_specs=out_specs, check_vma=False)
```

time: 68.7 us -> 66.5 us (0.968)
  starting transfers between devices: 45.9 us -> 43.6 us
    all_to_all x1, starting transfers between devices: 21.9 us -> 18.7 us  [body(): lax.all_to_all(parts, BOTH, 0, 0, tiled=True, axis_index_groups=column_gr...]
    all_to_all x1, starting transfers between devices: 4.54 us -> 5.34 us  [body(): lax.all_to_all(parts, BOTH, 0, 0, tiled=True, axis_index_groups=plane_gro...]
where the time goes in v7:
time: 66.5 us; the launch traced here: 66.1 us
  starting transfers between devices  43.6 us (66%)
  waiting for transfers between devices  13.8 us (21%)
  Pallas kernels  7.98 us (12%)
  between operations  0.74 us (1%)
    ppermute x6, starting transfers between devices, swap(): return lax.ppermute(block, axis, pairs + [(j, i) for i, j in pairs])  19.5 us
    all_to_all x1, starting transfers between devices, body(): lax.all_to_all(parts, BOTH, 0, 0, tiled=True, axis_index_groups=column_gr...  18.7 us
    all_to_all x1, waiting for transfers between devices, body(): lax.all_to_all(parts, BOTH, 0, 0, tiled=True, axis_index_groups=column_gr...  8.97 us
    all_to_all x1, starting transfers between devices, body(): lax.all_to_all(parts, BOTH, 0, 0, tiled=True, axis_index_groups=plane_gro...  5.34 us
    pallas_call x1, Pallas kernels, body(): pl.pallas_call(steps_kernel, out_shape=[pltpu.HBM((3, CE, CN, CZ), f32),...  3.29 us
    all_to_all x1, waiting for transfers between devices, body(): lax.all_to_all(parts, BOTH, 0, 0, tiled=True, axis_index_groups=plane_gro...  2.99 us
    pallas_call x1, Pallas kernels, body(): pl.pallas_call(load_kernel, out_shape=[*held] + [north_message] * 2 + [ea...  1.96 us
    ppermute x6, waiting for transfers between devices, swap(): return lax.ppermute(block, axis, pairs + [(j, i) for i, j in pairs])  1.84 us
  transfers between devices with their start and end apart: 8, of which 4 were waited for; matrix products, arithmetic and copies ran while one was open for 0% of the time, Pallas kernels for 2%

profile of v7, /device:TPU:1, one launch (start us, length us, event | category | flops | bytes accessed | tf_op | source)
XLA Modules:
  0.0 66.1 jit_solution(17937941920511153571)
XLA Ops:
  0.6 2.0 %load.1 = (f32[3,8,32,128]{3,2,1,0:T(8,128)S(1)}, f32[3,8,32,128]{3,2,1,0:T(8,128)S(1)}, f32[8,32,128]{2,1,0:T(8,128)S(1)}, f32[120,128]{1,0:T(8,128)S(1)}, f32[...) custom-call(f32[3,8,32,128]{3,2,1,0:T(8,128)} %before_far.1, ...), custom_call_target="tpu_custom_call" | custom-call | tf_op jit(solution)/shard_map/load/pallas_call | solution.py:415
  2.6 3.9 %collective-permute-start.2 = (f32[57,8,128]{2,1,0:T(8,128)S(1)}, f32[57,8,128]{2,1,0:T(8,128)S(1)}, u32[]{:S(2)}, u32[]{:S(2)}) collective-permute-start(f32[57,8,128]{2,1,0:T(8,128)S(1)} %get-tuple-element.20), channel_id=1, source_target_pairs={{0,8},{16,24},{32,40},{48,56},{64,72},{80,88},{96,104},{112,120},{... | collective-permute-start | bytes 700424 | tf_op jit(solution)/shard_map/ppermute | solution.py:51
  6.6 0.7 %collective-permute-start.3 = (f32[57,8,128]{2,1,0:T(8,128)S(1)}, f32[57,8,128]{2,1,0:T(8,128)S(1)}, u32[]{:S(2)}, u32[]{:S(2)}) collective-permute-start(f32[57,8,128]{2,1,0:T(8,128)S(1)} %get-tuple-element.21), channel_id=1, source_target_pairs={{8,16},{24,32},{40,48},{56,64},{72,80},{88,96},{104,112},{120,128}... | collective-permute-start | bytes 700424 | tf_op jit(solution)/shard_map/ppermute | solution.py:51
  7.2 8.5 %collective-permute-start = (f32[120,128]{1,0:T(8,128)S(1)}, f32[120,128]{1,0:T(8,128)S(1)}, u32[]{:S(2)}, u32[]{:S(2)}) collective-permute-start(f32[120,128]{1,0:T(8,128)S(1)} %get-tuple-element.18), channel_id=1, source_target_pairs={{1,2},{3,4},{5,6},{2,1},{4,3},{6,5},{9,10},{11,12},{13,14},{10,9},... | collective-permute-start | bytes 184328 | tf_op jit(solution)/shard_map/ppermute | solution.py:51
  15.7 2.6 %collective-permute-start.1 = (f32[120,128]{1,0:T(8,128)S(1)}, f32[120,128]{1,0:T(8,128)S(1)}, u32[]{:S(2)}, u32[]{:S(2)}) collective-permute-start(f32[120,128]{1,0:T(8,128)S(1)} %get-tuple-element.19), channel_id=1, source_target_pairs={{0,1},{2,3},{4,5},{6,7},{1,0},{3,2},{5,4},{7,6},{8,9},{10,11},{12,... | collective-permute-start | bytes 184328 | tf_op jit(solution)/shard_map/ppermute | solution.py:51
  18.3 0.0 collective-permute-done.far_pair
  18.3 0.9 %collective-permute-done.1.near_pair = f32[120,128]{1,0:T(8,128)S(1)} collective-permute-done((f32[120,128]{1,0:T(8,128)S(1)}, f32[120,128]{1,0:T(8,128)S(1)}, u32[]{:S(2)}, u32[]{:S(2)}) %collective-permute-start.1) | collective-permute-done | bytes 61472 | tf_op jit(solution)/shard_map/ppermute | solution.py:51
  19.2 0.0 collective-permute-done.2.low_pair
  19.2 0.0 collective-permute-done.3.high_pair
  19.2 3.3 %steps.1 = (f32[3,8,32,128]{3,2,1,0:T(8,128)}, f32[3,12,64,128]{3,2,1,0:T(8,128)S(1)}, f32[24,2,128]{2,1,0:T(2,128)}, f32[24,128]{1,0:T(8,128)S(1)}, f32[24,128]{1,0:T(8,128)S(1)}) custom-call(f32[3,8,32,128]{3,2,1,0:T(8,128)S(1)} %get-tuple-element.15.ahead, f32[3,8,32,128]{3,2,1,0:T(8,128)S(1)} %get-tuple-element.16.middle, ...), custom_call_target="tpu_custom_call" | custom-call | tf_op jit(solution)/shard_map/steps/pallas_call | solution.py:430
  22.5 18.7 %all-to-all-start = ((f32[24,2,128]{2,1,0:T(2,128)}), f32[24,2,128]{2,1,0:T(2,128)S(1)}, u32[]{:S(2)}, u32[]{:S(2)}) async-start(f32[24,2,128]{2,1,0:T(2,128)} %get-tuple-element.26), calls=%async_computation | async-start | bytes 49152 | tf_op jit(solution)/shard_map/all_to_all | solution.py:448
  41.3 0.7 %collective-permute-start.5 = (f32[24,128]{1,0:T(8,128)S(1)}, f32[24,128]{1,0:T(8,128)S(1)}, u32[]{:S(2)}, u32[]{:S(2)}) collective-permute-start(f32[24,128]{1,0:T(8,128)S(1)} %get-tuple-element.25), channel_id=1, source_target_pairs={{8,16},{24,32},{40,48},{56,64},{72,80},{88,96},{104,112},{120,128}... | collective-permute-start | bytes 36872 | tf_op jit(solution)/shard_map/ppermute | solution.py:51
  41.9 0.0 collective-permute-done.5.high_corner._
  41.9 9.0 %all-to-all-done.parts = f32[24,2,128]{2,1,0:T(2,128)S(1)} async-done(((f32[24,2,128]{2,1,0:T(2,128)}), f32[24,2,128]{2,1,0:T(2,128)S(1)}, u32[]{:S(2)}, u32[]{:S(2)}) %all-to-all-start) | async-done | bytes 24608 | tf_op jit(solution)/shard_map/all_to_all | solution.py:448
  50.9 0.6 spread.1
  51.5 5.3 %all-to-all-start.1 = ((f32[32,1,128]{2,1,0:T(1,128)}), f32[32,1,128]{2,1,0:T(1,128)S(1)}, u32[]{:S(2)}, u32[]{:S(2)}) async-start(f32[32,1,128]{2,1,0:T(1,128)} %spread.1), calls=%async_computation.1 | async-start | bytes 32768 | tf_op jit(solution)/shard_map/all_to_all | solution.py:453
  56.9 3.1 %collective-permute-start.4 = (f32[24,128]{1,0:T(8,128)S(1)}, f32[24,128]{1,0:T(8,128)S(1)}, u32[]{:S(2)}, u32[]{:S(2)}) collective-permute-start(f32[24,128]{1,0:T(8,128)S(1)} %get-tuple-element.24), channel_id=1, source_target_pairs={{0,8},{16,24},{32,40},{48,56},{64,72},{80,88},{96,104},{112,120},{... | collective-permute-start | bytes 36872 | tf_op jit(solution)/shard_map/ppermute | solution.py:51
  60.0 0.6 last.1
  60.7 1.0 %collective-permute-done.4.low_corner = f32[24,128]{1,0:T(8,128)S(1)} collective-permute-done((f32[24,128]{1,0:T(8,128)S(1)}, f32[24,128]{1,0:T(8,128)S(1)}, u32[]{:S(2)}, u32[]{:S(2)}) %collective-permute-start.4) | collective-permute-done | bytes 12320 | tf_op jit(solution)/shard_map/ppermute | solution.py:51
  61.6 0.8 %corners.1 = f32[3,8,32,128]{3,2,1,0:T(8,128)} custom-call(f32[3,8,32,128]{3,2,1,0:T(8,128)S(1)} %last.1, f32[8,32,128]{2,1,0:T(8,128)S(1)} %get-tuple-element.17.speed_sq, f32[120,128]{1,0:T(8,128)S(1)} %collective-permute-done.far_pair, f32[120,128]{1,0:T(8,128)S(1)} %collective-permute-done.1.near_pair, ...), custom_call_target="tpu_custom_call" | custom-call | tf_op jit(solution)/shard_map/corners/pallas_call | solution.py:458
  62.5 3.0 %all-to-all-done.1.parts = f32[32,1,128]{2,1,0:T(1,128)S(1)} async-done(((f32[32,1,128]{2,1,0:T(1,128)}), f32[32,1,128]{2,1,0:T(1,128)S(1)}, u32[]{:S(2)}, u32[]{:S(2)}) %all-to-all-start.1) | async-done | bytes 16416 | tf_op jit(solution)/shard_map/all_to_all | solution.py:453
  65.5 0.6 own.1
Async XLA Ops:
  2.6 16.6 %collective-permute-start.2 = (f32[57,8,128]{2,1,0:T(8,128)S(1)}, f32[57,8,128]{2,1,0:T(8,128)S(1)}, u32[]{:S(2)}, u32[]{:S(2)}) collective-permute-start(f32[57,8,128]{2,1,0:T(8,128)S(1)} %get-tuple-element.20), channel_id=1, source_target_pairs={{0,8},{16,24},{32,40},{48,56},{64,72},{80,88},{96,104},{112,120},{... | collective-permute-start | bytes 700424 | tf_op jit(solution)/shard_map/ppermute | solution.py:51
  6.6 12.6 %collective-permute-start.3 = (f32[57,8,128]{2,1,0:T(8,128)S(1)}, f32[57,8,128]{2,1,0:T(8,128)S(1)}, u32[]{:S(2)}, u32[]{:S(2)}) collective-permute-start(f32[57,8,128]{2,1,0:T(8,128)S(1)} %get-tuple-element.21), channel_id=1, source_target_pairs={{8,16},{24,32},{40,48},{56,64},{72,80},{88,96},{104,112},{120,128}... | collective-permute-start | bytes 700424 | tf_op jit(solution)/shard_map/ppermute | solution.py:51
  7.2 11.1 %collective-permute-start = (f32[120,128]{1,0:T(8,128)S(1)}, f32[120,128]{1,0:T(8,128)S(1)}, u32[]{:S(2)}, u32[]{:S(2)}) collective-permute-start(f32[120,128]{1,0:T(8,128)S(1)} %get-tuple-element.18), channel_id=1, source_target_pairs={{1,2},{3,4},{5,6},{2,1},{4,3},{6,5},{9,10},{11,12},{13,14},{10,9},... | collective-permute-start | bytes 184328 | tf_op jit(solution)/shard_map/ppermute | solution.py:51
  15.7 3.5 %collective-permute-start.1 = (f32[120,128]{1,0:T(8,128)S(1)}, f32[120,128]{1,0:T(8,128)S(1)}, u32[]{:S(2)}, u32[]{:S(2)}) collective-permute-start(f32[120,128]{1,0:T(8,128)S(1)} %get-tuple-element.19), channel_id=1, source_target_pairs={{0,1},{2,3},{4,5},{6,7},{1,0},{3,2},{5,4},{7,6},{8,9},{10,11},{12,... | collective-permute-start | bytes 184328 | tf_op jit(solution)/shard_map/ppermute | solution.py:51
  22.5 28.4 %all-to-all-start = ((f32[24,2,128]{2,1,0:T(2,128)}), f32[24,2,128]{2,1,0:T(2,128)S(1)}, u32[]{:S(2)}, u32[]{:S(2)}) async-start(f32[24,2,128]{2,1,0:T(2,128)} %get-tuple-element.26), calls=%async_computation | async-start | bytes 49152 | tf_op jit(solution)/shard_map/all_to_all | solution.py:448
  41.3 0.7 %collective-permute-start.5 = (f32[24,128]{1,0:T(8,128)S(1)}, f32[24,128]{1,0:T(8,128)S(1)}, u32[]{:S(2)}, u32[]{:S(2)}) collective-permute-start(f32[24,128]{1,0:T(8,128)S(1)} %get-tuple-element.25), channel_id=1, source_target_pairs={{8,16},{24,32},{40,48},{56,64},{72,80},{88,96},{104,112},{120,128}... | collective-permute-start | bytes 36872 | tf_op jit(solution)/shard_map/ppermute | solution.py:51
  51.5 13.9 %all-to-all-start.1 = ((f32[32,1,128]{2,1,0:T(1,128)}), f32[32,1,128]{2,1,0:T(1,128)S(1)}, u32[]{:S(2)}, u32[]{:S(2)}) async-start(f32[32,1,128]{2,1,0:T(1,128)} %spread.1), calls=%async_computation.1 | async-start | bytes 32768 | tf_op jit(solution)/shard_map/all_to_all | solution.py:453
  56.9 4.7 %collective-permute-start.4 = (f32[24,128]{1,0:T(8,128)S(1)}, f32[24,128]{1,0:T(8,128)S(1)}, u32[]{:S(2)}, u32[]{:S(2)}) collective-permute-start(f32[24,128]{1,0:T(8,128)S(1)} %get-tuple-element.24), channel_id=1, source_target_pairs={{0,8},{16,24},{32,40},{48,56},{64,72},{80,88},{96,104},{112,120},{... | collective-permute-start | bytes 36872 | tf_op jit(solution)/shard_map/ppermute | solution.py:51

commit v8 on v7

--- a/solution.py
+++ b/solution.py
@@ -180,7 +180,7 @@
 def steps_kernel(
     ahead, middle, speed_sq, far_pair, near_pair, low_pair, high_pair,
     mechanism_far, cells_far, patches_far, next_out, later, parts, low_corner, high_corner,
-    beyond, mechanism, cells, patches, theirs, sub_sems, out_sems,
+    beyond, mechanism, cells, patches, theirs, code_rows, codes, sub_sems, out_sems,
 ):
     subs = [
         pltpu.make_async_copy(a, b, sub_sems.at[i])
@@ -196,6 +196,15 @@
     ]
     for copy in subs:
         copy.start()
+    for m, block in enumerate((low_pair[E_SUBS], high_pair[E_SUBS], near_pair[N_SUBS:N_LEN, :], far_pair[N_SUBS:N_LEN, :])):
+        cell = block[0:1].astype(jnp.int32)
+        layer, row = cell >> 12, (cell >> 7) & (CN - 1)
+        corner = ((layer < 2) | (layer >= CE - 2)) & ((row < 2) | (row >= CN - 2))
+        at = jnp.where(layer < 2, layer, layer - CE + 4) * 4 + jnp.where(row < 2, row, row - CN + 4)
+        code_rows[2 * m : 2 * m + 1, :] = jnp.where(corner, at * CZ + (cell & (CZ - 1)), -1)
+        code_rows[2 * m + 1 : 2 * m + 2, :] = block[1:2].astype(jnp.int32)
+    coded = pltpu.make_async_copy(code_rows, codes, sub_sems.at[7])
+    coded.start()
 
     def next_copy(c):
         own = later.at[c, pl.ds(2, CE), pl.ds(TOP, CN)]
@@ -245,6 +254,12 @@
                     for j, value in enumerate(two(sums[0][i], sums[1][i])):
                         put(side, e + i * inward, n + j * step, value)
 
+    row_of_two = lax.broadcasted_iota(jnp.int32, (2, CZ), 0)
+    first_row, second_row = (jnp.where(row_of_two == r, NEAR, 0.0) for r in range(2))
+
+    def two_rows(block, mask):
+        return FAR * block + mask * jnp.concatenate([block[1:2], block[0:1]], axis=0)
+
     def first(c, carry):
         west_far, west_near = west(c * 2), west(c * 2 + 1)
         east_near, east_far = east(c * 2), east(c * 2 + 1)
@@ -259,17 +274,14 @@
                 new += speed_sq[e] * terms[e]
             later[c, k, TOP : TOP + CN, :] = new
             at = (c * CE + e) * 2
-            for take, n, step, one, two in ((south, 0, 1, 1, 0), (north, CN - 1, -1, 0, 1)):
-                theirs_near, theirs_far = take(at + one, 1), take(at + two, 1)
-                mine_near, mine_far = middle[c, e, n : n + 1, :], middle[c, e, n + step : n + step + 1, :]
-                for row, extra in ((n, NEAR * theirs_near + FAR * theirs_far), (n + step, FAR * theirs_near)):
-                    later[c, k, TOP + row : TOP + row + 1, :] += speed_sq[e, row : row + 1, :] * extra
-                for row, part, extra in (
-                    (n - step, one, NEAR * mine_near + FAR * mine_far), (n - 2 * step, two, FAR * mine_near)
-                ):
-                    later[c, k, TOP + row : TOP + row + 1, :] = (
-                        take(N_AHEAD + at + part, 1) + take(N_SPEED + e * 2 + part, 1) * extra
-                    )
+            for take, n, outside, own_mask, halo_mask in (
+                (south, 0, -2, first_row, second_row), (north, CN - 2, CN, second_row, first_row)
+            ):
+                inside = slice(TOP + n, TOP + n + 2)
+                later[c, k, inside, :] += speed_sq[e, n : n + 2, :] * two_rows(take(at, 2), own_mask)
+                later[c, k, TOP + outside : TOP + outside + 2, :] = take(N_AHEAD + at, 2) + take(
+                    N_SPEED + e * 2, 2
+                ) * two_rows(middle[c, e, n : n + 2, :], halo_mask)
         for k, take, part, extra in (
             (0, west, 0, FAR * middle[c, 0]), (1, west, 1, NEAR * middle[c, 0] + FAR * middle[c, 1]),
             (CE + 2, east, 0, NEAR * middle[c, CE - 1] + FAR * middle[c, CE - 2]),
@@ -316,19 +328,19 @@
 
     def neighbours(i, carry):
         for m, side in enumerate(sides):
-            cell = theirs[m, 0, i].astype(jnp.int32)
-            layer, row, depth = cell >> 12, (cell >> 7) & (CN - 1), cell & (CZ - 1)
-
-            @pl.when(((layer < 2) | (layer >= CE - 2)) & ((row < 2) | (row >= CN - 2)))
+            code = codes[2 * m, i]
+
+            @pl.when(code >= 0)
             def _():
-                at = jnp.where(layer < 2, layer, layer - 4) * 4 + jnp.where(row < 2, row, row - CN + 4)
+                at, depth = code >> 7, code & (CZ - 1)
                 total = jnp.zeros((1, CZ), jnp.float32)
                 for c in range(3):
                     total += theirs[m, 2 + c, i] * beyond[side, c, pl.ds(at, 1), :]
-                add(total, depth, theirs[m, 1, i].astype(jnp.int32))
+                add(total, depth, codes[2 * m + 1, i])
 
         return carry
 
+    coded.wait()
     lax.fori_loop(0, SUBS, neighbours, 0)
     for c in range(3):
         next_copy(c).wait()
@@ -434,8 +446,8 @@
         scratch_shapes=[
             pltpu.VMEM((4, 3, 16, CZ), f32),
             pltpu.SMEM((6, SUBS), f32), pltpu.SMEM((SUBS,), i32), pltpu.SMEM((SUBS,), i32),
-            pltpu.SMEM((4, S_LEN, CZ), f32),
-            pltpu.SemaphoreType.DMA((7,)), pltpu.SemaphoreType.DMA((3,)),
+            pltpu.SMEM((4, S_LEN, CZ), f32), pltpu.VMEM((8, CZ), i32), pltpu.SMEM((8, CZ), i32),
+            pltpu.SemaphoreType.DMA((8,)), pltpu.SemaphoreType.DMA((3,)),
         ],
         compiler_params=params, name="steps",
     )(ahead, field_now, speed_sq, *halos, inputs[3], inputs[4], inputs[7])

time: 66.5 us -> 66.2 us (level)
  no operation moved by 1% of the time
where the time goes in v8:
time: 66.2 us; the launch traced here: 65.8 us
  starting transfers between devices  43.2 us (65%)
  waiting for transfers between devices  13.8 us (21%)
  Pallas kernels  8.03 us (12%)
  between operations  0.74 us (1%)
    ppermute x6, starting transfers between devices, swap(): return lax.ppermute(block, axis, pairs + [(j, i) for i, j in pairs])  19.5 us
    all_to_all x1, starting transfers between devices, body(): lax.all_to_all(parts, BOTH, 0, 0, tiled=True, axis_index_groups=column_gr...  18.4 us
    all_to_all x1, waiting for transfers between devices, body(): lax.all_to_all(parts, BOTH, 0, 0, tiled=True, axis_index_groups=column_gr...  8.97 us
    all_to_all x1, starting transfers between devices, body(): lax.all_to_all(parts, BOTH, 0, 0, tiled=True, axis_index_groups=plane_gro...  5.35 us
    pallas_call x1, Pallas kernels, body(): pl.pallas_call(steps_kernel, out_shape=[pltpu.HBM((3, CE, CN, CZ), f32),...  3.35 us
    all_to_all x1, waiting for transfers between devices, body(): lax.all_to_all(parts, BOTH, 0, 0, tiled=True, axis_index_groups=plane_gro...  2.99 us
    pallas_call x1, Pallas kernels, body(): pl.pallas_call(load_kernel, out_shape=[*held] + [north_message] * 2 + [ea...  1.96 us
    ppermute x6, waiting for transfers between devices, swap(): return lax.ppermute(block, axis, pairs + [(j, i) for i, j in pairs])  1.84 us
  transfers between devices with their start and end apart: 8, of which 4 were waited for; matrix products, arithmetic and copies ran while one was open for 0% of the time, Pallas kernels for 2%

profile of v8, /device:TPU:1, one launch (start us, length us, event | category | flops | bytes accessed | tf_op | source)
XLA Modules:
  0.0 65.8 jit_solution(9360572026544506714)
XLA Ops:
  0.6 2.0 %load.1 = (f32[3,8,32,128]{3,2,1,0:T(8,128)S(1)}, f32[3,8,32,128]{3,2,1,0:T(8,128)S(1)}, f32[8,32,128]{2,1,0:T(8,128)S(1)}, f32[120,128]{1,0:T(8,128)S(1)}, f32[...) custom-call(f32[3,8,32,128]{3,2,1,0:T(8,128)} %before_far.1, ...), custom_call_target="tpu_custom_call" | custom-call | tf_op jit(solution)/shard_map/load/pallas_call | solution.py:427
  2.6 3.9 %collective-permute-start.2 = (f32[57,8,128]{2,1,0:T(8,128)S(1)}, f32[57,8,128]{2,1,0:T(8,128)S(1)}, u32[]{:S(2)}, u32[]{:S(2)}) collective-permute-start(f32[57,8,128]{2,1,0:T(8,128)S(1)} %get-tuple-element.20), channel_id=1, source_target_pairs={{0,8},{16,24},{32,40},{48,56},{64,72},{80,88},{96,104},{112,120},{... | collective-permute-start | bytes 700424 | tf_op jit(solution)/shard_map/ppermute | solution.py:51
  6.6 0.7 %collective-permute-start.3 = (f32[57,8,128]{2,1,0:T(8,128)S(1)}, f32[57,8,128]{2,1,0:T(8,128)S(1)}, u32[]{:S(2)}, u32[]{:S(2)}) collective-permute-start(f32[57,8,128]{2,1,0:T(8,128)S(1)} %get-tuple-element.21), channel_id=1, source_target_pairs={{8,16},{24,32},{40,48},{56,64},{72,80},{88,96},{104,112},{120,128}... | collective-permute-start | bytes 700424 | tf_op jit(solution)/shard_map/ppermute | solution.py:51
  7.2 8.5 %collective-permute-start = (f32[120,128]{1,0:T(8,128)S(1)}, f32[120,128]{1,0:T(8,128)S(1)}, u32[]{:S(2)}, u32[]{:S(2)}) collective-permute-start(f32[120,128]{1,0:T(8,128)S(1)} %get-tuple-element.18), channel_id=1, source_target_pairs={{1,2},{3,4},{5,6},{2,1},{4,3},{6,5},{9,10},{11,12},{13,14},{10,9},... | collective-permute-start | bytes 184328 | tf_op jit(solution)/shard_map/ppermute | solution.py:51
  15.7 2.6 %collective-permute-start.1 = (f32[120,128]{1,0:T(8,128)S(1)}, f32[120,128]{1,0:T(8,128)S(1)}, u32[]{:S(2)}, u32[]{:S(2)}) collective-permute-start(f32[120,128]{1,0:T(8,128)S(1)} %get-tuple-element.19), channel_id=1, source_target_pairs={{0,1},{2,3},{4,5},{6,7},{1,0},{3,2},{5,4},{7,6},{8,9},{10,11},{12,... | collective-permute-start | bytes 184328 | tf_op jit(solution)/shard_map/ppermute | solution.py:51
  18.3 0.0 collective-permute-done.far_pair
  18.3 0.9 %collective-permute-done.1.near_pair = f32[120,128]{1,0:T(8,128)S(1)} collective-permute-done((f32[120,128]{1,0:T(8,128)S(1)}, f32[120,128]{1,0:T(8,128)S(1)}, u32[]{:S(2)}, u32[]{:S(2)}) %collective-permute-start.1) | collective-permute-done | bytes 61472 | tf_op jit(solution)/shard_map/ppermute | solution.py:51
  19.2 0.0 collective-permute-done.2.low_pair
  19.2 0.0 collective-permute-done.3.high_pair
  19.2 3.3 %steps.1 = (f32[3,8,32,128]{3,2,1,0:T(8,128)}, f32[3,12,64,128]{3,2,1,0:T(8,128)S(1)}, f32[24,2,128]{2,1,0:T(2,128)}, f32[24,128]{1,0:T(8,128)S(1)}, f32[24,128]{1,0:T(8,128)S(1)}) custom-call(f32[3,8,32,128]{3,2,1,0:T(8,128)S(1)} %get-tuple-element.15.ahead, f32[3,8,32,128]{3,2,1,0:T(8,128)S(1)} %get-tuple-element.16.middle, ...), custom_call_target="tpu_custom_call" | custom-call | tf_op jit(solution)/shard_map/steps/pallas_call | solution.py:442
  22.6 18.4 %all-to-all-start = ((f32[24,2,128]{2,1,0:T(2,128)}), f32[24,2,128]{2,1,0:T(2,128)S(1)}, u32[]{:S(2)}, u32[]{:S(2)}) async-start(f32[24,2,128]{2,1,0:T(2,128)} %get-tuple-element.26), calls=%async_computation | async-start | bytes 49152 | tf_op jit(solution)/shard_map/all_to_all | solution.py:460
  40.9 0.7 %collective-permute-start.5 = (f32[24,128]{1,0:T(8,128)S(1)}, f32[24,128]{1,0:T(8,128)S(1)}, u32[]{:S(2)}, u32[]{:S(2)}) collective-permute-start(f32[24,128]{1,0:T(8,128)S(1)} %get-tuple-element.25), channel_id=1, source_target_pairs={{8,16},{24,32},{40,48},{56,64},{72,80},{88,96},{104,112},{120,128}... | collective-permute-start | bytes 36872 | tf_op jit(solution)/shard_map/ppermute | solution.py:51
  41.6 0.0 collective-permute-done.5.high_corner._
  41.6 9.0 %all-to-all-done.parts = f32[24,2,128]{2,1,0:T(2,128)S(1)} async-done(((f32[24,2,128]{2,1,0:T(2,128)}), f32[24,2,128]{2,1,0:T(2,128)S(1)}, u32[]{:S(2)}, u32[]{:S(2)}) %all-to-all-start) | async-done | bytes 24608 | tf_op jit(solution)/shard_map/all_to_all | solution.py:460
  50.6 0.6 spread.1
  51.2 5.3 %all-to-all-start.1 = ((f32[32,1,128]{2,1,0:T(1,128)}), f32[32,1,128]{2,1,0:T(1,128)S(1)}, u32[]{:S(2)}, u32[]{:S(2)}) async-start(f32[32,1,128]{2,1,0:T(1,128)} %spread.1), calls=%async_computation.1 | async-start | bytes 32768 | tf_op jit(solution)/shard_map/all_to_all | solution.py:465
  56.6 3.1 %collective-permute-start.4 = (f32[24,128]{1,0:T(8,128)S(1)}, f32[24,128]{1,0:T(8,128)S(1)}, u32[]{:S(2)}, u32[]{:S(2)}) collective-permute-start(f32[24,128]{1,0:T(8,128)S(1)} %get-tuple-element.24), channel_id=1, source_target_pairs={{0,8},{16,24},{32,40},{48,56},{64,72},{80,88},{96,104},{112,120},{... | collective-permute-start | bytes 36872 | tf_op jit(solution)/shard_map/ppermute | solution.py:51
  59.7 0.6 last.1
  60.3 1.0 %collective-permute-done.4.low_corner = f32[24,128]{1,0:T(8,128)S(1)} collective-permute-done((f32[24,128]{1,0:T(8,128)S(1)}, f32[24,128]{1,0:T(8,128)S(1)}, u32[]{:S(2)}, u32[]{:S(2)}) %collective-permute-start.4) | collective-permute-done | bytes 12320 | tf_op jit(solution)/shard_map/ppermute | solution.py:51
  61.3 0.8 %corners.1 = f32[3,8,32,128]{3,2,1,0:T(8,128)} custom-call(f32[3,8,32,128]{3,2,1,0:T(8,128)S(1)} %last.1, f32[8,32,128]{2,1,0:T(8,128)S(1)} %get-tuple-element.17.speed_sq, f32[120,128]{1,0:T(8,128)S(1)} %collective-permute-done.far_pair, f32[120,128]{1,0:T(8,128)S(1)} %collective-permute-done.1.near_pair, ...), custom_call_target="tpu_custom_call" | custom-call | tf_op jit(solution)/shard_map/corners/pallas_call | solution.py:470
  62.2 3.0 %all-to-all-done.1.parts = f32[32,1,128]{2,1,0:T(1,128)S(1)} async-done(((f32[32,1,128]{2,1,0:T(1,128)}), f32[32,1,128]{2,1,0:T(1,128)S(1)}, u32[]{:S(2)}, u32[]{:S(2)}) %all-to-all-start.1) | async-done | bytes 16416 | tf_op jit(solution)/shard_map/all_to_all | solution.py:465
  65.2 0.6 own.1
Async XLA Ops:
  2.6 16.6 %collective-permute-start.2 = (f32[57,8,128]{2,1,0:T(8,128)S(1)}, f32[57,8,128]{2,1,0:T(8,128)S(1)}, u32[]{:S(2)}, u32[]{:S(2)}) collective-permute-start(f32[57,8,128]{2,1,0:T(8,128)S(1)} %get-tuple-element.20), channel_id=1, source_target_pairs={{0,8},{16,24},{32,40},{48,56},{64,72},{80,88},{96,104},{112,120},{... | collective-permute-start | bytes 700424 | tf_op jit(solution)/shard_map/ppermute | solution.py:51
  6.6 12.6 %collective-permute-start.3 = (f32[57,8,128]{2,1,0:T(8,128)S(1)}, f32[57,8,128]{2,1,0:T(8,128)S(1)}, u32[]{:S(2)}, u32[]{:S(2)}) collective-permute-start(f32[57,8,128]{2,1,0:T(8,128)S(1)} %get-tuple-element.21), channel_id=1, source_target_pairs={{8,16},{24,32},{40,48},{56,64},{72,80},{88,96},{104,112},{120,128}... | collective-permute-start | bytes 700424 | tf_op jit(solution)/shard_map/ppermute | solution.py:51
  7.2 11.1 %collective-permute-start = (f32[120,128]{1,0:T(8,128)S(1)}, f32[120,128]{1,0:T(8,128)S(1)}, u32[]{:S(2)}, u32[]{:S(2)}) collective-permute-start(f32[120,128]{1,0:T(8,128)S(1)} %get-tuple-element.18), channel_id=1, source_target_pairs={{1,2},{3,4},{5,6},{2,1},{4,3},{6,5},{9,10},{11,12},{13,14},{10,9},... | collective-permute-start | bytes 184328 | tf_op jit(solution)/shard_map/ppermute | solution.py:51
  15.7 3.5 %collective-permute-start.1 = (f32[120,128]{1,0:T(8,128)S(1)}, f32[120,128]{1,0:T(8,128)S(1)}, u32[]{:S(2)}, u32[]{:S(2)}) collective-permute-start(f32[120,128]{1,0:T(8,128)S(1)} %get-tuple-element.19), channel_id=1, source_target_pairs={{0,1},{2,3},{4,5},{6,7},{1,0},{3,2},{5,4},{7,6},{8,9},{10,11},{12,... | collective-permute-start | bytes 184328 | tf_op jit(solution)/shard_map/ppermute | solution.py:51
  22.6 28.0 %all-to-all-start = ((f32[24,2,128]{2,1,0:T(2,128)}), f32[24,2,128]{2,1,0:T(2,128)S(1)}, u32[]{:S(2)}, u32[]{:S(2)}) async-start(f32[24,2,128]{2,1,0:T(2,128)} %get-tuple-element.26), calls=%async_computation | async-start | bytes 49152 | tf_op jit(solution)/shard_map/all_to_all | solution.py:460
  40.9 0.7 %collective-permute-start.5 = (f32[24,128]{1,0:T(8,128)S(1)}, f32[24,128]{1,0:T(8,128)S(1)}, u32[]{:S(2)}, u32[]{:S(2)}) collective-permute-start(f32[24,128]{1,0:T(8,128)S(1)} %get-tuple-element.25), channel_id=1, source_target_pairs={{8,16},{24,32},{40,48},{56,64},{72,80},{88,96},{104,112},{120,128}... | collective-permute-start | bytes 36872 | tf_op jit(solution)/shard_map/ppermute | solution.py:51
  51.2 13.9 %all-to-all-start.1 = ((f32[32,1,128]{2,1,0:T(1,128)}), f32[32,1,128]{2,1,0:T(1,128)S(1)}, u32[]{:S(2)}, u32[]{:S(2)}) async-start(f32[32,1,128]{2,1,0:T(1,128)} %spread.1), calls=%async_computation.1 | async-start | bytes 32768 | tf_op jit(solution)/shard_map/all_to_all | solution.py:465
  56.6 4.7 %collective-permute-start.4 = (f32[24,128]{1,0:T(8,128)S(1)}, f32[24,128]{1,0:T(8,128)S(1)}, u32[]{:S(2)}, u32[]{:S(2)}) collective-permute-start(f32[24,128]{1,0:T(8,128)S(1)} %get-tuple-element.24), channel_id=1, source_target_pairs={{0,8},{16,24},{32,40},{48,56},{64,72},{80,88},{96,104},{112,120},{... | collective-permute-start | bytes 36872 | tf_op jit(solution)/shard_map/ppermute | solution.py:51

commit v9 on v8

--- a/solution.py
+++ b/solution.py
@@ -65,17 +65,26 @@
     ahead, middle, speed_sq, far, near, low_pair, high_pair,
     before, wide, mechanism, cells, cells_row, patches_row, sems,
 ):
+    def piece(c):
+        return (
+            pltpu.make_async_copy(middle_far.at[c], middle.at[c], sems.at[5 + c]),
+            pltpu.make_async_copy(before_far.at[c], before.at[c], sems.at[8 + c]),
+        )
+
     copies = [
-        (middle_far, middle), (before_far, before), (speed_far, speed_sq), (mechanism_far, mechanism),
+        (speed_far, speed_sq), (mechanism_far, mechanism),
         (cells_far, cells), (cells_row_far, cells_row), (patches_row_far, patches_row),
     ]
     started = [pltpu.make_async_copy(a, b, sems.at[i]) for i, (a, b) in enumerate(copies)]
-    for copy in started:
+    started[0].start()
+    for c in range(3):
+        for copy in piece(c):
+            copy.start()
+    for copy in started[1:]:
         copy.start()
     odd = (lax.axis_index("east") & 1) == 1
     odd_north = (lax.axis_index("north") & 1) == 1
-    for copy in started:
-        copy.wait()
+    started[0].wait()
 
     def put_east(k, low, high):
         low, high = low.reshape(TILES, 8, CZ), high.reshape(TILES, 8, CZ)
@@ -88,6 +97,8 @@
         far[pl.ds(at, 2), :] = jnp.where(odd_north, high, low)
 
     def component(c, carry):
+        for copy in piece(c):
+            copy.wait()
         for e in range(CE):
             here = middle[c, e]
             wide[e, 6:8, :] = jnp.zeros((2, CZ), jnp.float32)
@@ -117,6 +128,8 @@
         put_east(E_SPEED + k, speed_sq[k], speed_sq[CE - 2 + k])
     for e in range(CE):
         put_north(N_SPEED + e * 2, speed_sq[e])
+    for copy in started[1:]:
+        copy.wait()
     lane = lax.broadcasted_iota(jnp.int32, (1, CZ), 1)
     speeds = jnp.zeros((1, CZ), jnp.float32)
     for i in range(SUBS):
@@ -429,7 +442,7 @@
         in_specs=[HBM] * 7, out_specs=[VMEM] * 7,
         scratch_shapes=[
             field, pltpu.VMEM((CE, CN + 16, CZ), f32), pltpu.VMEM((6, SUBS), f32), pltpu.SMEM((SUBS,), i32),
-            pltpu.VMEM((1, SUBS), i32), pltpu.VMEM((1, SUBS), i32), pltpu.SemaphoreType.DMA((7,)),
+            pltpu.VMEM((1, SUBS), i32), pltpu.VMEM((1, SUBS), i32), pltpu.SemaphoreType.DMA((11,)),
         ],
         compiler_params=params, name="load",
     )(*inputs[:7])

time: 66.2 us -> 66 us (level)
  no operation moved by 1% of the time
where the time goes in v9:
time: 66 us; the launch traced here: 65.6 us
  starting transfers between devices  43.1 us (65%)
  waiting for transfers between devices  13.8 us (21%)
  Pallas kernels  7.97 us (12%)
  between operations  0.74 us (1%)
    ppermute x6, starting transfers between devices, swap(): return lax.ppermute(block, axis, pairs + [(j, i) for i, j in pairs])  19.5 us
    all_to_all x1, starting transfers between devices, body(): lax.all_to_all(parts, BOTH, 0, 0, tiled=True, axis_index_groups=column_gr...  18.4 us
    all_to_all x1, waiting for transfers between devices, body(): lax.all_to_all(parts, BOTH, 0, 0, tiled=True, axis_index_groups=column_gr...  8.97 us
    all_to_all x1, starting transfers between devices, body(): lax.all_to_all(parts, BOTH, 0, 0, tiled=True, axis_index_groups=plane_gro...  5.3 us
    pallas_call x1, Pallas kernels, body(): pl.pallas_call(steps_kernel, out_shape=[pltpu.HBM((3, CE, CN, CZ), f32),...  3.34 us
    all_to_all x1, waiting for transfers between devices, body(): lax.all_to_all(parts, BOTH, 0, 0, tiled=True, axis_index_groups=plane_gro...  2.99 us
    pallas_call x1, Pallas kernels, body(): pl.pallas_call(load_kernel, out_shape=[*held] + [north_message] * 2 + [ea...  1.91 us
    ppermute x6, waiting for transfers between devices, swap(): return lax.ppermute(block, axis, pairs + [(j, i) for i, j in pairs])  1.84 us
  transfers between devices with their start and end apart: 8, of which 4 were waited for; matrix products, arithmetic and copies ran while one was open for 0% of the time, Pallas kernels for 2%

profile of v9, /device:TPU:1, one launch (start us, length us, event | category | flops | bytes accessed | tf_op | source)
XLA Modules:
  0.0 65.6 jit_solution(2280901803599298872)
XLA Ops:
  0.6 1.9 %load.1 = (f32[3,8,32,128]{3,2,1,0:T(8,128)S(1)}, f32[3,8,32,128]{3,2,1,0:T(8,128)S(1)}, f32[8,32,128]{2,1,0:T(8,128)S(1)}, f32[120,128]{1,0:T(8,128)S(1)}, f32[...) custom-call(f32[3,8,32,128]{3,2,1,0:T(8,128)} %before_far.1, ...), custom_call_target="tpu_custom_call" | custom-call | tf_op jit(solution)/shard_map/load/pallas_call | solution.py:440
  2.5 3.9 %collective-permute-start.2 = (f32[57,8,128]{2,1,0:T(8,128)S(1)}, f32[57,8,128]{2,1,0:T(8,128)S(1)}, u32[]{:S(2)}, u32[]{:S(2)}) collective-permute-start(f32[57,8,128]{2,1,0:T(8,128)S(1)} %get-tuple-element.20), channel_id=1, source_target_pairs={{0,8},{16,24},{32,40},{48,56},{64,72},{80,88},{96,104},{112,120},{... | collective-permute-start | bytes 700424 | tf_op jit(solution)/shard_map/ppermute | solution.py:51
  6.5 0.7 %collective-permute-start.3 = (f32[57,8,128]{2,1,0:T(8,128)S(1)}, f32[57,8,128]{2,1,0:T(8,128)S(1)}, u32[]{:S(2)}, u32[]{:S(2)}) collective-permute-start(f32[57,8,128]{2,1,0:T(8,128)S(1)} %get-tuple-element.21), channel_id=1, source_target_pairs={{8,16},{24,32},{40,48},{56,64},{72,80},{88,96},{104,112},{120,128}... | collective-permute-start | bytes 700424 | tf_op jit(solution)/shard_map/ppermute | solution.py:51
  7.2 8.5 %collective-permute-start = (f32[120,128]{1,0:T(8,128)S(1)}, f32[120,128]{1,0:T(8,128)S(1)}, u32[]{:S(2)}, u32[]{:S(2)}) collective-permute-start(f32[120,128]{1,0:T(8,128)S(1)} %get-tuple-element.18), channel_id=1, source_target_pairs={{1,2},{3,4},{5,6},{2,1},{4,3},{6,5},{9,10},{11,12},{13,14},{10,9},... | collective-permute-start | bytes 184328 | tf_op jit(solution)/shard_map/ppermute | solution.py:51
  15.7 2.6 %collective-permute-start.1 = (f32[120,128]{1,0:T(8,128)S(1)}, f32[120,128]{1,0:T(8,128)S(1)}, u32[]{:S(2)}, u32[]{:S(2)}) collective-permute-start(f32[120,128]{1,0:T(8,128)S(1)} %get-tuple-element.19), channel_id=1, source_target_pairs={{0,1},{2,3},{4,5},{6,7},{1,0},{3,2},{5,4},{7,6},{8,9},{10,11},{12,... | collective-permute-start | bytes 184328 | tf_op jit(solution)/shard_map/ppermute | solution.py:51
  18.3 0.0 collective-permute-done.far_pair
  18.3 0.9 %collective-permute-done.1.near_pair = f32[120,128]{1,0:T(8,128)S(1)} collective-permute-done((f32[120,128]{1,0:T(8,128)S(1)}, f32[120,128]{1,0:T(8,128)S(1)}, u32[]{:S(2)}, u32[]{:S(2)}) %collective-permute-start.1) | collective-permute-done | bytes 61472 | tf_op jit(solution)/shard_map/ppermute | solution.py:51
  19.1 0.0 collective-permute-done.2.low_pair
  19.1 0.0 collective-permute-done.3.high_pair
  19.1 3.3 %steps.1 = (f32[3,8,32,128]{3,2,1,0:T(8,128)}, f32[3,12,64,128]{3,2,1,0:T(8,128)S(1)}, f32[24,2,128]{2,1,0:T(2,128)}, f32[24,128]{1,0:T(8,128)S(1)}, f32[24,128]{1,0:T(8,128)S(1)}) custom-call(f32[3,8,32,128]{3,2,1,0:T(8,128)S(1)} %get-tuple-element.15.ahead, f32[3,8,32,128]{3,2,1,0:T(8,128)S(1)} %get-tuple-element.16.middle, ...), custom_call_target="tpu_custom_call" | custom-call | tf_op jit(solution)/shard_map/steps/pallas_call | solution.py:455
  22.5 18.4 %all-to-all-start = ((f32[24,2,128]{2,1,0:T(2,128)}), f32[24,2,128]{2,1,0:T(2,128)S(1)}, u32[]{:S(2)}, u32[]{:S(2)}) async-start(f32[24,2,128]{2,1,0:T(2,128)} %get-tuple-element.26), calls=%async_computation | async-start | bytes 49152 | tf_op jit(solution)/shard_map/all_to_all | solution.py:473
  40.9 0.7 %collective-permute-start.5 = (f32[24,128]{1,0:T(8,128)S(1)}, f32[24,128]{1,0:T(8,128)S(1)}, u32[]{:S(2)}, u32[]{:S(2)}) collective-permute-start(f32[24,128]{1,0:T(8,128)S(1)} %get-tuple-element.25), channel_id=1, source_target_pairs={{8,16},{24,32},{40,48},{56,64},{72,80},{88,96},{104,112},{120,128}... | collective-permute-start | bytes 36872 | tf_op jit(solution)/shard_map/ppermute | solution.py:51
  41.5 0.0 collective-permute-done.5.high_corner._
  41.5 9.0 %all-to-all-done.parts = f32[24,2,128]{2,1,0:T(2,128)S(1)} async-done(((f32[24,2,128]{2,1,0:T(2,128)}), f32[24,2,128]{2,1,0:T(2,128)S(1)}, u32[]{:S(2)}, u32[]{:S(2)}) %all-to-all-start) | async-done | bytes 24608 | tf_op jit(solution)/shard_map/all_to_all | solution.py:473
  50.5 0.6 spread.1
  51.1 5.3 %all-to-all-start.1 = ((f32[32,1,128]{2,1,0:T(1,128)}), f32[32,1,128]{2,1,0:T(1,128)S(1)}, u32[]{:S(2)}, u32[]{:S(2)}) async-start(f32[32,1,128]{2,1,0:T(1,128)} %spread.1), calls=%async_computation.1 | async-start | bytes 32768 | tf_op jit(solution)/shard_map/all_to_all | solution.py:478
  56.4 3.1 %collective-permute-start.4 = (f32[24,128]{1,0:T(8,128)S(1)}, f32[24,128]{1,0:T(8,128)S(1)}, u32[]{:S(2)}, u32[]{:S(2)}) collective-permute-start(f32[24,128]{1,0:T(8,128)S(1)} %get-tuple-element.24), channel_id=1, source_target_pairs={{0,8},{16,24},{32,40},{48,56},{64,72},{80,88},{96,104},{112,120},{... | collective-permute-start | bytes 36872 | tf_op jit(solution)/shard_map/ppermute | solution.py:51
  59.6 0.6 last.1
  60.2 1.0 %collective-permute-done.4.low_corner = f32[24,128]{1,0:T(8,128)S(1)} collective-permute-done((f32[24,128]{1,0:T(8,128)S(1)}, f32[24,128]{1,0:T(8,128)S(1)}, u32[]{:S(2)}, u32[]{:S(2)}) %collective-permute-start.4) | collective-permute-done | bytes 12320 | tf_op jit(solution)/shard_map/ppermute | solution.py:51
  61.2 0.8 %corners.1 = f32[3,8,32,128]{3,2,1,0:T(8,128)} custom-call(f32[3,8,32,128]{3,2,1,0:T(8,128)S(1)} %last.1, f32[8,32,128]{2,1,0:T(8,128)S(1)} %get-tuple-element.17.speed_sq, f32[120,128]{1,0:T(8,128)S(1)} %collective-permute-done.far_pair, f32[120,128]{1,0:T(8,128)S(1)} %collective-permute-done.1.near_pair, ...), custom_call_target="tpu_custom_call" | custom-call | tf_op jit(solution)/shard_map/corners/pallas_call | solution.py:483
  62.0 3.0 %all-to-all-done.1.parts = f32[32,1,128]{2,1,0:T(1,128)S(1)} async-done(((f32[32,1,128]{2,1,0:T(1,128)}), f32[32,1,128]{2,1,0:T(1,128)S(1)}, u32[]{:S(2)}, u32[]{:S(2)}) %all-to-all-start.1) | async-done | bytes 16416 | tf_op jit(solution)/shard_map/all_to_all | solution.py:478
  65.0 0.6 own.1
Async XLA Ops:
  2.5 16.6 %collective-permute-start.2 = (f32[57,8,128]{2,1,0:T(8,128)S(1)}, f32[57,8,128]{2,1,0:T(8,128)S(1)}, u32[]{:S(2)}, u32[]{:S(2)}) collective-permute-start(f32[57,8,128]{2,1,0:T(8,128)S(1)} %get-tuple-element.20), channel_id=1, source_target_pairs={{0,8},{16,24},{32,40},{48,56},{64,72},{80,88},{96,104},{112,120},{... | collective-permute-start | bytes 700424 | tf_op jit(solution)/shard_map/ppermute | solution.py:51
  6.5 12.6 %collective-permute-start.3 = (f32[57,8,128]{2,1,0:T(8,128)S(1)}, f32[57,8,128]{2,1,0:T(8,128)S(1)}, u32[]{:S(2)}, u32[]{:S(2)}) collective-permute-start(f32[57,8,128]{2,1,0:T(8,128)S(1)} %get-tuple-element.21), channel_id=1, source_target_pairs={{8,16},{24,32},{40,48},{56,64},{72,80},{88,96},{104,112},{120,128}... | collective-permute-start | bytes 700424 | tf_op jit(solution)/shard_map/ppermute | solution.py:51
  7.2 11.1 %collective-permute-start = (f32[120,128]{1,0:T(8,128)S(1)}, f32[120,128]{1,0:T(8,128)S(1)}, u32[]{:S(2)}, u32[]{:S(2)}) collective-permute-start(f32[120,128]{1,0:T(8,128)S(1)} %get-tuple-element.18), channel_id=1, source_target_pairs={{1,2},{3,4},{5,6},{2,1},{4,3},{6,5},{9,10},{11,12},{13,14},{10,9},... | collective-permute-start | bytes 184328 | tf_op jit(solution)/shard_map/ppermute | solution.py:51
  15.7 3.5 %collective-permute-start.1 = (f32[120,128]{1,0:T(8,128)S(1)}, f32[120,128]{1,0:T(8,128)S(1)}, u32[]{:S(2)}, u32[]{:S(2)}) collective-permute-start(f32[120,128]{1,0:T(8,128)S(1)} %get-tuple-element.19), channel_id=1, source_target_pairs={{0,1},{2,3},{4,5},{6,7},{1,0},{3,2},{5,4},{7,6},{8,9},{10,11},{12,... | collective-permute-start | bytes 184328 | tf_op jit(solution)/shard_map/ppermute | solution.py:51
  22.5 28.0 %all-to-all-start = ((f32[24,2,128]{2,1,0:T(2,128)}), f32[24,2,128]{2,1,0:T(2,128)S(1)}, u32[]{:S(2)}, u32[]{:S(2)}) async-start(f32[24,2,128]{2,1,0:T(2,128)} %get-tuple-element.26), calls=%async_computation | async-start | bytes 49152 | tf_op jit(solution)/shard_map/all_to_all | solution.py:473
  40.9 0.7 %collective-permute-start.5 = (f32[24,128]{1,0:T(8,128)S(1)}, f32[24,128]{1,0:T(8,128)S(1)}, u32[]{:S(2)}, u32[]{:S(2)}) collective-permute-start(f32[24,128]{1,0:T(8,128)S(1)} %get-tuple-element.25), channel_id=1, source_target_pairs={{8,16},{24,32},{40,48},{56,64},{72,80},{88,96},{104,112},{120,128}... | collective-permute-start | bytes 36872 | tf_op jit(solution)/shard_map/ppermute | solution.py:51
  51.1 13.9 %all-to-all-start.1 = ((f32[32,1,128]{2,1,0:T(1,128)}), f32[32,1,128]{2,1,0:T(1,128)S(1)}, u32[]{:S(2)}, u32[]{:S(2)}) async-start(f32[32,1,128]{2,1,0:T(1,128)} %spread.1), calls=%async_computation.1 | async-start | bytes 32768 | tf_op jit(solution)/shard_map/all_to_all | solution.py:478
  56.4 4.7 %collective-permute-start.4 = (f32[24,128]{1,0:T(8,128)S(1)}, f32[24,128]{1,0:T(8,128)S(1)}, u32[]{:S(2)}, u32[]{:S(2)}) collective-permute-start(f32[24,128]{1,0:T(8,128)S(1)} %get-tuple-element.24), channel_id=1, source_target_pairs={{0,8},{16,24},{32,40},{48,56},{64,72},{80,88},{96,104},{112,120},{... | collective-permute-start | bytes 36872 | tf_op jit(solution)/shard_map/ppermute | solution.py:51

commit v10 on v9

--- a/solution.py
+++ b/solution.py
@@ -192,7 +192,7 @@
 
 def steps_kernel(
     ahead, middle, speed_sq, far_pair, near_pair, low_pair, high_pair,
-    mechanism_far, cells_far, patches_far, next_out, later, parts, low_corner, high_corner,
+    mechanism_far, cells_far, patches_far, next_out, later, parts,
     beyond, mechanism, cells, patches, theirs, code_rows, codes, sub_sems, out_sems,
 ):
     subs = [
@@ -226,7 +226,6 @@
 
     west, east = east_layers(low_pair, high_pair)
     south, north = north_rows(near_pair, far_pair)
-    put_corners(south, north, low_corner, high_corner)
     beyond[...] = jnp.zeros_like(beyond)
 
     def put_beyond(c):
@@ -359,6 +358,10 @@
         next_copy(c).wait()
 
 
+def corner_strips_kernel(far_pair, near_pair, _, low_corner, high_corner):
+    put_corners(*north_rows(near_pair, far_pair), low_corner, high_corner)
+
+
 def last_kernel(middle, speed_sq, later, out):
     def component(c, carry):
         for e in range(CE):
@@ -452,10 +455,10 @@
     later = pltpu.VMEM((3, LAYERS, CN + 2 * TOP, CZ), f32)
     parts = pltpu.VMEM((COLUMN, ROWS, CZ), f32)
     corner = pltpu.VMEM((C_LEN, CZ), f32)
-    field_next, later, parts, low_corner, high_corner = pl.pallas_call(
+    field_next, later, parts = pl.pallas_call(
         steps_kernel,
-        out_shape=[pltpu.HBM((3, CE, CN, CZ), f32), later, parts, corner, corner],
-        in_specs=[VMEM] * 7 + [HBM] * 3, out_specs=[HBM] + [VMEM] * 4,
+        out_shape=[pltpu.HBM((3, CE, CN, CZ), f32), later, parts],
+        in_specs=[VMEM] * 7 + [HBM] * 3, out_specs=[HBM] + [VMEM] * 2,
         scratch_shapes=[
             pltpu.VMEM((4, 3, 16, CZ), f32),
             pltpu.SMEM((6, SUBS), f32), pltpu.SMEM((SUBS,), i32), pltpu.SMEM((SUBS,), i32),
@@ -464,6 +467,10 @@
         ],
         compiler_params=params, name="steps",
     )(ahead, field_now, speed_sq, *halos, inputs[3], inputs[4], inputs[7])
+    low_corner, high_corner = pl.pallas_call(
+        corner_strips_kernel, out_shape=[corner, corner], in_specs=[VMEM] * 3, out_specs=[VMEM] * 2,
+        compiler_params=params, name="corner_strips",
+    )(far_pair, near_pair, later)
     corners = swap(low_corner, "east", 0), swap(high_corner, "east", 1)
     field_last = pl.pallas_call(
         last_kernel, out_shape=pltpu.VMEM((3, CE, CN, CZ), f32), in_specs=[VMEM] * 3, out_specs=VMEM,

time: 66 us -> 65.9 us (level)
  no operation moved by 1% of the time
where the time goes in v10:
time: 65.9 us; the launch traced here: 65.6 us
  starting transfers between devices  43.1 us (65%)
  waiting for transfers between devices  13.6 us (21%)
  Pallas kernels  8.14 us (12%)
  between operations  0.75 us (1%)
    ppermute x6, starting transfers between devices, swap(): return lax.ppermute(block, axis, pairs + [(j, i) for i, j in pairs])  19.5 us
    all_to_all x1, starting transfers between devices, body(): lax.all_to_all(parts, BOTH, 0, 0, tiled=True, axis_index_groups=column_gr...  18.1 us
    all_to_all x1, waiting for transfers between devices, body(): lax.all_to_all(parts, BOTH, 0, 0, tiled=True, axis_index_groups=column_gr...  8.94 us
    all_to_all x1, starting transfers between devices, body(): lax.all_to_all(parts, BOTH, 0, 0, tiled=True, axis_index_groups=plane_gro...  5.45 us
    pallas_call x1, Pallas kernels, body(): pl.pallas_call(steps_kernel, out_shape=[pltpu.HBM((3, CE, CN, CZ), f32),...  3.5 us
    all_to_all x1, waiting for transfers between devices, body(): lax.all_to_all(parts, BOTH, 0, 0, tiled=True, axis_index_groups=plane_gro...  2.84 us
    pallas_call x1, Pallas kernels, body(): pl.pallas_call(load_kernel, out_shape=[*held] + [north_message] * 2 + [ea...  1.91 us
    ppermute x6, waiting for transfers between devices, swap(): return lax.ppermute(block, axis, pairs + [(j, i) for i, j in pairs])  1.84 us
  transfers between devices with their start and end apart: 8, of which 4 were waited for; matrix products, arithmetic and copies ran while one was open for 0% of the time, Pallas kernels for 2%

profile of v10, /device:TPU:1, one launch (start us, length us, event | category | flops | bytes accessed | tf_op | source)
XLA Modules:
  0.0 65.6 jit_solution(5602900942531279887)
XLA Ops:
  0.6 1.9 %load.1 = (f32[3,8,32,128]{3,2,1,0:T(8,128)S(1)}, f32[3,8,32,128]{3,2,1,0:T(8,128)S(1)}, f32[8,32,128]{2,1,0:T(8,128)S(1)}, f32[120,128]{1,0:T(8,128)S(1)}, f32[...) custom-call(f32[3,8,32,128]{3,2,1,0:T(8,128)} %before_far.1, ...), custom_call_target="tpu_custom_call" | custom-call | tf_op jit(solution)/shard_map/load/pallas_call | solution.py:443
  2.5 3.9 %collective-permute-start.2 = (f32[57,8,128]{2,1,0:T(8,128)S(1)}, f32[57,8,128]{2,1,0:T(8,128)S(1)}, u32[]{:S(2)}, u32[]{:S(2)}) collective-permute-start(f32[57,8,128]{2,1,0:T(8,128)S(1)} %get-tuple-element.20), channel_id=1, source_target_pairs={{0,8},{16,24},{32,40},{48,56},{64,72},{80,88},{96,104},{112,120},{... | collective-permute-start | bytes 700424 | tf_op jit(solution)/shard_map/ppermute | solution.py:51
  6.5 0.7 %collective-permute-start.3 = (f32[57,8,128]{2,1,0:T(8,128)S(1)}, f32[57,8,128]{2,1,0:T(8,128)S(1)}, u32[]{:S(2)}, u32[]{:S(2)}) collective-permute-start(f32[57,8,128]{2,1,0:T(8,128)S(1)} %get-tuple-element.21), channel_id=1, source_target_pairs={{8,16},{24,32},{40,48},{56,64},{72,80},{88,96},{104,112},{120,128}... | collective-permute-start | bytes 700424 | tf_op jit(solution)/shard_map/ppermute | solution.py:51
  7.2 8.5 %collective-permute-start = (f32[120,128]{1,0:T(8,128)S(1)}, f32[120,128]{1,0:T(8,128)S(1)}, u32[]{:S(2)}, u32[]{:S(2)}) collective-permute-start(f32[120,128]{1,0:T(8,128)S(1)} %get-tuple-element.18), channel_id=1, source_target_pairs={{1,2},{3,4},{5,6},{2,1},{4,3},{6,5},{9,10},{11,12},{13,14},{10,9},... | collective-permute-start | bytes 184328 | tf_op jit(solution)/shard_map/ppermute | solution.py:51
  15.7 2.6 %collective-permute-start.1 = (f32[120,128]{1,0:T(8,128)S(1)}, f32[120,128]{1,0:T(8,128)S(1)}, u32[]{:S(2)}, u32[]{:S(2)}) collective-permute-start(f32[120,128]{1,0:T(8,128)S(1)} %get-tuple-element.19), channel_id=1, source_target_pairs={{0,1},{2,3},{4,5},{6,7},{1,0},{3,2},{5,4},{7,6},{8,9},{10,11},{12,... | collective-permute-start | bytes 184328 | tf_op jit(solution)/shard_map/ppermute | solution.py:51
  18.3 0.0 collective-permute-done.far_pair
  18.3 0.9 %collective-permute-done.1.near_pair = f32[120,128]{1,0:T(8,128)S(1)} collective-permute-done((f32[120,128]{1,0:T(8,128)S(1)}, f32[120,128]{1,0:T(8,128)S(1)}, u32[]{:S(2)}, u32[]{:S(2)}) %collective-permute-start.1) | collective-permute-done | bytes 61472 | tf_op jit(solution)/shard_map/ppermute | solution.py:51
  19.1 0.0 collective-permute-done.2.low_pair
  19.1 0.0 collective-permute-done.3.high_pair
  19.1 3.5 %steps.1 = (f32[3,8,32,128]{3,2,1,0:T(8,128)}, f32[3,12,64,128]{3,2,1,0:T(8,128)S(1)}, f32[24,2,128]{2,1,0:T(2,128)}) custom-call(f32[3,8,32,128]{3,2,1,0:T(8,128)S(1)} %get-tuple-element.15.ahead, f32[3,8,32,128]{3,2,1,0:T(8,128)S(1)} %get-tuple-element.16.middle, f32[8,32,128]{2,1,0:T(8,128)S(1)} %get-tuple-element.17.speed_sq, ...), custom_call_target="tpu_custom_call" | custom-call | tf_op jit(solution)/shard_map/steps/pallas_call | solution.py:458
  22.6 18.1 %all-to-all-start = ((f32[24,2,128]{2,1,0:T(2,128)}), f32[24,2,128]{2,1,0:T(2,128)S(1)}, u32[]{:S(2)}, u32[]{:S(2)}) async-start(f32[24,2,128]{2,1,0:T(2,128)} %get-tuple-element.26), calls=%async_computation | async-start | bytes 49152 | tf_op jit(solution)/shard_map/all_to_all | solution.py:480
  40.8 0.7 %collective-permute-start.5 = (f32[24,128]{1,0:T(8,128)S(1)}, f32[24,128]{1,0:T(8,128)S(1)}, u32[]{:S(2)}, u32[]{:S(2)}) collective-permute-start(f32[24,128]{1,0:T(8,128)S(1)} %get-tuple-element.25), channel_id=1, source_target_pairs={{8,16},{24,32},{40,48},{56,64},{72,80},{88,96},{104,112},{120,128}... | collective-permute-start | bytes 36872 | tf_op jit(solution)/shard_map/ppermute | solution.py:51
  41.5 0.0 collective-permute-done.5.high_corner._
  41.5 8.9 %all-to-all-done.parts = f32[24,2,128]{2,1,0:T(2,128)S(1)} async-done(((f32[24,2,128]{2,1,0:T(2,128)}), f32[24,2,128]{2,1,0:T(2,128)S(1)}, u32[]{:S(2)}, u32[]{:S(2)}) %all-to-all-start) | async-done | bytes 24608 | tf_op jit(solution)/shard_map/all_to_all | solution.py:480
  50.4 0.6 spread.1
  51.1 5.5 %all-to-all-start.1 = ((f32[32,1,128]{2,1,0:T(1,128)}), f32[32,1,128]{2,1,0:T(1,128)S(1)}, u32[]{:S(2)}, u32[]{:S(2)}) async-start(f32[32,1,128]{2,1,0:T(1,128)} %spread.1), calls=%async_computation.1 | async-start | bytes 32768 | tf_op jit(solution)/shard_map/all_to_all | solution.py:485
  56.5 3.1 %collective-permute-start.4 = (f32[24,128]{1,0:T(8,128)S(1)}, f32[24,128]{1,0:T(8,128)S(1)}, u32[]{:S(2)}, u32[]{:S(2)}) collective-permute-start(f32[24,128]{1,0:T(8,128)S(1)} %get-tuple-element.24), channel_id=1, source_target_pairs={{0,8},{16,24},{32,40},{48,56},{64,72},{80,88},{96,104},{112,120},{... | collective-permute-start | bytes 36872 | tf_op jit(solution)/shard_map/ppermute | solution.py:51
  59.7 0.6 last.1
  60.3 1.0 %collective-permute-done.4.low_corner = f32[24,128]{1,0:T(8,128)S(1)} collective-permute-done((f32[24,128]{1,0:T(8,128)S(1)}, f32[24,128]{1,0:T(8,128)S(1)}, u32[]{:S(2)}, u32[]{:S(2)}) %collective-permute-start.4) | collective-permute-done | bytes 12320 | tf_op jit(solution)/shard_map/ppermute | solution.py:51
  61.3 0.8 %corners.1 = f32[3,8,32,128]{3,2,1,0:T(8,128)} custom-call(f32[3,8,32,128]{3,2,1,0:T(8,128)S(1)} %last.1, f32[8,32,128]{2,1,0:T(8,128)S(1)} %get-tuple-element.17.speed_sq, f32[120,128]{1,0:T(8,128)S(1)} %collective-permute-done.far_pair, f32[120,128]{1,0:T(8,128)S(1)} %collective-permute-done.1.near_pair, ...), custom_call_target="tpu_custom_call" | custom-call | tf_op jit(solution)/shard_map/corners/pallas_call | solution.py:490
  62.1 2.8 %all-to-all-done.1.parts = f32[32,1,128]{2,1,0:T(1,128)S(1)} async-done(((f32[32,1,128]{2,1,0:T(1,128)}), f32[32,1,128]{2,1,0:T(1,128)S(1)}, u32[]{:S(2)}, u32[]{:S(2)}) %all-to-all-start.1) | async-done | bytes 16416 | tf_op jit(solution)/shard_map/all_to_all | solution.py:485
  65.0 0.6 own.1
  (1 shorter events, 0.0 us)
Async XLA Ops:
  2.5 16.6 %collective-permute-start.2 = (f32[57,8,128]{2,1,0:T(8,128)S(1)}, f32[57,8,128]{2,1,0:T(8,128)S(1)}, u32[]{:S(2)}, u32[]{:S(2)}) collective-permute-start(f32[57,8,128]{2,1,0:T(8,128)S(1)} %get-tuple-element.20), channel_id=1, source_target_pairs={{0,8},{16,24},{32,40},{48,56},{64,72},{80,88},{96,104},{112,120},{... | collective-permute-start | bytes 700424 | tf_op jit(solution)/shard_map/ppermute | solution.py:51
  6.5 12.6 %collective-permute-start.3 = (f32[57,8,128]{2,1,0:T(8,128)S(1)}, f32[57,8,128]{2,1,0:T(8,128)S(1)}, u32[]{:S(2)}, u32[]{:S(2)}) collective-permute-start(f32[57,8,128]{2,1,0:T(8,128)S(1)} %get-tuple-element.21), channel_id=1, source_target_pairs={{8,16},{24,32},{40,48},{56,64},{72,80},{88,96},{104,112},{120,128}... | collective-permute-start | bytes 700424 | tf_op jit(solution)/shard_map/ppermute | solution.py:51
  7.2 11.1 %collective-permute-start = (f32[120,128]{1,0:T(8,128)S(1)}, f32[120,128]{1,0:T(8,128)S(1)}, u32[]{:S(2)}, u32[]{:S(2)}) collective-permute-start(f32[120,128]{1,0:T(8,128)S(1)} %get-tuple-element.18), channel_id=1, source_target_pairs={{1,2},{3,4},{5,6},{2,1},{4,3},{6,5},{9,10},{11,12},{13,14},{10,9},... | collective-permute-start | bytes 184328 | tf_op jit(solution)/shard_map/ppermute | solution.py:51
  15.7 3.5 %collective-permute-start.1 = (f32[120,128]{1,0:T(8,128)S(1)}, f32[120,128]{1,0:T(8,128)S(1)}, u32[]{:S(2)}, u32[]{:S(2)}) collective-permute-start(f32[120,128]{1,0:T(8,128)S(1)} %get-tuple-element.19), channel_id=1, source_target_pairs={{0,1},{2,3},{4,5},{6,7},{1,0},{3,2},{5,4},{7,6},{8,9},{10,11},{12,... | collective-permute-start | bytes 184328 | tf_op jit(solution)/shard_map/ppermute | solution.py:51
  22.6 27.8 %all-to-all-start = ((f32[24,2,128]{2,1,0:T(2,128)}), f32[24,2,128]{2,1,0:T(2,128)S(1)}, u32[]{:S(2)}, u32[]{:S(2)}) async-start(f32[24,2,128]{2,1,0:T(2,128)} %get-tuple-element.26), calls=%async_computation | async-start | bytes 49152 | tf_op jit(solution)/shard_map/all_to_all | solution.py:480
  40.8 0.7 %collective-permute-start.5 = (f32[24,128]{1,0:T(8,128)S(1)}, f32[24,128]{1,0:T(8,128)S(1)}, u32[]{:S(2)}, u32[]{:S(2)}) collective-permute-start(f32[24,128]{1,0:T(8,128)S(1)} %get-tuple-element.25), channel_id=1, source_target_pairs={{8,16},{24,32},{40,48},{56,64},{72,80},{88,96},{104,112},{120,128}... | collective-permute-start | bytes 36872 | tf_op jit(solution)/shard_map/ppermute | solution.py:51
  51.1 13.9 %all-to-all-start.1 = ((f32[32,1,128]{2,1,0:T(1,128)}), f32[32,1,128]{2,1,0:T(1,128)S(1)}, u32[]{:S(2)}, u32[]{:S(2)}) async-start(f32[32,1,128]{2,1,0:T(1,128)} %spread.1), calls=%async_computation.1 | async-start | bytes 32768 | tf_op jit(solution)/shard_map/all_to_all | solution.py:485
  56.5 4.7 %collective-permute-start.4 = (f32[24,128]{1,0:T(8,128)S(1)}, f32[24,128]{1,0:T(8,128)S(1)}, u32[]{:S(2)}, u32[]{:S(2)}) collective-permute-start(f32[24,128]{1,0:T(8,128)S(1)} %get-tuple-element.24), channel_id=1, source_target_pairs={{0,8},{16,24},{32,40},{48,56},{64,72},{80,88},{96,104},{112,120},{... | collective-permute-start | bytes 36872 | tf_op jit(solution)/shard_map/ppermute | solution.py:51
